TPU v7x, 512 devices: a whole 4x4x16 slice. The times are simulated.
512 devices in a mesh: front: 16 (over y, x), rows: 32 (over z, core).
Axes of the slice: x: 4, y: 4, z: 16, core: 2. Of those that a mesh axis runs over, the one named last changes fastest.
Arguments:
- own_rows: float32 [16, 8192, 1024], P('front', 'rows'), may hold values from -6 to 6
- child_tile: float32 [16, 1024, 1024], P('front', 'rows'), as said below
- col_map: int32 [16, 1024], replicated, may hold values from 0 to 1023, each once within a row
- parent: int32 [16], replicated, may hold values from 0 to 15
- live_rows: int32 [16], replicated, may hold values from 1024 to 8192
Outputs:
- r_factor: float32 [16, 1024, 1024], P('front', 'rows')
- q_panel: float32 [16, 8192, 1024], P('front', 'rows')
Inputs may be any that keep to these rules, and one draw needn't show every extreme that they name: `child_tile`: each child's tile is upper triangular with a positive diagonal.
All inputs are finite; a program needn't handle non-finite values.
Results may differ from a plain program's by a relative error of at most 0.0003.
Values sent between devices are 32-bit elements; how exact they have to be, the bound alone decides.
No kernel may reach another device: no remote copies, remote signals or barrier semaphores. Data moves between devices by JAX's collectives and lax.ppermute only.
A program may use at most 64 MiB of HBM per device.

v0:
```python
import jax
import jax.numpy as jnp
from jax import lax
from jax.sharding import PartitionSpec as P


def place_columns(slot, cmap):
    return jnp.zeros_like(slot).at[:, cmap].set(slot)


def reduce_gram(local):
    return lax.psum(local, "rows")


def body(own_rows, child_tile, col_map, parent, live_rows):
    highest = lax.Precision.HIGHEST
    group = lax.axis_index("front")
    place = lax.axis_index("rows")
    groups = lax.axis_size("front")
    row_devs = lax.axis_size("rows")
    own = own_rows[0]
    tile = child_tile[0]
    local_rows = own.shape[0]
    width = own.shape[1]
    tile_rows = tile.shape[0]
    total_rows = local_rows * row_devs
    fronts_iota = jnp.arange(groups, dtype=jnp.int32)
    live = jnp.sum(jnp.where(fronts_iota == group, live_rows, 0))
    my_parent = jnp.sum(jnp.where(fronts_iota == group, parent, 0))
    rowid = place * local_rows + jnp.arange(local_rows, dtype=jnp.int32)
    own_live = jnp.where((rowid < live)[:, None], own, jnp.float32(0.0))
    buffer = jnp.where((fronts_iota == my_parent)[:, None, None], tile[None], jnp.float32(0.0))
    arrivals = lax.all_to_all(buffer, "front", split_axis=0, concat_axis=0, tiled=True)

    def place_owned(items):
        slot, cmap, owner = items
        return lax.cond(
            owner == group, lambda: place_columns(slot, cmap), lambda: jnp.zeros_like(slot)
        )

    arrivals = lax.map(place_owned, (arrivals, col_map, parent))
    stacked = jnp.concatenate([own_live, arrivals.reshape(-1, width)], axis=0)
    squares = lax.psum(jnp.sum(stacked * stacked, axis=0), "rows")
    scale = (squares / total_rows + 1e-06) ** (-0.5)
    scaled = stacked * scale[None, :]
    gram = reduce_gram(jnp.dot(scaled.T, scaled, precision=highest))
    gram = gram + 0.25 * total_rows * jnp.eye(width, dtype=jnp.float32)
    lower = jnp.linalg.cholesky(gram)
    upper_rows = lax.dynamic_slice_in_dim(lower.T, place * tile_rows, tile_rows, 0)
    panel = lax.linalg.triangular_solve(
        lower, own_live * scale[None, :], left_side=False, lower=True, transpose_a=True
    )
    return (upper_rows[None], panel[None])


def solution(mesh):
    placed = (P("front", "rows", None), P("front", "rows", None), P(), P(), P())
    return jax.shard_map(
        body,
        mesh=mesh,
        in_specs=placed,
        out_specs=(P("front", "rows", None), P("front", "rows", None)),
        check_vma=False,
    )
```

profile of v0, /device:TPU:1, one launch (start us, length us, event | category | flops | bytes accessed | tf_op | source)
XLA Modules:
  0.0 767.0 jit_solution(3523690356955551152)
XLA Ops:
  9.2 2.6 broadcast_select_fusion
  11.8 7.6 all-to-all-start
  21.2 23.4 %all-to-all-done = f32[16,32,1024]{2,1,0:T(8,128)S(1)} async-done(((f32[16,32,1024]{2,1,0:T(8,128)}), f32[16,32,1024]{2,1,0:T(8,128)S(1)}, u32[]{:S(2)}, u32[]{:S(2)}) %all-to-all-start) | async-done | bytes 2097184 | tf_op jit(solution)/shard_map/all_to_all | solution.py:33
  44.6 4.7 copy.35
  49.3 42.9 %while.13 = (s32[]{:T(128)}, f32[16,32,1024]{2,1,0:T(8,128)}, s32[16]{0:T(128)S(1)}, s32[]{:T(128)}, s32[16,1024]{1,0:T(8,128)}, /*index=5*/f32[16,32,1024]{1,2,0:T(8,128)}) while((s32[]{:T(128)}, f32[16,32,1024]{2,1,0:T(8,128)}, s32[16]{0:T(128)S(1)}, s32[]{:T(128)}, s32[16,1024]{1,0:T(8,128)}, ...), condition=%wide.region_6.7_spmd.clone, body=%wide.region_2.6_spmd.sunk.clone | while | flops 3076 | bytes 1190027 | solution.py:41
  71.8 4.4 conditional.3
  72.6 3.6 scatter_custom_fusion
  86.9 4.4 conditional.3
  87.7 3.6 scatter_custom_fusion
  94.0 59.2 %psum.14 = f32[1024]{0:T(1024)S(1)} all-reduce(f32[1024]{0:T(1024)S(1)} %multiply_reduce_fusion), channel_id=1, replica_groups=mesh['front'=16,'rows'=32] {'rows'}, use_global_device_ids=true, to_apply=%region_8.9 | all-reduce | flops 1024 | bytes 8192 | tf_op jit(solution)/shard_map/psum | solution.py:43
  153.3 13.8 %fusion.6 = f32[1024,1024]{0,1:T(8,128)} fusion(f32[512,1024]{1,0:T(8,128)} %bitcast.130, f32[256,1024]{1,0:T(8,128)S(1)} %copy-done.2, f32[1024]{0:T(1024)S(1)} %add_power_fusion), kind=kOutput, calls=%fused_computation.17 | convolution fusion | flops 9665249280 | bytes 7344128 | tf_op jit(solution)/shard_map/dot_general | solution.py:46
  167.2 231.8 %all-reduce.3.cloned.1.call-done = f32[1024,1024]{0,1:T(8,128)} async-done(((f32[1024,1024]{0,1:T(8,128)}), f32[1024,1024]{0,1:T(8,128)}) %all-reduce.3.cloned.1.call-update) | async-done | bytes 4194320 | tf_op jit(solution)/shard_map/psum | solution.py:12
  399.0 4.8 select_add_fusion
  403.9 5.8 copy.38
  409.7 4.5 fusion.4
  416.1 11.7 %cholesky.222 = f32[128,128]{1,0:T(8,128)S(1)} custom-call(f32[128,128]{1,0:T(8,128)S(1)} %cholesky.577), custom_call_target="Cholesky" | custom-call | tf_op jit(solution)/shard_map/jit(cholesky)/cholesky | solution.py:48
  427.9 9.8 %custom-call.62 = f32[1,128,128]{1,2,0:T(8,128)S(1)} custom-call(f32[1,128,128]{2,1,0:T(8,128)S(1)} %get-tuple-element.165), custom_call_target="InvertDiagBlocksLowerTriangular" | custom-call | tf_op jit(solution)/shard_map/jit(cholesky)/cholesky | solution.py:48
  437.7 2.5 cholesky.254
  440.2 2.5 constant_dynamic-update-slice_fusion.32
  444.6 11.8 %cholesky.243 = f32[128,128]{1,0:T(8,128)S(1)} custom-call(f32[128,128]{1,0:T(8,128)S(1)} %cholesky.581), custom_call_target="Cholesky" | custom-call | tf_op jit(solution)/shard_map/jit(cholesky)/cholesky | solution.py:48
  456.6 9.8 %custom-call.63 = f32[1,128,128]{1,2,0:T(8,128)S(1)} custom-call(f32[1,128,128]{2,1,0:T(8,128)S(1)} %get-tuple-element.163), custom_call_target="InvertDiagBlocksLowerTriangular" | custom-call | tf_op jit(solution)/shard_map/jit(cholesky)/cholesky | solution.py:48
  468.4 2.7 convolution_subtract_fusion.1
  471.1 11.7 %cholesky.466 = f32[128,128]{1,0:T(8,128)S(1)} custom-call(f32[128,128]{1,0:T(8,128)S(1)} %cholesky.586), custom_call_target="Cholesky" | custom-call | tf_op jit(solution)/shard_map/jit(cholesky)/cholesky | solution.py:48
  483.6 9.8 %custom-call.64 = f32[1,128,128]{1,2,0:T(8,128)S(1)} custom-call(f32[1,128,128]{2,1,0:T(8,128)S(1)} %get-tuple-element.161), custom_call_target="InvertDiagBlocksLowerTriangular" | custom-call | tf_op jit(solution)/shard_map/jit(cholesky)/cholesky | solution.py:48
  494.7 3.3 convolution_subtract_fusion.2
  498.0 11.7 %cholesky.485 = f32[128,128]{1,0:T(8,128)S(1)} custom-call(f32[128,128]{1,0:T(8,128)S(1)} %cholesky.591), custom_call_target="Cholesky" | custom-call | tf_op jit(solution)/shard_map/jit(cholesky)/cholesky | solution.py:48
  510.5 9.8 %custom-call.65 = f32[1,128,128]{1,2,0:T(8,128)S(1)} custom-call(f32[1,128,128]{2,1,0:T(8,128)S(1)} %get-tuple-element.159), custom_call_target="InvertDiagBlocksLowerTriangular" | custom-call | tf_op jit(solution)/shard_map/jit(cholesky)/cholesky | solution.py:48
  521.5 3.2 convolution_subtract_fusion.3
  524.6 12.1 %cholesky.504 = f32[128,128]{1,0:T(8,128)S(1)} custom-call(f32[128,128]{1,0:T(8,128)S(1)} %cholesky.596), custom_call_target="Cholesky" | custom-call | tf_op jit(solution)/shard_map/jit(cholesky)/cholesky | solution.py:48
  537.5 9.8 %custom-call.66 = f32[1,128,128]{1,2,0:T(8,128)S(1)} custom-call(f32[1,128,128]{2,1,0:T(8,128)S(1)} %get-tuple-element.157), custom_call_target="InvertDiagBlocksLowerTriangular" | custom-call | tf_op jit(solution)/shard_map/jit(cholesky)/cholesky | solution.py:48
  548.5 3.2 convolution_subtract_fusion.4
  551.7 11.7 %cholesky.524 = f32[128,128]{1,0:T(8,128)S(1)} custom-call(f32[128,128]{1,0:T(8,128)S(1)} %cholesky.601), custom_call_target="Cholesky" | custom-call | tf_op jit(solution)/shard_map/jit(cholesky)/cholesky | solution.py:48
  564.2 9.8 %custom-call.67 = f32[1,128,128]{1,2,0:T(8,128)S(1)} custom-call(f32[1,128,128]{2,1,0:T(8,128)S(1)} %get-tuple-element.155), custom_call_target="InvertDiagBlocksLowerTriangular" | custom-call | tf_op jit(solution)/shard_map/jit(cholesky)/cholesky | solution.py:48
  575.0 2.9 convolution_subtract_fusion.11
  577.9 11.7 %cholesky.544 = f32[128,128]{1,0:T(8,128)S(1)} custom-call(f32[128,128]{1,0:T(8,128)S(1)} %cholesky.606), custom_call_target="Cholesky" | custom-call | tf_op jit(solution)/shard_map/jit(cholesky)/cholesky | solution.py:48
  590.4 9.8 %custom-call.68 = f32[1,128,128]{1,2,0:T(8,128)S(1)} custom-call(f32[1,128,128]{2,1,0:T(8,128)S(1)} %get-tuple-element.153), custom_call_target="InvertDiagBlocksLowerTriangular" | custom-call | tf_op jit(solution)/shard_map/jit(cholesky)/cholesky | solution.py:48
  601.1 2.2 convolution_subtract_fusion.13
  603.3 11.7 %cholesky.562 = f32[128,128]{1,0:T(8,128)S(1)} custom-call(f32[128,128]{1,0:T(8,128)S(1)} %convolution_subtract_fusion.13), custom_call_target="Cholesky" | custom-call | tf_op jit(solution)/shard_map/jit(cholesky)/cholesky | solution.py:48
  626.2 6.8 fusion.5
  632.9 28.2 %while.14 = (s32[]{:T(128)}, f32[1024,1024]{0,1:T(8,128)}, s32[8,2]{0,1:T(2,128)S(1)}, f32[8,128,128]{2,1,0:T(8,128)}) while((s32[]{:T(128)}, f32[1024,1024]{0,1:T(8,128)}, s32[8,2]{0,1:T(2,128)S(1)}, f32[8,128,128]{2,1,0:T(8,128)}) %tuple.103), condition=%wide.while_cond.clone, body=%wide.while_body.sunk.clone | while | flops 2 | bytes 393321 | solution.py:50
  633.6 2.2 dynamic-slice.14
  637.1 2.2 dynamic-slice.14
  644.2 2.2 dynamic-slice.14
  647.7 2.2 dynamic-slice.14
  661.2 79.4 %custom-call.69 = f32[8,128,128]{1,2,0:T(8,128)S(1)} custom-call(f32[8,128,128]{2,1,0:T(8,128)} %get-tuple-element.78), custom_call_target="InvertDiagBlocksLowerTriangular" | custom-call | tf_op jit(solution)/shard_map/triangular_solve | solution.py:50
  748.7 2.2 convolution_subtract_fusion.5
  751.3 2.4 convolution_subtract_fusion.9
  754.0 2.7 convolution_subtract_fusion.12
  (194 shorter events, 84.7 us)
Async XLA Ops:
  7.2 13.0 %copy-start.1 = (f32[1,256,1024]{2,1,0:T(8,128)S(1)}, f32[1,256,1024]{2,1,0:T(8,128)}, u32[]{:S(2)}) copy-start(f32[1,256,1024]{2,1,0:T(8,128)} %param.9) | copy-start | bytes 3145732
  11.8 32.8 %all-to-all-start = ((f32[16,32,1024]{2,1,0:T(8,128)}), f32[16,32,1024]{2,1,0:T(8,128)S(1)}, u32[]{:S(2)}, u32[]{:S(2)}) async-start(f32[16,32,1024]{2,1,0:T(8,128)} %broadcast_select_fusion), calls=%async_computation | async-start | bytes 4194304 | tf_op jit(solution)/shard_map/all_to_all | solution.py:33
  19.4 379.7 %all-reduce.3.cloned.1.call-start = ((), (), s32[]{:S(2)}) async-start(), calls=%async_computation.1 | async-start | bytes 8388608 | tf_op jit(solution)/shard_map/psum | solution.py:12
  21.2 28.0 %copy-start.3 = (s32[16]{0:T(128)S(1)}, s32[16]{0:T(128)}, u32[]{:S(2)}) copy-start(s32[16]{0:T(128)} %param.12) | copy-start | bytes 196
  49.2 42.9 %copy-start.2 = (f32[256,1024]{1,0:T(8,128)S(1)}, f32[256,1024]{1,0:T(8,128)}, u32[]{:S(2)}) copy-start(f32[256,1024]{1,0:T(8,128)} %bitcast_select_fusion) | copy-start | bytes 3145732
  414.1 1.9 copy-start
Sparse Core Ops, SparseCore 0:
  167.2 231.8 all-reduce.2
where the time goes:
time: 776 us; the launch traced here: 767 us
  other arithmetic  274 us (35%)
  waiting for transfers between devices  255 us (33%)
  local copies, waits for them, and re-layouts  82.2 us (11%)
  blocking collectives  59.2 us (8%)
  matrix products  58.7 us (8%)
  between operations  19.7 us (3%)
  loops' own time  10.4 us (1%)
    psum x1, waiting for transfers between devices, reduce_gram(): return lax.psum(local, 'rows')  232 us
    another operation x31, other arithmetic, body(): lower = jnp.linalg.cholesky(gram)  168 us
    another operation x3, other arithmetic, body(): lax.linalg.triangular_solve(lower, own_live * scale[None, :], left_side=F...  86.2 us
    psum x1, blocking collectives, body(): squares = lax.psum(jnp.sum(stacked * stacked, axis=0), 'rows')  59.2 us
    another operation x14, matrix products, body(): lower = jnp.linalg.cholesky(gram)  28.6 us
    another operation x40, local copies, waits for them, and re-layouts  28.1 us
    all_to_all x1, waiting for transfers between devices, body(): lax.all_to_all(buffer, 'front', split_axis=0, concat_axis=0, tiled=True)  23.4 us
    another operation x15, matrix products, body(): lax.linalg.triangular_solve(lower, own_live * scale[None, :], left_side=F...  16.4 us
  transfers between devices with their start and end apart: 2, of which 2 were waited for; matrix products, arithmetic and copies ran while one was open for 0% of the time, Pallas kernels for 0%

commit v1 on v0

v1 whole, which is shorter than its diff:
```python
import jax
import jax.numpy as jnp
from jax import lax
from jax.experimental import pallas as pl
from jax.experimental.pallas import tpu as pltpu
from jax.sharding import PartitionSpec as P

F32 = jnp.float32
LB = 128
NN = ((1,), (0,))
TN = ((0,), (0,))
NT = ((1,), (1,))
VMEM = pl.BlockSpec(memory_space=pltpu.VMEM)
SMEM = pl.BlockSpec(memory_space=pltpu.SMEM)
PARAMS = pltpu.CompilerParams(vmem_limit_bytes=48 << 20)


def split(x):
    hi = x.astype(jnp.bfloat16)
    lo = (x - hi.astype(F32)).astype(jnp.bfloat16)
    return hi, lo


def dot(a, b, dims):
    return lax.dot_general(a, b, (dims, ((), ())), preferred_element_type=F32)


def dot3(a, b, dims):
    return dot(a[0], b[0], dims) + (dot(a[0], b[1], dims) + dot(a[1], b[0], dims))


def upper_blocks(width):
    n = width // LB
    return [(i, j) for i in range(n) for j in range(i, n)]


def map_kernel(tile_ref, map_ref, out_ref):
    width = tile_ref.shape[1]
    rows = tile_ref.shape[0]
    tile = tile_ref[...]
    first = tile.astype(jnp.bfloat16)
    rest = tile - first.astype(F32)
    second = rest.astype(jnp.bfloat16)
    third = (rest - second.astype(F32)).astype(jnp.bfloat16)
    parts = jnp.concatenate([first, second, third], axis=0)
    for i in range(width // LB):
        target = lax.broadcasted_iota(jnp.int32, (LB, width), 0) + i * LB
        onehot = (target == map_ref[...]).astype(F32).astype(jnp.bfloat16)
        moved = dot(parts, onehot, NT)
        out_ref[:, i * LB : (i + 1) * LB] = (
            moved[:rows] + moved[rows : 2 * rows] + moved[2 * rows :]
        )


def map_columns(tile, cmap):
    return pl.pallas_call(
        map_kernel,
        out_shape=jax.ShapeDtypeStruct(tile.shape, F32),
        in_specs=[VMEM, VMEM],
        out_specs=VMEM,
        compiler_params=PARAMS,
        name="map_columns",
    )(tile, cmap)


def gram_kernel(live_ref, own_ref, arrived_ref, out_ref, hi_ref, lo_ref):
    local, width = own_ref.shape
    rows = lax.broadcasted_iota(jnp.int32, own_ref.shape, 0)
    own = jnp.where(rows < live_ref[0], own_ref[...], F32(0))
    hi, lo = split(own)
    hi_ref[:local, :] = hi
    lo_ref[:local, :] = lo
    hi, lo = split(arrived_ref[...])
    hi_ref[local:, :] = hi
    lo_ref[local:, :] = lo
    at = 0
    for i in range(width // LB):
        left = slice(i * LB, (i + 1) * LB)
        right = slice(i * LB, width)
        strip = dot3(
            (hi_ref[:, left], lo_ref[:, left]), (hi_ref[:, right], lo_ref[:, right]), TN
        )
        for j in range(strip.shape[1] // LB):
            out_ref[at : at + LB, :] = strip[:, j * LB : (j + 1) * LB]
            at += LB


def packed_gram(live, own, arrived):
    total = own.shape[0] + arrived.shape[0]
    width = own.shape[1]
    return pl.pallas_call(
        gram_kernel,
        out_shape=jax.ShapeDtypeStruct((len(upper_blocks(width)) * LB, LB), F32),
        in_specs=[SMEM, VMEM, VMEM],
        out_specs=VMEM,
        scratch_shapes=[
            pltpu.VMEM((total, width), jnp.bfloat16),
            pltpu.VMEM((total, width), jnp.bfloat16),
        ],
        compiler_params=PARAMS,
        name="packed_gram",
    )(live, own, arrived)


def row8(x, i):
    return jnp.broadcast_to(x[i : i + 1, :], (8, LB))


def lane8(x, j):
    return jnp.broadcast_to(x[:, j : j + 1], (8, LB))


def total8(terms):
    while len(terms) > 1:
        terms = [terms[i] + terms[i + 1] for i in range(0, len(terms), 2)]
    return terms[0]


def factor_block(slabs):
    count = len(slabs)
    sub = lax.broadcasted_iota(jnp.int32, (8, LB), 0)
    lane = lax.broadcasted_iota(jnp.int32, (8, LB), 1)
    inv = [jnp.where(lane == sub + 8 * v, F32(1), F32(0)) for v in range(count)]
    slabs = list(slabs)
    r_out, inv_out = [], []
    for b in range(count):
        t, x = slabs[b], inv[b]
        cols = [lane8(t, 8 * b + j) for j in range(8)]
        a = [[row8(cols[j], i) if i <= j else None for j in range(8)] for i in range(8)]
        r = [row8(t, i) for i in range(8)]
        y = [row8(x, i) for i in range(8)]
        rd = [None] * 8
        m = [[None] * 8 for _ in range(8)]
        for k in range(8):
            rd[k] = 1.0 / a[k][k]
            for j in range(k + 1, 8):
                m[k][j] = a[k][j] * rd[k]
                for i in range(j, 8):
                    a[j][i] = a[j][i] - m[k][j] * a[k][i]
                r[j] = r[j] - m[k][j] * r[k]
                y[j] = y[j] - m[k][j] * y[k]
        pivots, rows, invs = a[0][0], r[0], y[0]
        for k in range(1, 8):
            pivots = jnp.where(sub == k, a[k][k], pivots)
            rows = jnp.where(sub == k, r[k], rows)
            invs = jnp.where(sub == k, y[k], invs)
        rs = lax.rsqrt(pivots)
        r_out.append(jnp.where(lane >= sub + 8 * b, rows * rs, F32(0)))
        inv_out.append(invs * rs)
        if b + 1 < count:
            z, w = [None] * 8, [None] * 8
            for k in reversed(range(8)):
                z[k] = r[k] * rd[k]
                w[k] = y[k] * rd[k]
                for i in range(k + 1, 8):
                    z[k] = z[k] - m[k][i] * z[i]
                    w[k] = w[k] - m[k][i] * w[i]
            for v in range(b + 1, count):
                cv = [lane8(slabs[v], 8 * b + j) for j in range(8)]
                slabs[v] = slabs[v] - total8([cv[j] * z[j] for j in range(8)])
                inv[v] = inv[v] - total8([cv[j] * w[j] for j in range(8)])
    return r_out, inv_out


def factor_kernel(total_rows, where_ref, packed_ref, own_ref, r_ref, q_ref, a_ref, inv_ref):
    local, width = own_ref.shape
    n = width // LB
    diag = lax.broadcasted_iota(jnp.int32, (LB, LB), 0) == lax.broadcasted_iota(
        jnp.int32, (LB, LB), 1
    )
    blocks = upper_blocks(width)
    across, down = [], []
    for i in range(n):
        at = blocks.index((i, i)) * LB
        only = jnp.where(diag, packed_ref[at : at + LB, :], F32(0))
        across.append(
            lax.rsqrt(jnp.sum(only, axis=0, keepdims=True) / total_rows + F32(1e-6))
        )
        down.append(lax.rsqrt(jnp.sum(only, axis=1, keepdims=True) / total_rows + F32(1e-6)))
    shift = jnp.where(diag, F32(0.25 * total_rows), F32(0))
    for at, (i, j) in enumerate(blocks):
        block = packed_ref[at * LB : (at + 1) * LB, :] * down[i] * across[j]
        if i == j:
            block = block + shift
        a_ref[i * LB : (i + 1) * LB, j * LB : (j + 1) * LB] = block
    rows = lax.broadcasted_iota(jnp.int32, (local, LB), 0)
    for j in range(n):
        cols = slice(j * LB, (j + 1) * LB)
        q_ref[:, cols] = jnp.where(rows < where_ref[0], own_ref[:, cols] * across[j], F32(0))
    column = lax.broadcasted_iota(jnp.int32, (LB, width), 1)

    def step(k, carry):
        o = pl.multiple_of(k * LB, LB)
        r_rows, inv_rows = factor_block(
            [a_ref[pl.ds(o + 8 * v, 8), pl.ds(o, LB)] for v in range(LB // 8)]
        )
        for v in range(LB // 8):
            inv_ref[8 * v : 8 * v + 8, :] = inv_rows[v]
        inv = split(inv_ref[...])
        strip = dot3(inv, split(a_ref[pl.ds(o, LB), :]), NN)
        strip = jnp.where(column >= o + LB, strip, F32(0))
        a_ref[pl.ds(o, LB), :] = strip
        for v in range(LB // 8):
            a_ref[pl.ds(o + 8 * v, 8), pl.ds(o, LB)] = r_rows[v]
        strip = split(strip)
        q_now = dot3(split(q_ref[:, pl.ds(o, LB)]), inv, NT)
        q_ref[...] = q_ref[...] - dot3(split(q_now), strip, NN)
        q_ref[:, pl.ds(o, LB)] = q_now

        def update(i, carry):
            oi = pl.multiple_of(i * LB, LB)
            mine = split(a_ref[pl.ds(o, LB), pl.ds(oi, LB)])
            a_ref[pl.ds(oi, LB), :] = a_ref[pl.ds(oi, LB), :] - dot3(mine, strip, TN)
            return carry

        lax.fori_loop(k + 1, n, update, 0)
        return carry

    lax.fori_loop(0, n, step, 0)
    r_ref[...] = a_ref[pl.ds(pl.multiple_of(where_ref[1], 8), r_ref.shape[0]), :]


def factor(where, packed, own, out_rows, total_rows):
    width = own.shape[1]
    return pl.pallas_call(
        lambda *refs: factor_kernel(total_rows, *refs),
        out_shape=(
            jax.ShapeDtypeStruct((out_rows, width), F32),
            jax.ShapeDtypeStruct(own.shape, F32),
        ),
        in_specs=[SMEM, VMEM, VMEM],
        out_specs=(VMEM, VMEM),
        scratch_shapes=[pltpu.VMEM((width, width), F32), pltpu.VMEM((LB, LB), F32)],
        compiler_params=PARAMS,
        name="factor",
    )(where, packed, own)


def shift_z(x, k, devices):
    return lax.ppermute(x, "rows", [(i, (i + 2 * k) % devices) for i in range(devices)])


def sum_over_rows(packed, devices):
    me = lax.axis_index("rows")
    core, z = me % 2, me // 2
    length = packed.shape[0]
    half, quarter = length // 2, length // 8
    pairs = [(i, i ^ 1) for i in range(devices)]
    chips = devices // 2
    classes = [
        [2 * (a + 4 * i) + c for i in range(chips // 4)] for c in range(2) for a in range(4)
    ]
    cut = lambda x, at, size: lax.dynamic_slice_in_dim(x, at, size, 0)
    mine = cut(packed, core * half, half) + lax.ppermute(
        cut(packed, (1 - core) * half, half), "rows", pairs
    )
    part = lambda k: cut(mine, ((z + k) % 4) * quarter, quarter)
    from_left = shift_z(part(1), 1, devices)
    from_right = shift_z(part(3), -1, devices)
    far = part(2)
    far_left = shift_z(far[: quarter // 2], 2, devices)
    far_right = shift_z(far[quarter // 2 :], -2, devices)
    summed = part(0) + from_left + from_right + jnp.concatenate([far_left, far_right])
    pieces = lax.all_to_all(
        summed, "rows", split_axis=0, concat_axis=0, axis_index_groups=classes, tiled=True
    )
    done = jnp.sum(pieces.reshape(chips // 4, -1, LB), axis=0)
    whole = lax.all_gather(done, "rows", axis=0, axis_index_groups=classes, tiled=True)
    left = shift_z(whole, 1, devices)
    right = shift_z(whole, -1, devices)
    far_left = shift_z(whole[: quarter // 2], 2, devices)
    far_right = shift_z(whole[quarter // 2 :], -2, devices)
    stack = jnp.stack([whole, right, jnp.concatenate([far_left, far_right]), left])
    order = (jnp.arange(4) - z) % 4
    mine = jnp.take(stack, order, axis=0).reshape(half, LB)
    other = lax.ppermute(mine, "rows", pairs)
    return jnp.where(
        core == 0, jnp.concatenate([mine, other]), jnp.concatenate([other, mine])
    )


def body(own_rows, child_tile, col_map, parent, live_rows):
    group = lax.axis_index("front")
    place = lax.axis_index("rows")
    groups = lax.axis_size("front")
    devices = lax.axis_size("rows")
    own, tile = own_rows[0], child_tile[0]
    local, width = own.shape
    tile_rows = tile.shape[0]
    fronts = jnp.arange(groups, dtype=jnp.int32)
    live = lax.dynamic_index_in_dim(live_rows, group, keepdims=False)
    my_parent = lax.dynamic_index_in_dim(parent, group, keepdims=False)
    mapped = map_columns(tile, lax.dynamic_slice_in_dim(col_map, group, 1, 0))
    buffer = jnp.where((fronts == my_parent)[:, None, None], mapped[None], F32(0))
    arrived = lax.all_to_all(buffer, "front", split_axis=0, concat_axis=0, tiled=True)
    where = jnp.stack([live - place * local, place * tile_rows]).astype(jnp.int32)
    packed = packed_gram(where, own, arrived.reshape(-1, width))
    packed = sum_over_rows(packed, devices)
    r_rows, panel = factor(where, packed, own, tile_rows, local * devices)
    return (r_rows[None], panel[None])


def solution(mesh):
    placed = (P("front", "rows", None), P("front", "rows", None), P(), P(), P())
    return jax.shard_map(
        body,
        mesh=mesh,
        in_specs=placed,
        out_specs=(P("front", "rows", None), P("front", "rows", None)),
        check_vma=False,
    )
```

time: 776 us -> 236 us (0.30); the launches traced: 767 us -> 235 us
  other arithmetic: 274 us -> 7.17 us
  waiting for transfers between devices: 255 us -> 59.1 us
  Pallas kernels: 0 us -> 72.7 us
  local copies, waits for them, and re-layouts: 82.2 us -> 10.5 us
  starting transfers between devices: 7.62 us -> 67.2 us
  matrix products: 58.7 us -> 0 us
  blocking collectives: 59.2 us -> 17.1 us
  between operations: 19.7 us -> 1.64 us
  loops' own time: 10.4 us -> 0 us
    another operation x34 -> x3, other arithmetic: 255 us -> 0.17 us  [the longest x2 0.1 us: sum_over_rows(): jnp.stack([whole, right, jnp.concatenate([far_left, far_right]), left])]
    psum x1 -> x0, waiting for transfers between devices: 232 us -> none  [reduce_gram(): return lax.psum(local, 'rows')]
    pallas_call x0 -> x3, Pallas kernels: none -> 72.7 us  [the longest x1 67.7 us: factor(): pl.pallas_call(lambda *refs: factor_kernel(total_rows, *refs), out_shape=...]
    psum x1 -> x0, blocking collectives: 59.2 us -> none  [body(): squares = lax.psum(jnp.sum(stacked * stacked, axis=0), 'rows')]
    ppermute x0 -> x10, starting transfers between devices: none -> 50.2 us  [the longest x8 40 us: shift_z(): lax.ppermute(x, 'rows', [(i, (i + 2 * k) % devices) for i in range(device...]
    another operation x29 -> x0, matrix products: 45 us -> none  [the longest x14 28.6 us: body(): lower = jnp.linalg.cholesky(gram)]
    another operation x64 -> x0, local copies, waits for them, and re-layouts: 35.9 us -> none
    ppermute x0 -> x10, waiting for transfers between devices: none -> 19.6 us  [the longest x8 14.6 us: shift_z(): lax.ppermute(x, 'rows', [(i, (i + 2 * k) % devices) for i in range(device...]
  transfers between devices with their start and end apart: 2 -> 12, of which waited for: 2 -> 8; matrix products, arithmetic and copies ran while one was open for 0% -> 1% of each run, Pallas kernels for 0% -> 0%
where the time goes in v1:
time: 236 us; the launch traced here: 235 us
  Pallas kernels  72.7 us (31%)
  starting transfers between devices  67.2 us (28%)
  waiting for transfers between devices  59.1 us (25%)
  blocking collectives  17.1 us (7%)
  local copies, waits for them, and re-layouts  10.5 us (4%)
  other arithmetic  7.17 us (3%)
    pallas_call x1, Pallas kernels, factor(): pl.pallas_call(lambda *refs: factor_kernel(total_rows, *refs), out_shape=...  67.7 us
    ppermute x8, starting transfers between devices, shift_z(): lax.ppermute(x, 'rows', [(i, (i + 2 * k) % devices) for i in range(device...  40 us
    all_to_all x1, waiting for transfers between devices, body(): lax.all_to_all(buffer, 'front', split_axis=0, concat_axis=0, tiled=True)  23.9 us
    all_gather x1, blocking collectives, sum_over_rows(): lax.all_gather(done, 'rows', axis=0, axis_index_groups=classes, tiled=True)  17.1 us
    all_to_all x1, waiting for transfers between devices, sum_over_rows(): lax.all_to_all(summed, 'rows', split_axis=0, concat_axis=0, axis_index_gr...  15.7 us
    ppermute x8, waiting for transfers between devices, shift_z(): lax.ppermute(x, 'rows', [(i, (i + 2 * k) % devices) for i in range(device...  14.6 us
    all_to_all x1, starting transfers between devices, sum_over_rows(): lax.all_to_all(summed, 'rows', split_axis=0, concat_axis=0, axis_index_gr...  9.26 us
    all_to_all x1, starting transfers between devices, body(): lax.all_to_all(buffer, 'front', split_axis=0, concat_axis=0, tiled=True)  7.72 us
  transfers between devices with their start and end apart: 12, of which 8 were waited for; matrix products, arithmetic and copies ran while one was open for 1% of the time, Pallas kernels for 0%

profile of v1, /device:TPU:1, one launch (start us, length us, event | category | flops | bytes accessed | tf_op | source)
XLA Modules:
  0.0 235.4 jit_solution(6427232359717989705)
XLA Ops:
  0.6 0.0 copy-start
  0.7 0.8 copy-done
  1.5 1.2 dynamic_slice.29
  2.7 0.6 iota_compare_fusion
  3.4 0.0 copy-start.4
  3.4 0.9 copy-done.4
  4.3 0.8 map_columns.1
  5.1 1.7 broadcast_select_fusion
  6.7 7.7 %all-to-all-start = ((f32[16,32,1024]{2,1,0:T(8,128)}), f32[16,32,1024]{2,1,0:T(8,128)S(1)}, u32[]{:S(2)}, u32[]{:S(2)}) async-start(f32[16,32,1024]{2,1,0:T(8,128)} %broadcast_select_fusion), calls=%async_computation | async-start | bytes 4194304 | tf_op jit(solution)/shard_map/all_to_all | solution.py:295
  14.5 0.6 dynamic_slice.28
  15.7 0.1 pad_add_fusion.live_ref.refs_0_
  15.8 23.9 %all-to-all-done = f32[16,32,1024]{2,1,0:T(8,128)S(1)} async-done(((f32[16,32,1024]{2,1,0:T(8,128)}), f32[16,32,1024]{2,1,0:T(8,128)S(1)}, u32[]{:S(2)}, u32[]{:S(2)}) %all-to-all-start) | async-done | bytes 2097184 | tf_op jit(solution)/shard_map/all_to_all | solution.py:295
  39.6 1.3 copy-done.1
  41.0 1.6 copy-done.2
  42.6 4.3 %packed_gram.1 = f32[4608,128]{1,0:T(8,128)S(1)} custom-call(s32[2]{0:T(128)S(1)} %pad_add_fusion.live_ref.refs_0_, f32[256,1024]{1,0:T(8,128)S(1)} %bitcast.20, f32[512,1024]{1,0:T(8,128)S(1)} %bitcast.19), custom_call_target="tpu_custom_call" | custom-call | tf_op jit(solution)/shard_map/packed_gram/pallas_call | solution.py:91
  46.9 1.1 constant_dynamic-slice_fusion.4
  48.0 7.6 %collective-permute-start = (f32[2304,128]{1,0:T(8,128)}, f32[2304,128]{1,0:T(8,128)}, u32[]{:S(2)}, u32[]{:S(2)}) collective-permute-start(f32[2304,128]{1,0:T(8,128)} %constant_dynamic-slice_fusion.4), channel_id=1, source_target_pairs={{0,1},{1,0},{2,3},{3,2},{4,5},{5,4},{6,7},{7,6},{8,9},{9,8},{10,11... | collective-permute-start | bytes 3538952 | tf_op jit(solution)/shard_map/ppermute | solution.py:254
  55.6 2.7 %collective-permute-done = f32[2304,128]{1,0:T(8,128)} collective-permute-done((f32[2304,128]{1,0:T(8,128)}, f32[2304,128]{1,0:T(8,128)}, u32[]{:S(2)}, u32[]{:S(2)}) %collective-permute-start) | collective-permute-done | bytes 1179680 | tf_op jit(solution)/shard_map/ppermute | solution.py:254
  58.4 1.4 dynamic-slice_add_fusion
  59.8 1.0 copy-done.5
  60.9 5.3 %collective-permute-start.1 = (f32[576,128]{1,0:T(8,128)S(1)}, f32[576,128]{1,0:T(8,128)S(1)}, u32[]{:S(2)}, u32[]{:S(2)}) collective-permute-start(f32[576,128]{1,0:T(8,128)S(1)} %get-tuple-element.6), channel_id=1, source_target_pairs={{0,2},{1,3},{2,4},{3,5},{4,6},{5,7},{6,8},{7,9},{8,10},{9,11},{10,... | collective-permute-start | bytes 884744 | tf_op jit(solution)/shard_map/ppermute | solution.py:240
  66.2 9.5 %collective-permute-start.2 = (f32[576,128]{1,0:T(8,128)S(1)}, f32[576,128]{1,0:T(8,128)S(1)}, u32[]{:S(2)}, u32[]{:S(2)}) collective-permute-start(f32[576,128]{1,0:T(8,128)S(1)} %get-tuple-element.7), channel_id=1, source_target_pairs={{0,30},{1,31},{2,0},{3,1},{4,2},{5,3},{6,4},{7,5},{8,6},{9,7},{10,... | collective-permute-start | bytes 884744 | tf_op jit(solution)/shard_map/ppermute | solution.py:240
  75.7 1.0 constant_dynamic-slice_fusion
  76.7 1.9 collective-permute-start.3
  78.7 5.5 %collective-permute-start.4 = (f32[288,128]{1,0:T(8,128)S(1)}, f32[288,128]{1,0:T(8,128)S(1)}, u32[]{:S(2)}, u32[]{:S(2)}) collective-permute-start(f32[288,128]{1,0:T(8,128)S(1)} %get-tuple-element.9), channel_id=1, source_target_pairs={{0,28},{1,29},{2,30},{3,31},{4,0},{5,1},{6,2},{7,3},{8,4},{9,5},{1... | collective-permute-start | bytes 442376 | tf_op jit(solution)/shard_map/ppermute | solution.py:240
  84.2 4.1 %collective-permute-done.3 = f32[288,128]{1,0:T(8,128)S(1)} collective-permute-done((f32[288,128]{1,0:T(8,128)S(1)}, f32[288,128]{1,0:T(8,128)S(1)}, u32[]{:S(2)}, u32[]{:S(2)}) %collective-permute-start.3) | collective-permute-done | bytes 147488 | tf_op jit(solution)/shard_map/ppermute | solution.py:240
  88.3 0.7 collective-permute-done.4
  89.0 0.0 collective-permute-done.1
  89.0 1.7 maximum_add_fusion
  90.7 9.3 %all-to-all-start.1 = ((f32[4,144,128]{2,1,0:T(8,128)}), f32[4,144,128]{2,1,0:T(8,128)S(1)}, u32[]{:S(2)}, u32[]{:S(2)}) async-start(f32[4,144,128]{2,1,0:T(8,128)} %bitcast.7), calls=%async_computation.1 | async-start | bytes 589824 | tf_op jit(solution)/shard_map/all_to_all | solution.py:264
  100.0 15.7 %all-to-all-done.1 = f32[4,144,128]{2,1,0:T(8,128)S(1)} async-done(((f32[4,144,128]{2,1,0:T(8,128)}), f32[4,144,128]{2,1,0:T(8,128)S(1)}, u32[]{:S(2)}, u32[]{:S(2)}) %all-to-all-start.1) | async-done | bytes 294944 | tf_op jit(solution)/shard_map/all_to_all | solution.py:264
  115.7 17.1 %all_gather.3 = f32[576,128]{1,0:T(8,128)S(1)} all-gather(f32[144,128]{1,0:T(8,128)S(1)} %reduce_sum.9), channel_id=1, replica_groups={{0,8,16,24},{2,10,18,26},{4,12,20,28},{6,14,22,30},{1,9,17,25},{3,11,19..., dimensions={0}, use_global_device_ids=true | all-gather | bytes 368640 | tf_op jit(solution)/shard_map/all_gather | solution.py:268
  132.8 1.9 collective-permute-start.8
  134.8 4.6 %collective-permute-start.5 = (f32[576,128]{1,0:T(8,128)S(1)}, f32[576,128]{1,0:T(8,128)S(1)}, u32[]{:S(2)}, u32[]{:S(2)}) collective-permute-start(f32[576,128]{1,0:T(8,128)S(1)} %all_gather.3), channel_id=1, source_target_pairs={{0,30},{1,31},{2,0},{3,1},{4,2},{5,3},{6,4},{7,5},{8,6},{9,7},{10,... | collective-permute-start | bytes 884744 | tf_op jit(solution)/shard_map/ppermute | solution.py:240
  139.3 9.4 %collective-permute-start.6 = (f32[288,128]{1,0:T(8,128)S(1)}, f32[288,128]{1,0:T(8,128)S(1)}, u32[]{:S(2)}, u32[]{:S(2)}) collective-permute-start(f32[288,128]{1,0:T(8,128)S(1)} %get-tuple-element.10), channel_id=1, source_target_pairs={{0,4},{1,5},{2,6},{3,7},{4,8},{5,9},{6,10},{7,11},{8,12},{9,13},{1... | collective-permute-start | bytes 442376 | tf_op jit(solution)/shard_map/ppermute | solution.py:240
  148.7 1.9 collective-permute-start.7
  150.7 0.1 broadcast_in_dim.42
  150.8 0.1 broadcast_in_dim.43
  150.9 1.1 collective-permute-done.6
  152.0 8.6 %collective-permute-done.7 = f32[288,128]{1,0:T(8,128)S(1)} collective-permute-done((f32[288,128]{1,0:T(8,128)S(1)}, f32[288,128]{1,0:T(8,128)S(1)}, u32[]{:S(2)}, u32[]{:S(2)}) %collective-permute-start.7) | collective-permute-done | bytes 147488 | tf_op jit(solution)/shard_map/ppermute | solution.py:240
  160.6 0.0 collective-permute-done.8
  160.7 0.1 pad_maximum_fusion
  160.7 0.6 gather_fusion
  161.4 1.2 bitcast_select_fusion
  162.6 2.6 %collective-permute-start.9 = (f32[2304,128]{1,0:T(8,128)S(1)}, f32[2304,128]{1,0:T(8,128)S(1)}, u32[]{:S(2)}, u32[]{:S(2)}) collective-permute-start(f32[2304,128]{1,0:T(8,128)S(1)} %bitcast_select_fusion), channel_id=1, source_target_pairs={{0,1},{1,0},{2,3},{3,2},{4,5},{5,4},{6,7},{7,6},{8,9},{9,8},{10,11... | collective-permute-start | bytes 3538952 | tf_op jit(solution)/shard_map/ppermute | solution.py:276
  165.3 2.3 collective-permute-done.9
  167.5 0.2 maximum_select_fusion.refs_1_
  167.8 67.7 %factor.1 = (f32[32,1024]{1,0:T(8,128)}, f32[256,1024]{1,0:T(8,128)}) custom-call(s32[2]{0:T(128)S(1)} %pad_add_fusion.live_ref.refs_0_, f32[4608,128]{1,0:T(8,128)S(1)} %maximum_select_fusion.refs_1_, f32[256,1024]{1,0:T(8,128)S(1)} %bitcast.21), custom_call_target="tpu_custom_call" | custom-call | tf_op jit(solution)/shard_map/factor/pallas_call | solution.py:225
  (17 shorter events, 0.2 us)
Async XLA Ops:
  0.6 0.8 copy-start
  3.4 0.9 copy-start.4
  6.7 7.7 %copy-start.6 = (s32[16]{0:T(128)S(1)}, s32[16]{0:T(128)}, u32[]{:S(2)}) copy-start(s32[16]{0:T(128)} %param.9) | copy-start | bytes 196
  6.7 34.3 %copy-start.3 = (f32[1,256,1024]{2,1,0:T(8,128)S(1)}, f32[1,256,1024]{2,1,0:T(8,128)}, u32[]{:S(2)}) copy-start(f32[1,256,1024]{2,1,0:T(8,128)} %param.5) | copy-start | bytes 3145732
  6.7 32.9 %all-to-all-start = ((f32[16,32,1024]{2,1,0:T(8,128)}), f32[16,32,1024]{2,1,0:T(8,128)S(1)}, u32[]{:S(2)}, u32[]{:S(2)}) async-start(f32[16,32,1024]{2,1,0:T(8,128)} %broadcast_select_fusion), calls=%async_computation | async-start | bytes 4194304 | tf_op jit(solution)/shard_map/all_to_all | solution.py:295
  39.6 1.3 copy-start.1
  41.0 1.6 copy-start.2
  48.0 10.4 %collective-permute-start = (f32[2304,128]{1,0:T(8,128)}, f32[2304,128]{1,0:T(8,128)}, u32[]{:S(2)}, u32[]{:S(2)}) collective-permute-start(f32[2304,128]{1,0:T(8,128)} %constant_dynamic-slice_fusion.4), channel_id=1, source_target_pairs={{0,1},{1,0},{2,3},{3,2},{4,5},{5,4},{6,7},{7,6},{8,9},{9,8},{10,11... | collective-permute-start | bytes 3538952 | tf_op jit(solution)/shard_map/ppermute | solution.py:254
  59.8 1.0 copy-start.5
  60.9 28.1 %collective-permute-start.1 = (f32[576,128]{1,0:T(8,128)S(1)}, f32[576,128]{1,0:T(8,128)S(1)}, u32[]{:S(2)}, u32[]{:S(2)}) collective-permute-start(f32[576,128]{1,0:T(8,128)S(1)} %get-tuple-element.6), channel_id=1, source_target_pairs={{0,2},{1,3},{2,4},{3,5},{4,6},{5,7},{6,8},{7,9},{8,10},{9,11},{10,... | collective-permute-start | bytes 884744 | tf_op jit(solution)/shard_map/ppermute | solution.py:240
  66.2 22.8 %collective-permute-start.2 = (f32[576,128]{1,0:T(8,128)S(1)}, f32[576,128]{1,0:T(8,128)S(1)}, u32[]{:S(2)}, u32[]{:S(2)}) collective-permute-start(f32[576,128]{1,0:T(8,128)S(1)} %get-tuple-element.7), channel_id=1, source_target_pairs={{0,30},{1,31},{2,0},{3,1},{4,2},{5,3},{6,4},{7,5},{8,6},{9,7},{10,... | collective-permute-start | bytes 884744 | tf_op jit(solution)/shard_map/ppermute | solution.py:240
  76.7 11.6 %collective-permute-start.3 = (f32[288,128]{1,0:T(8,128)S(1)}, f32[288,128]{1,0:T(8,128)S(1)}, u32[]{:S(2)}, u32[]{:S(2)}) collective-permute-start(f32[288,128]{1,0:T(8,128)S(1)} %get-tuple-element.8), channel_id=1, source_target_pairs={{0,4},{1,5},{2,6},{3,7},{4,8},{5,9},{6,10},{7,11},{8,12},{9,13},{1... | collective-permute-start | bytes 442376 | tf_op jit(solution)/shard_map/ppermute | solution.py:240
  78.7 10.3 %collective-permute-start.4 = (f32[288,128]{1,0:T(8,128)S(1)}, f32[288,128]{1,0:T(8,128)S(1)}, u32[]{:S(2)}, u32[]{:S(2)}) collective-permute-start(f32[288,128]{1,0:T(8,128)S(1)} %get-tuple-element.9), channel_id=1, source_target_pairs={{0,28},{1,29},{2,30},{3,31},{4,0},{5,1},{6,2},{7,3},{8,4},{9,5},{1... | collective-permute-start | bytes 442376 | tf_op jit(solution)/shard_map/ppermute | solution.py:240
  90.7 25.0 %all-to-all-start.1 = ((f32[4,144,128]{2,1,0:T(8,128)}), f32[4,144,128]{2,1,0:T(8,128)S(1)}, u32[]{:S(2)}, u32[]{:S(2)}) async-start(f32[4,144,128]{2,1,0:T(8,128)} %bitcast.7), calls=%async_computation.1 | async-start | bytes 589824 | tf_op jit(solution)/shard_map/all_to_all | solution.py:264
  132.8 27.8 %collective-permute-start.8 = (f32[576,128]{1,0:T(8,128)S(1)}, f32[576,128]{1,0:T(8,128)S(1)}, u32[]{:S(2)}, u32[]{:S(2)}) collective-permute-start(f32[576,128]{1,0:T(8,128)S(1)} %all_gather.3), channel_id=1, source_target_pairs={{0,2},{1,3},{2,4},{3,5},{4,6},{5,7},{6,8},{7,9},{8,10},{9,11},{10,... | collective-permute-start | bytes 884744 | tf_op jit(solution)/shard_map/ppermute | solution.py:240
  134.8 25.9 %collective-permute-start.5 = (f32[576,128]{1,0:T(8,128)S(1)}, f32[576,128]{1,0:T(8,128)S(1)}, u32[]{:S(2)}, u32[]{:S(2)}) collective-permute-start(f32[576,128]{1,0:T(8,128)S(1)} %all_gather.3), channel_id=1, source_target_pairs={{0,30},{1,31},{2,0},{3,1},{4,2},{5,3},{6,4},{7,5},{8,6},{9,7},{10,... | collective-permute-start | bytes 884744 | tf_op jit(solution)/shard_map/ppermute | solution.py:240
  139.3 12.6 %collective-permute-start.6 = (f32[288,128]{1,0:T(8,128)S(1)}, f32[288,128]{1,0:T(8,128)S(1)}, u32[]{:S(2)}, u32[]{:S(2)}) collective-permute-start(f32[288,128]{1,0:T(8,128)S(1)} %get-tuple-element.10), channel_id=1, source_target_pairs={{0,4},{1,5},{2,6},{3,7},{4,8},{5,9},{6,10},{7,11},{8,12},{9,13},{1... | collective-permute-start | bytes 442376 | tf_op jit(solution)/shard_map/ppermute | solution.py:240
  148.7 11.9 %collective-permute-start.7 = (f32[288,128]{1,0:T(8,128)S(1)}, f32[288,128]{1,0:T(8,128)S(1)}, u32[]{:S(2)}, u32[]{:S(2)}) collective-permute-start(f32[288,128]{1,0:T(8,128)S(1)} %get-tuple-element.11), channel_id=1, source_target_pairs={{0,28},{1,29},{2,30},{3,31},{4,0},{5,1},{6,2},{7,3},{8,4},{9,5},{1... | collective-permute-start | bytes 442376 | tf_op jit(solution)/shard_map/ppermute | solution.py:240
  162.6 4.9 %collective-permute-start.9 = (f32[2304,128]{1,0:T(8,128)S(1)}, f32[2304,128]{1,0:T(8,128)S(1)}, u32[]{:S(2)}, u32[]{:S(2)}) collective-permute-start(f32[2304,128]{1,0:T(8,128)S(1)} %bitcast_select_fusion), channel_id=1, source_target_pairs={{0,1},{1,0},{2,3},{3,2},{4,5},{5,4},{6,7},{7,6},{8,9},{9,8},{10,11... | collective-permute-start | bytes 3538952 | tf_op jit(solution)/shard_map/ppermute | solution.py:276

commit v2 on v1

v2 whole, which is shorter than its diff:
```python
import functools

import jax
import jax.numpy as jnp
from jax import lax
from jax.experimental import pallas as pl
from jax.experimental.pallas import tpu as pltpu
from jax.sharding import PartitionSpec as P

F32 = jnp.float32
LB = 128
NN = ((1,), (0,))
TN = ((0,), (0,))
NT = ((1,), (1,))
VMEM = pl.BlockSpec(memory_space=pltpu.VMEM)
SMEM = pl.BlockSpec(memory_space=pltpu.SMEM)
PARAMS = pltpu.CompilerParams(vmem_limit_bytes=48 << 20)


def split(x):
    hi = x.astype(jnp.bfloat16)
    lo = (x - hi.astype(F32)).astype(jnp.bfloat16)
    return hi, lo


def dot(a, b, dims):
    return lax.dot_general(a, b, (dims, ((), ())), preferred_element_type=F32)


def dot3(a, b, dims):
    return dot(a[0], b[0], dims) + (dot(a[0], b[1], dims) + dot(a[1], b[0], dims))


def upper_blocks(width):
    n = width // LB
    return [(i, j) for i in range(n) for j in range(i, n)]


def place_kernel(at_ref, tile_ref, map_ref, out_ref):
    rows, width = tile_ref.shape
    tile = tile_ref[...]
    first = tile.astype(jnp.bfloat16)
    rest = tile - first.astype(F32)
    second = rest.astype(jnp.bfloat16)
    third = (rest - second.astype(F32)).astype(jnp.bfloat16)
    parts = jnp.concatenate([first, second, third], axis=0)
    columns = map_ref[pl.ds(at_ref[0], 1), :]
    out_ref[...] = jnp.zeros(out_ref.shape, F32)
    for i in range(width // LB):
        target = lax.broadcasted_iota(jnp.int32, (LB, width), 0) + i * LB
        onehot = (target == columns).astype(F32).astype(jnp.bfloat16)
        moved = dot(parts, onehot, NT)
        out_ref[at_ref[1], :, i * LB : (i + 1) * LB] = (
            moved[:rows] + moved[rows : 2 * rows] + moved[2 * rows :]
        )


def place_child(at, tile, col_map):
    return pl.pallas_call(
        place_kernel,
        out_shape=jax.ShapeDtypeStruct((col_map.shape[0],) + tile.shape, F32),
        in_specs=[SMEM, VMEM, VMEM],
        out_specs=VMEM,
        compiler_params=PARAMS,
        name="place_child",
    )(at, tile, col_map)


def own_gram_kernel(place_ref, own_ref, out_ref, hi_ref, lo_ref):
    width = own_ref.shape[1]
    rows = lax.broadcasted_iota(jnp.int32, own_ref.shape, 0)
    own = jnp.where(rows < place_ref[0], own_ref[...], F32(0))
    hi_ref[...], lo_ref[...] = split(own)
    at = 0
    for i in range(width // LB):
        left = slice(i * LB, (i + 1) * LB)
        right = slice(i * LB, width)
        strip = dot3(
            (hi_ref[:, left], lo_ref[:, left]), (hi_ref[:, right], lo_ref[:, right]), TN
        )
        for j in range(strip.shape[1] // LB):
            out_ref[at : at + LB, :] = strip[:, j * LB : (j + 1) * LB]
            at += LB


def own_gram(place, own):
    width = own.shape[1]
    return pl.pallas_call(
        own_gram_kernel,
        out_shape=jax.ShapeDtypeStruct((len(upper_blocks(width)) * LB, LB), F32),
        in_specs=[SMEM, VMEM],
        out_specs=VMEM,
        scratch_shapes=[pltpu.VMEM(own.shape, jnp.bfloat16)] * 2,
        compiler_params=PARAMS,
        name="own_gram",
    )(place, own)


def packed_rows(at, chip, half):
    quarter = half // 4
    piece = LB // 2
    side, first = divmod(at * LB, half)
    found = []
    for s in range(2):
        q, inner = divmod(first + s * piece, quarter)
        found.append(pl.multiple_of(((q + 4 - chip % 4) % 4) * quarter + inner, piece))
    return side, found


def gram_kernel(place_ref, mine_ref, arrived_ref, keep_ref, send_ref, hi_ref, lo_ref):
    width = arrived_ref.shape[1]
    half = keep_ref.shape[0]
    core, chip = place_ref[2], place_ref[3]
    hi_ref[...], lo_ref[...] = split(arrived_ref[...])
    piece = LB // 2
    at = 0
    for i in range(width // LB):
        left = slice(i * LB, (i + 1) * LB)
        right = slice(i * LB, width)
        strip = dot3(
            (hi_ref[:, left], lo_ref[:, left]), (hi_ref[:, right], lo_ref[:, right]), TN
        )
        for j in range(strip.shape[1] // LB):
            block = strip[:, j * LB : (j + 1) * LB] + mine_ref[at * LB : (at + 1) * LB, :]
            side, rows = packed_rows(at, chip, half)
            for s in range(2):

                def put(ref, s=s, rows=rows, block=block):
                    ref[pl.ds(rows[s], piece), :] = block[s * piece : (s + 1) * piece]

                pl.when(core == side)(lambda: put(keep_ref))
                pl.when(core != side)(lambda: put(send_ref))
            at += 1


def add_children(place, mine, arrived):
    half = jax.ShapeDtypeStruct((mine.shape[0] // 2, LB), F32)
    return pl.pallas_call(
        gram_kernel,
        out_shape=(half, half),
        in_specs=[SMEM, VMEM, VMEM],
        out_specs=(VMEM, VMEM),
        scratch_shapes=[pltpu.VMEM(arrived.shape, jnp.bfloat16)] * 2,
        compiler_params=PARAMS,
        name="add_children",
    )(place, mine, arrived)


def row8(x, i):
    return jnp.broadcast_to(x[i : i + 1, :], (8, LB))


def lane8(x, j):
    return jnp.broadcast_to(x[:, j : j + 1], (8, LB))


def total8(terms):
    while len(terms) > 1:
        terms = [terms[i] + terms[i + 1] for i in range(0, len(terms), 2)]
    return terms[0]


def factor_block(slabs):
    count, panel = len(slabs), 4
    sub = lax.broadcasted_iota(jnp.int32, (8, LB), 0)
    lane = lax.broadcasted_iota(jnp.int32, (8, LB), 1)
    inv = [jnp.where(lane == sub + 8 * v, F32(1), F32(0)) for v in range(count)]
    slabs = list(slabs)
    r_out, inv_out = [], []
    for p in range(0, count, panel):
        end = p + panel
        here = [jnp.maximum(lane8(slabs[p], 8 * p + j), F32(-3e38)) for j in range(8)]
        for b in range(p, end):
            a = [[row8(here[j], i) if i <= j else None for j in range(8)] for i in range(8)]
            r = [row8(slabs[b], i) for i in range(8)]
            y = [row8(inv[b], i) for i in range(8)]
            rd = [None] * 8
            m = [[None] * 8 for _ in range(8)]
            vectors = [r, y]
            if b + 1 < end:
                c = [lane8(slabs[b + 1], 8 * b + j) for j in range(8)]
                here = [lane8(slabs[b + 1], 8 * (b + 1) + j) for j in range(8)]
                vectors.append(c)
            for k in range(8):
                rd[k] = 1.0 / a[k][k]
                for j in range(k + 1, 8):
                    m[k][j] = a[k][j] * rd[k]
                    for i in range(j, 8):
                        a[j][i] = a[j][i] - m[k][j] * a[k][i]
                    for vector in vectors:
                        vector[j] = vector[j] - m[k][j] * vector[k]
            pivots, rows, invs = a[0][0], r[0], y[0]
            for k in range(1, 8):
                pivots = jnp.where(sub == k, a[k][k], pivots)
                rows = jnp.where(sub == k, r[k], rows)
                invs = jnp.where(sub == k, y[k], invs)
            rs = lax.rsqrt(pivots)
            r_out.append(jnp.where(lane >= sub + 8 * b, rows * rs, F32(0)))
            inv_out.append(invs * rs)
            if b + 1 == end:
                continue
            u = [c[j] * rd[j] for j in range(8)]
            for j in range(8):
                slabs[b + 1] = slabs[b + 1] - u[j] * r[j]
                inv[b + 1] = inv[b + 1] - u[j] * y[j]
            for j in range(8):
                for k in range(8):
                    here[j] = here[j] - u[k] * row8(c[k], j)
            if b + 2 == end:
                continue
            z, w = [None] * 8, [None] * 8
            for k in reversed(range(8)):
                z[k] = r[k] * rd[k]
                w[k] = y[k] * rd[k]
                for i in range(k + 1, 8):
                    z[k] = z[k] - m[k][i] * z[i]
                    w[k] = w[k] - m[k][i] * w[i]
            for v in range(b + 2, end):
                cv = [lane8(slabs[v], 8 * b + j) for j in range(8)]
                slabs[v] = slabs[v] - total8([cv[j] * z[j] for j in range(8)])
                inv[v] = inv[v] - total8([cv[j] * w[j] for j in range(8)])
        if end < count:
            both = jnp.concatenate(
                [jnp.concatenate(x[p:end], axis=0) for x in (r_out, inv_out)], axis=1
            )
            hi, lo = split(both)
            taken = dot(
                jnp.concatenate([hi[:, :LB], hi[:, :LB], lo[:, :LB]], axis=0),
                jnp.concatenate([hi, lo, hi], axis=0),
                TN,
            )
            for v in range(end, count):
                slabs[v] = slabs[v] - taken[8 * v : 8 * v + 8, :LB]
                inv[v] = inv[v] - taken[8 * v : 8 * v + 8, LB:]
    return r_out, inv_out


def tall(a, axis):
    return jnp.concatenate([a[0], a[0], a[1]], axis=axis)


def wide(b, axis):
    return jnp.concatenate([b[0], b[1], b[0]], axis=axis)


def product(a, b, dims):
    return dot(tall(a, dims[0][0]), wide(b, dims[1][0]), dims)


def factor_kernel(
    total_rows, place_ref, mine_ref, other_ref, own_ref, r_ref, q_ref,
    a_ref, inv_ref, strip_ref, q_now_ref,
):
    local, width = own_ref.shape
    n = width // LB
    half = mine_ref.shape[0]
    core, chip = place_ref[2], place_ref[3]
    diag = lax.broadcasted_iota(jnp.int32, (LB, LB), 0) == lax.broadcasted_iota(
        jnp.int32, (LB, LB), 1
    )
    blocks = upper_blocks(width)

    def fetch(at):
        side, rows = packed_rows(at, chip, half)
        parts = [
            jnp.where(
                core == side, mine_ref[pl.ds(o, LB // 2), :], other_ref[pl.ds(o, LB // 2), :]
            )
            for o in rows
        ]
        return jnp.concatenate(parts, axis=0)

    across, down = [], []
    for i in range(n):
        only = jnp.where(diag, fetch(blocks.index((i, i))), F32(0))
        across.append(
            lax.rsqrt(jnp.sum(only, axis=0, keepdims=True) / total_rows + F32(1e-6))
        )
        down.append(lax.rsqrt(jnp.sum(only, axis=1, keepdims=True) / total_rows + F32(1e-6)))
    shift = jnp.where(diag, F32(0.25 * total_rows), F32(0))
    for at, (i, j) in enumerate(blocks):
        block = fetch(at) * down[i] * across[j]
        if i == j:
            block = block + shift
        a_ref[i * LB : (i + 1) * LB, j * LB : (j + 1) * LB] = block
    rows = lax.broadcasted_iota(jnp.int32, (local, LB), 0)
    for j in range(n):
        cols = slice(j * LB, (j + 1) * LB)
        q_ref[:, cols] = jnp.where(rows < place_ref[0], own_ref[:, cols] * across[j], F32(0))
    strip_ref[...] = jnp.zeros(strip_ref.shape, F32)
    q_now_ref[...] = jnp.zeros(q_now_ref.shape, F32)

    def step(first, k, carry):
        o = pl.multiple_of(k * LB, LB)
        left = first * LB
        slabs = [a_ref[pl.ds(o + 8 * v, 8), pl.ds(o, LB)] for v in range(LB // 8)]
        old = split(strip_ref[...])
        old_tall, old_wide = tall(old, 0), wide(old, 0)
        for i in range(first, n):
            at = slice(i * LB, (i + 1) * LB)
            a_ref[at, i * LB :] = a_ref[at, i * LB :] - dot(
                old_tall[:, at], old_wide[:, i * LB :], TN
            )
        q_ref[:, left:] = q_ref[:, left:] - dot(
            tall(split(q_now_ref[...]), 1), old_wide[:, left:], NN
        )
        r_rows, inv_rows = factor_block(slabs)
        for v in range(LB // 8):
            inv_ref[8 * v : 8 * v + 8, :] = inv_rows[v]
        inv = split(inv_ref[...])
        strip = product(inv, split(a_ref[pl.ds(o, LB), left:]), NN)
        column = lax.broadcasted_iota(jnp.int32, strip.shape, 1) + left
        strip = jnp.where(column >= o + LB, strip, F32(0))
        strip_ref[:, left:] = strip
        a_ref[pl.ds(o, LB), left:] = strip
        for v in range(LB // 8):
            a_ref[pl.ds(o + 8 * v, 8), pl.ds(o, LB)] = r_rows[v]
        after = pl.multiple_of(jnp.minimum(k + 1, n - 1) * LB, LB)
        new = split(strip_ref[:, pl.ds(after, LB)])
        a_ref[pl.ds(after, LB), pl.ds(after, LB)] = a_ref[
            pl.ds(after, LB), pl.ds(after, LB)
        ] - product(new, new, TN)
        q_now = product(split(q_ref[:, pl.ds(o, LB)]), inv, NT)
        q_now_ref[...] = q_now
        q_ref[:, pl.ds(o, LB)] = q_now
        return carry

    for first in (0, n // 2):
        lax.fori_loop(first, first + n // 2, functools.partial(step, first), 0)
    start = pl.multiple_of(place_ref[1], 8)
    mine = a_ref[pl.ds(start, r_ref.shape[0]), :]
    row = start + lax.broadcasted_iota(jnp.int32, mine.shape, 0)
    column = lax.broadcasted_iota(jnp.int32, mine.shape, 1)
    r_ref[...] = jnp.where(column >= row, mine, F32(0))


def factor(place, mine, other, own, out_rows, total_rows):
    local, width = own.shape
    return pl.pallas_call(
        functools.partial(factor_kernel, total_rows),
        out_shape=(
            jax.ShapeDtypeStruct((out_rows, width), F32),
            jax.ShapeDtypeStruct(own.shape, F32),
        ),
        in_specs=[SMEM, VMEM, VMEM, VMEM],
        out_specs=(VMEM, VMEM),
        scratch_shapes=[
            pltpu.VMEM((width, width), F32),
            pltpu.VMEM((LB, LB), F32),
            pltpu.VMEM((LB, width), F32),
            pltpu.VMEM((local, LB), F32),
        ],
        compiler_params=PARAMS,
        name="factor",
    )(place, mine, other, own)


def to_chip(x, k):
    devices = lax.axis_size("rows")
    return lax.ppermute(x, "rows", [(i, (i + 2 * k) % devices) for i in range(devices)])


def to_core(x):
    return lax.ppermute(x, "rows", [(i, i ^ 1) for i in range(lax.axis_size("rows"))])


def sum_over_rows(keep, send):
    chips = lax.axis_size("rows") // 2
    classes = [
        [2 * (a + 4 * i) + c for i in range(chips // 4)] for c in range(2) for a in range(4)
    ]
    quarter = keep.shape[0] // 4
    got = to_core(send)
    part = [
        keep[k * quarter : (k + 1) * quarter] + got[k * quarter : (k + 1) * quarter]
        for k in range(4)
    ]
    passing = to_chip(part[2], -1)
    before = to_chip(part[1], 1)
    after = to_chip(passing + part[3], -1)
    summed = part[0] + before + after
    pieces = lax.all_to_all(
        summed, "rows", split_axis=0, concat_axis=0, axis_index_groups=classes, tiled=True
    )
    done = jnp.sum(pieces.reshape(chips // 4, -1, LB), axis=0)
    whole = lax.all_gather(done, "rows", axis=0, axis_index_groups=classes, tiled=True)
    right = to_chip(whole, -1)
    left = to_chip(whole, 1)
    far = to_chip(right, -1)
    mine = jnp.concatenate([whole, right, far, left])
    return mine, to_core(mine)


def body(own_rows, child_tile, col_map, parent, live_rows):
    group = lax.axis_index("front")
    place = lax.axis_index("rows")
    own, tile = own_rows[0], child_tile[0]
    local, width = own.shape
    tile_rows = tile.shape[0]
    live = lax.dynamic_index_in_dim(live_rows, group, keepdims=False)
    my_parent = lax.dynamic_index_in_dim(parent, group, keepdims=False)
    at = jnp.stack([group, my_parent]).astype(jnp.int32)
    arrived = lax.all_to_all(
        place_child(at, tile, col_map), "front", split_axis=0, concat_axis=0, tiled=True
    )
    where = jnp.stack(
        [live - place * local, place * tile_rows, place % 2, place // 2]
    ).astype(jnp.int32)
    keep, send = add_children(where, own_gram(where, own), arrived.reshape(-1, width))
    mine, other = sum_over_rows(keep, send)
    r_rows, panel = factor(
        where, mine, other, own, tile_rows, local * lax.axis_size("rows")
    )
    return (r_rows[None], panel[None])


def solution(mesh):
    placed = (P("front", "rows", None), P("front", "rows", None), P(), P(), P())
    return jax.shard_map(
        body,
        mesh=mesh,
        in_specs=placed,
        out_specs=(P("front", "rows", None), P("front", "rows", None)),
        check_vma=False,
    )
```

time: 236 us -> 199 us (0.84)
  Pallas kernels: 72.7 us -> 41.3 us
  blocking collectives: 17.1 us -> 40.8 us
  waiting for transfers between devices: 59.1 us -> 46.5 us
  starting transfers between devices: 67.2 us -> 60.5 us
  other arithmetic: 7.17 us -> 0.97 us
  local copies, waits for them, and re-layouts: 10.5 us -> 6.52 us
    pallas_call x3 -> x4, Pallas kernels: 72.7 us -> 41.3 us  [the longest x1 31.2 us: factor(): pl.pallas_call(functools.partial(factor_kernel, total_rows), out_shape=(j...]
    all_to_all x0 -> x1, blocking collectives: none -> 21.5 us  [sum_over_rows(): lax.all_to_all(summed, 'rows', split_axis=0, concat_axis=0, axis_index_gr...]
    all_to_all x2 -> x1, waiting for transfers between devices: 39.6 us -> 20.4 us  [body(): lax.all_to_all(place_child(at, tile, col_map), 'front', split_axis=0, con...]
    all_to_all x2 -> x1, starting transfers between devices: 17 us -> 7.72 us  [body(): lax.all_to_all(place_child(at, tile, col_map), 'front', split_axis=0, con...]
    ppermute x10 -> x8, waiting for transfers between devices: 19.6 us -> 26.1 us  [the longest x6 21.4 us: to_chip(): lax.ppermute(x, 'rows', [(i, (i + 2 * k) % devices) for i in range(device...]
    select_n x4 -> x0, other arithmetic: 3.15 us -> none  [the longest x1 1.66 us: body(): jnp.where((fronts == my_parent)[:, None, None], mapped[None], F32(0))]
    add x2 -> x3, other arithmetic: 3.15 us -> 0.16 us  [the longest x2 0.11 us: sum_over_rows(): keep[k * quarter:(k + 1) * quarter] + got[k * quarter:(k + 1) * quarter]]
    ppermute x10 -> x8, starting transfers between devices: 50.2 us -> 52.7 us  [the longest x6 34.9 us: to_chip(): lax.ppermute(x, 'rows', [(i, (i + 2 * k) % devices) for i in range(device...]
  transfers between devices with their start and end apart: 12 -> 9, of which waited for: 8 -> 9; matrix products, arithmetic and copies ran while one was open for 1% -> 0% of each run, Pallas kernels for 0% -> 1%
where the time goes in v2:
time: 199 us; the launch traced here: 198 us
  starting transfers between devices  60.5 us (30%)
  waiting for transfers between devices  46.5 us (23%)
  Pallas kernels  41.3 us (21%)
  blocking collectives  40.8 us (21%)
  local copies, waits for them, and re-layouts  6.52 us (3%)
    ppermute x6, starting transfers between devices, to_chip(): lax.ppermute(x, 'rows', [(i, (i + 2 * k) % devices) for i in range(device...  34.9 us
    pallas_call x1, Pallas kernels, factor(): pl.pallas_call(functools.partial(factor_kernel, total_rows), out_shape=(j...  31.2 us
    all_to_all x1, blocking collectives, sum_over_rows(): lax.all_to_all(summed, 'rows', split_axis=0, concat_axis=0, axis_index_gr...  21.5 us
    ppermute x6, waiting for transfers between devices, to_chip(): lax.ppermute(x, 'rows', [(i, (i + 2 * k) % devices) for i in range(device...  21.4 us
    all_to_all x1, waiting for transfers between devices, body(): lax.all_to_all(place_child(at, tile, col_map), 'front', split_axis=0, con...  20.4 us
    all_gather x1, blocking collectives, sum_over_rows(): lax.all_gather(done, 'rows', axis=0, axis_index_groups=classes, tiled=True)  19.3 us
    ppermute x2, starting transfers between devices, to_core(): lax.ppermute(x, 'rows', [(i, i ^ 1) for i in range(lax.axis_size('rows'))])  17.9 us
    all_to_all x1, starting transfers between devices, body(): lax.all_to_all(place_child(at, tile, col_map), 'front', split_axis=0, con...  7.72 us
  transfers between devices with their start and end apart: 9, of which 9 were waited for; matrix products, arithmetic and copies ran while one was open for 0% of the time, Pallas kernels for 1%

profile of v2, /device:TPU:1, one launch (start us, length us, event | category | flops | bytes accessed | tf_op | source)
XLA Modules:
  0.0 198.0 jit_solution(13147316788098318983)
XLA Ops:
  0.6 1.2 dynamic_slice.8
  1.9 0.7 pad_add_fusion.1.at_ref
  2.6 0.0 copy-start.3
  2.6 0.9 copy-done.3
  3.5 0.0 copy-start.4
  3.5 0.8 copy-done.4
  4.3 1.4 place_child.1
  5.8 0.0 copy-start.1
  5.8 1.3 copy-done.1
  7.1 0.0 copy-start.5
  7.1 0.0 copy-start.2
  7.1 7.7 %all-to-all-start = ((f32[16,32,1024]{2,1,0:T(8,128)}), f32[16,32,1024]{2,1,0:T(8,128)S(1)}, u32[]{:S(2)}, u32[]{:S(2)}) async-start(f32[16,32,1024]{2,1,0:T(8,128)} %copy-done.1), calls=%async_computation | async-start | bytes 4194304 | tf_op jit(solution)/shard_map/all_to_all | solution.py:403
  14.9 0.0 copy-done.5
  14.9 0.7 dynamic_slice.7
  16.2 0.1 pad_add_fusion.place_ref
  16.3 0.0 copy-done.2
  16.3 1.9 own_gram.1.mine_ref
  18.2 0.0 copy-start
  18.2 1.4 copy-done
  19.7 20.4 %all-to-all-done = f32[16,32,1024]{2,1,0:T(8,128)S(1)} async-done(((f32[16,32,1024]{2,1,0:T(8,128)}), f32[16,32,1024]{2,1,0:T(8,128)S(1)}, u32[]{:S(2)}, u32[]{:S(2)}) %all-to-all-start) | async-done | bytes 2097184 | tf_op jit(solution)/shard_map/all_to_all | solution.py:403
  40.0 6.7 %add_children.1 = (f32[2304,128]{1,0:T(8,128)S(1)}, f32[2304,128]{1,0:T(8,128)S(1)}) custom-call(s32[4]{0:T(128)S(1)} %pad_add_fusion.place_ref, f32[4608,128]{1,0:T(8,128)} %copy-done, f32[512,1024]{1,0:T(8,128)S(1)} %bitcast.12), custom_call_target="tpu_custom_call" | custom-call | tf_op jit(solution)/shard_map/add_children/pallas_call | solution.py:138
  46.7 7.6 %collective-permute-start = (f32[2304,128]{1,0:T(8,128)S(1)}, f32[2304,128]{1,0:T(8,128)S(1)}, u32[]{:S(2)}, u32[]{:S(2)}) collective-permute-start(f32[2304,128]{1,0:T(8,128)S(1)} %get-tuple-element.7), channel_id=1, source_target_pairs={{0,1},{1,0},{2,3},{3,2},{4,5},{5,4},{6,7},{7,6},{8,9},{9,8},{10,11... | collective-permute-start | bytes 3538952 | tf_op jit(solution)/shard_map/ppermute | solution.py:364
  54.3 2.5 %collective-permute-done = f32[2304,128]{1,0:T(8,128)S(1)} collective-permute-done((f32[2304,128]{1,0:T(8,128)S(1)}, f32[2304,128]{1,0:T(8,128)S(1)}, u32[]{:S(2)}, u32[]{:S(2)}) %collective-permute-start) | collective-permute-done | bytes 1179680 | tf_op jit(solution)/shard_map/ppermute | solution.py:364
  56.8 12.9 %collective-permute-start.2 = (f32[576,128]{1,0:T(8,128)S(1)}, f32[576,128]{1,0:T(8,128)S(1)}, u32[]{:S(2)}, u32[]{:S(2)}) collective-permute-start(f32[576,128]{1,0:T(8,128)S(1)} %slice_add_fusion.1), channel_id=1, source_target_pairs={{0,30},{1,31},{2,0},{3,1},{4,2},{5,3},{6,4},{7,5},{8,6},{9,7},{10,... | collective-permute-start | bytes 884744 | tf_op jit(solution)/shard_map/ppermute | solution.py:360
  69.7 6.0 %collective-permute-done.2 = f32[576,128]{1,0:T(8,128)S(1)} collective-permute-done((f32[576,128]{1,0:T(8,128)S(1)}, f32[576,128]{1,0:T(8,128)S(1)}, u32[]{:S(2)}, u32[]{:S(2)}) %collective-permute-start.2) | collective-permute-done | bytes 294944 | tf_op jit(solution)/shard_map/ppermute | solution.py:360
  75.7 0.1 slice_add_fusion.2
  75.8 1.9 collective-permute-start.1
  77.7 5.3 %collective-permute-start.3 = (f32[576,128]{1,0:T(8,128)S(1)}, f32[576,128]{1,0:T(8,128)S(1)}, u32[]{:S(2)}, u32[]{:S(2)}) collective-permute-start(f32[576,128]{1,0:T(8,128)S(1)} %get-tuple-element.11), channel_id=1, source_target_pairs={{0,30},{1,31},{2,0},{3,1},{4,2},{5,3},{6,4},{7,5},{8,6},{9,7},{10,... | collective-permute-start | bytes 884744 | tf_op jit(solution)/shard_map/ppermute | solution.py:360
  83.0 4.2 %collective-permute-done.1 = f32[576,128]{1,0:T(8,128)S(1)} collective-permute-done((f32[576,128]{1,0:T(8,128)S(1)}, f32[576,128]{1,0:T(8,128)S(1)}, u32[]{:S(2)}, u32[]{:S(2)}) %collective-permute-start.1) | collective-permute-done | bytes 294944 | tf_op jit(solution)/shard_map/ppermute | solution.py:360
  87.2 0.9 collective-permute-done.3
  88.1 0.1 fusion.2
  88.2 21.5 %all_to_all.14 = f32[4,144,128]{2,1,0:T(8,128)S(1)} all-to-all(f32[4,144,128]{2,1,0:T(8,128)S(1)} %bitcast.16), channel_id=1, replica_groups={{0,8,16,24},{2,10,18,26},{4,12,20,28},{6,14,22,30},{1,9,17,25},{3,11,19..., dimensions={0} | all-to-all | bytes 589824 | tf_op jit(solution)/shard_map/all_to_all | solution.py:382
  109.7 19.3 %all_gather.3 = f32[576,128]{1,0:T(8,128)S(1)} all-gather(f32[144,128]{1,0:T(8,128)S(1)} %reduce_sum.9), channel_id=1, replica_groups={{0,8,16,24},{2,10,18,26},{4,12,20,28},{6,14,22,30},{1,9,17,25},{3,11,19..., dimensions={0}, use_global_device_ids=true | all-gather | bytes 368640 | tf_op jit(solution)/shard_map/all_gather | solution.py:386
  129.0 7.7 %collective-permute-start.4 = (f32[576,128]{1,0:T(8,128)S(1)}, f32[576,128]{1,0:T(8,128)S(1)}, u32[]{:S(2)}, u32[]{:S(2)}) collective-permute-start(f32[576,128]{1,0:T(8,128)S(1)} %all_gather.3), channel_id=1, source_target_pairs={{0,30},{1,31},{2,0},{3,1},{4,2},{5,3},{6,4},{7,5},{8,6},{9,7},{10,... | collective-permute-start | bytes 884744 | tf_op jit(solution)/shard_map/ppermute | solution.py:360
  136.7 3.6 %collective-permute-done.4 = f32[576,128]{1,0:T(8,128)S(1)} collective-permute-done((f32[576,128]{1,0:T(8,128)S(1)}, f32[576,128]{1,0:T(8,128)S(1)}, u32[]{:S(2)}, u32[]{:S(2)}) %collective-permute-start.4) | collective-permute-done | bytes 294944 | tf_op jit(solution)/shard_map/ppermute | solution.py:360
  140.4 5.1 %collective-permute-start.5 = (f32[576,128]{1,0:T(8,128)S(1)}, f32[576,128]{1,0:T(8,128)S(1)}, u32[]{:S(2)}, u32[]{:S(2)}) collective-permute-start(f32[576,128]{1,0:T(8,128)S(1)} %collective-permute-done.4), channel_id=1, source_target_pairs={{0,30},{1,31},{2,0},{3,1},{4,2},{5,3},{6,4},{7,5},{8,6},{9,7},{10,... | collective-permute-start | bytes 884744 | tf_op jit(solution)/shard_map/ppermute | solution.py:360
  145.5 1.9 collective-permute-start.6
  147.5 2.9 %collective-permute-done.5 = f32[576,128]{1,0:T(8,128)S(1)} collective-permute-done((f32[576,128]{1,0:T(8,128)S(1)}, f32[576,128]{1,0:T(8,128)S(1)}, u32[]{:S(2)}, u32[]{:S(2)}) %collective-permute-start.5) | collective-permute-done | bytes 294944 | tf_op jit(solution)/shard_map/ppermute | solution.py:360
  150.5 3.7 %collective-permute-done.6 = f32[576,128]{1,0:T(8,128)S(1)} collective-permute-done((f32[576,128]{1,0:T(8,128)S(1)}, f32[576,128]{1,0:T(8,128)S(1)}, u32[]{:S(2)}, u32[]{:S(2)}) %collective-permute-start.6) | collective-permute-done | bytes 294944 | tf_op jit(solution)/shard_map/ppermute | solution.py:360
  154.2 10.3 %collective-permute-start.7 = (f32[2304,128]{1,0:T(8,128)S(1)}, f32[2304,128]{1,0:T(8,128)S(1)}, u32[]{:S(2)}, u32[]{:S(2)}) collective-permute-start(f32[2304,128]{1,0:T(8,128)S(1)} %constant_dynamic-update-slice_fusion.mine_ref), channel_id=1, source_target_pairs={{0,1},{1,0},{2,3},{3,2},{4,5},{5,4},{6,7},{7,6},{8,9},{9,8},{10,11... | collective-permute-start | bytes 3538952 | tf_op jit(solution)/shard_map/ppermute | solution.py:364
  164.5 2.3 %collective-permute-done.7.other_ref = f32[2304,128]{1,0:T(8,128)S(1)} collective-permute-done((f32[2304,128]{1,0:T(8,128)S(1)}, f32[2304,128]{1,0:T(8,128)S(1)}, u32[]{:S(2)}, u32[]{:S(2)}) %collective-permute-start.7) | collective-permute-done | bytes 1179680 | tf_op jit(solution)/shard_map/ppermute | solution.py:364
  166.8 31.2 %factor.1 = (f32[32,1024]{1,0:T(8,128)}, f32[256,1024]{1,0:T(8,128)}) custom-call(s32[4]{0:T(128)S(1)} %pad_add_fusion.place_ref, f32[2304,128]{1,0:T(8,128)S(1)} %constant_dynamic-update-slice_fusion.mine_ref, f32[2304,128]{1,0:T(8,128)S(1)} %collective-permute-done.7.other_ref, f32[256,1024]{1,0:T(8,128)S(1)} %bitcast.14), custom_call_target="tpu_custom_call" | custom-call | tf_op jit(solution)/shard_map/factor/pallas_call | solution.py:339
  (6 shorter events, 0.1 us)
Async XLA Ops:
  2.6 0.9 copy-start.3
  3.5 0.8 copy-start.4
  5.8 1.3 copy-start.1
  7.1 7.7 %copy-start.5 = (s32[16]{0:T(128)S(1)}, s32[16]{0:T(128)}, u32[]{:S(2)}) copy-start(s32[16]{0:T(128)} %param.9) | copy-start | bytes 196
  7.1 9.2 %copy-start.2 = (f32[1,256,1024]{2,1,0:T(8,128)S(1)}, f32[1,256,1024]{2,1,0:T(8,128)}, u32[]{:S(2)}) copy-start(f32[1,256,1024]{2,1,0:T(8,128)} %param.5) | copy-start | bytes 3145732
  7.1 32.9 %all-to-all-start = ((f32[16,32,1024]{2,1,0:T(8,128)}), f32[16,32,1024]{2,1,0:T(8,128)S(1)}, u32[]{:S(2)}, u32[]{:S(2)}) async-start(f32[16,32,1024]{2,1,0:T(8,128)} %copy-done.1), calls=%async_computation | async-start | bytes 4194304 | tf_op jit(solution)/shard_map/all_to_all | solution.py:403
  18.2 1.4 copy-start
  46.7 10.0 %collective-permute-start = (f32[2304,128]{1,0:T(8,128)S(1)}, f32[2304,128]{1,0:T(8,128)S(1)}, u32[]{:S(2)}, u32[]{:S(2)}) collective-permute-start(f32[2304,128]{1,0:T(8,128)S(1)} %get-tuple-element.7), channel_id=1, source_target_pairs={{0,1},{1,0},{2,3},{3,2},{4,5},{5,4},{6,7},{7,6},{8,9},{9,8},{10,11... | collective-permute-start | bytes 3538952 | tf_op jit(solution)/shard_map/ppermute | solution.py:364
  56.8 18.9 %collective-permute-start.2 = (f32[576,128]{1,0:T(8,128)S(1)}, f32[576,128]{1,0:T(8,128)S(1)}, u32[]{:S(2)}, u32[]{:S(2)}) collective-permute-start(f32[576,128]{1,0:T(8,128)S(1)} %slice_add_fusion.1), channel_id=1, source_target_pairs={{0,30},{1,31},{2,0},{3,1},{4,2},{5,3},{6,4},{7,5},{8,6},{9,7},{10,... | collective-permute-start | bytes 884744 | tf_op jit(solution)/shard_map/ppermute | solution.py:360
  75.8 11.4 %collective-permute-start.1 = (f32[576,128]{1,0:T(8,128)S(1)}, f32[576,128]{1,0:T(8,128)S(1)}, u32[]{:S(2)}, u32[]{:S(2)}) collective-permute-start(f32[576,128]{1,0:T(8,128)S(1)} %get-tuple-element.10), channel_id=1, source_target_pairs={{0,2},{1,3},{2,4},{3,5},{4,6},{5,7},{6,8},{7,9},{8,10},{9,11},{10,... | collective-permute-start | bytes 884744 | tf_op jit(solution)/shard_map/ppermute | solution.py:360
  77.7 10.4 %collective-permute-start.3 = (f32[576,128]{1,0:T(8,128)S(1)}, f32[576,128]{1,0:T(8,128)S(1)}, u32[]{:S(2)}, u32[]{:S(2)}) collective-permute-start(f32[576,128]{1,0:T(8,128)S(1)} %get-tuple-element.11), channel_id=1, source_target_pairs={{0,30},{1,31},{2,0},{3,1},{4,2},{5,3},{6,4},{7,5},{8,6},{9,7},{10,... | collective-permute-start | bytes 884744 | tf_op jit(solution)/shard_map/ppermute | solution.py:360
  129.0 11.4 %collective-permute-start.4 = (f32[576,128]{1,0:T(8,128)S(1)}, f32[576,128]{1,0:T(8,128)S(1)}, u32[]{:S(2)}, u32[]{:S(2)}) collective-permute-start(f32[576,128]{1,0:T(8,128)S(1)} %all_gather.3), channel_id=1, source_target_pairs={{0,30},{1,31},{2,0},{3,1},{4,2},{5,3},{6,4},{7,5},{8,6},{9,7},{10,... | collective-permute-start | bytes 884744 | tf_op jit(solution)/shard_map/ppermute | solution.py:360
  140.4 10.1 %collective-permute-start.5 = (f32[576,128]{1,0:T(8,128)S(1)}, f32[576,128]{1,0:T(8,128)S(1)}, u32[]{:S(2)}, u32[]{:S(2)}) collective-permute-start(f32[576,128]{1,0:T(8,128)S(1)} %collective-permute-done.4), channel_id=1, source_target_pairs={{0,30},{1,31},{2,0},{3,1},{4,2},{5,3},{6,4},{7,5},{8,6},{9,7},{10,... | collective-permute-start | bytes 884744 | tf_op jit(solution)/shard_map/ppermute | solution.py:360
  145.5 8.7 %collective-permute-start.6 = (f32[576,128]{1,0:T(8,128)S(1)}, f32[576,128]{1,0:T(8,128)S(1)}, u32[]{:S(2)}, u32[]{:S(2)}) collective-permute-start(f32[576,128]{1,0:T(8,128)S(1)} %all_gather.3), channel_id=1, source_target_pairs={{0,2},{1,3},{2,4},{3,5},{4,6},{5,7},{6,8},{7,9},{8,10},{9,11},{10,... | collective-permute-start | bytes 884744 | tf_op jit(solution)/shard_map/ppermute | solution.py:360
  154.2 12.6 %collective-permute-start.7 = (f32[2304,128]{1,0:T(8,128)S(1)}, f32[2304,128]{1,0:T(8,128)S(1)}, u32[]{:S(2)}, u32[]{:S(2)}) collective-permute-start(f32[2304,128]{1,0:T(8,128)S(1)} %constant_dynamic-update-slice_fusion.mine_ref), channel_id=1, source_target_pairs={{0,1},{1,0},{2,3},{3,2},{4,5},{5,4},{6,7},{7,6},{8,9},{9,8},{10,11... | collective-permute-start | bytes 3538952 | tf_op jit(solution)/shard_map/ppermute | solution.py:364

commit v3 on v2

--- a/solution.py
+++ b/solution.py
@@ -14,7 +14,7 @@
 NT = ((1,), (1,))
 VMEM = pl.BlockSpec(memory_space=pltpu.VMEM)
 SMEM = pl.BlockSpec(memory_space=pltpu.SMEM)
-PARAMS = pltpu.CompilerParams(vmem_limit_bytes=48 << 20)
+PARAMS = pltpu.CompilerParams(vmem_limit_bytes=32 << 20)
 
 
 def split(x):
@@ -36,40 +36,48 @@
     return [(i, j) for i in range(n) for j in range(i, n)]
 
 
-def place_kernel(at_ref, tile_ref, map_ref, out_ref):
+def place_kernel(parent_ref, tile_ref, map_ref, out_ref, moved_ref, sem):
     rows, width = tile_ref.shape
+    group = lax.axis_index("front")
     tile = tile_ref[...]
     first = tile.astype(jnp.bfloat16)
     rest = tile - first.astype(F32)
     second = rest.astype(jnp.bfloat16)
     third = (rest - second.astype(F32)).astype(jnp.bfloat16)
     parts = jnp.concatenate([first, second, third], axis=0)
-    columns = map_ref[pl.ds(at_ref[0], 1), :]
-    out_ref[...] = jnp.zeros(out_ref.shape, F32)
+    columns = map_ref[pl.ds(group, 1), :]
     for i in range(width // LB):
         target = lax.broadcasted_iota(jnp.int32, (LB, width), 0) + i * LB
         onehot = (target == columns).astype(F32).astype(jnp.bfloat16)
         moved = dot(parts, onehot, NT)
-        out_ref[at_ref[1], :, i * LB : (i + 1) * LB] = (
+        moved_ref[:, i * LB : (i + 1) * LB] = (
             moved[:rows] + moved[rows : 2 * rows] + moved[2 * rows :]
         )
-
-
-def place_child(at, tile, col_map):
+    copy = pltpu.make_async_copy(moved_ref, out_ref.at[parent_ref[group]], sem)
+    copy.start()
+    copy.wait()
+
+
+def place_child(parent, tile, col_map):
     return pl.pallas_call(
         place_kernel,
         out_shape=jax.ShapeDtypeStruct((col_map.shape[0],) + tile.shape, F32),
         in_specs=[SMEM, VMEM, VMEM],
-        out_specs=VMEM,
+        out_specs=pl.BlockSpec(memory_space=pl.ANY),
+        scratch_shapes=[pltpu.VMEM(tile.shape, F32), pltpu.SemaphoreType.DMA(())],
         compiler_params=PARAMS,
         name="place_child",
-    )(at, tile, col_map)
-
-
-def own_gram_kernel(place_ref, own_ref, out_ref, hi_ref, lo_ref):
-    width = own_ref.shape[1]
+    )(parent, tile, col_map)
+
+
+def live_here(live_ref, local):
+    return live_ref[lax.axis_index("front")] - lax.axis_index("rows") * local
+
+
+def own_gram_kernel(live_ref, own_ref, out_ref, hi_ref, lo_ref):
+    local, width = own_ref.shape
     rows = lax.broadcasted_iota(jnp.int32, own_ref.shape, 0)
-    own = jnp.where(rows < place_ref[0], own_ref[...], F32(0))
+    own = jnp.where(rows < live_here(live_ref, local), own_ref[...], F32(0))
     hi_ref[...], lo_ref[...] = split(own)
     at = 0
     for i in range(width // LB):
@@ -83,7 +91,7 @@
             at += LB
 
 
-def own_gram(place, own):
+def own_gram(live_rows, own):
     width = own.shape[1]
     return pl.pallas_call(
         own_gram_kernel,
@@ -93,57 +101,104 @@
         scratch_shapes=[pltpu.VMEM(own.shape, jnp.bfloat16)] * 2,
         compiler_params=PARAMS,
         name="own_gram",
-    )(place, own)
+    )(live_rows, own)
 
 
 def packed_rows(at, chip, half):
     quarter = half // 4
     piece = LB // 2
     side, first = divmod(at * LB, half)
+    turn = chip % 4
     found = []
     for s in range(2):
         q, inner = divmod(first + s * piece, quarter)
-        found.append(pl.multiple_of(((q + 4 - chip % 4) % 4) * quarter + inner, piece))
+        position = (q + 4 - turn) % 4 if side == 0 else (turn + 4 - q) % 4
+        found.append(pl.multiple_of(position * quarter + inner, piece))
     return side, found
 
 
-def gram_kernel(place_ref, mine_ref, arrived_ref, keep_ref, send_ref, hi_ref, lo_ref):
-    width = arrived_ref.shape[1]
+CHUNK = 128
+
+
+def gram_kernel(parent_ref, mine_ref, arrived_ref, keep_ref, send_ref, hi_ref, lo_ref, sum_ref):
+    children, rows, width = arrived_ref.shape
     half = keep_ref.shape[0]
-    core, chip = place_ref[2], place_ref[3]
-    hi_ref[...], lo_ref[...] = split(arrived_ref[...])
+    group = lax.axis_index("front")
+    core, chip = lax.axis_index("rows") % 2, lax.axis_index("rows") // 2
+
+    def pack(child, count):
+        mine = parent_ref[child] == group
+
+        @pl.when(mine)
+        def _():
+            at = pl.ds(pl.multiple_of(count * rows, rows), rows)
+            hi_ref[at, :], lo_ref[at, :] = split(arrived_ref[child])
+
+        return count + mine.astype(jnp.int32)
+
+    count = lax.fori_loop(0, children, pack, jnp.int32(0))
+    each = CHUNK // rows
+    chunks = (count + each - 1) // each
+    empty = jnp.zeros((rows, width), jnp.bfloat16)
+
+    def clear(child, carry):
+        at = pl.ds(pl.multiple_of(child * rows, rows), rows)
+        hi_ref[at, :] = empty
+        lo_ref[at, :] = empty
+        return carry
+
+    lax.fori_loop(count, jnp.maximum(chunks, 1) * each, clear, 0)
+
+    def add(chunk, base_ref):
+        at_rows = pl.ds(pl.multiple_of(chunk * CHUNK, CHUNK), CHUNK)
+        at = 0
+        for i in range(width // LB):
+            left = slice(i * LB, (i + 1) * LB)
+            right = slice(i * LB, width)
+            strip = dot3(
+                (hi_ref[at_rows, left], lo_ref[at_rows, left]),
+                (hi_ref[at_rows, right], lo_ref[at_rows, right]),
+                TN,
+            )
+            for j in range(strip.shape[1] // LB):
+                here = slice(at, at + LB)
+                sum_ref[here, :] = strip[:, j * LB : (j + 1) * LB] + base_ref[here, :]
+                at += LB
+
+    add(0, mine_ref)
+
+    def more(chunk, carry):
+        add(chunk, sum_ref)
+        return carry
+
+    lax.fori_loop(1, chunks, more, 0)
     piece = LB // 2
-    at = 0
-    for i in range(width // LB):
-        left = slice(i * LB, (i + 1) * LB)
-        right = slice(i * LB, width)
-        strip = dot3(
-            (hi_ref[:, left], lo_ref[:, left]), (hi_ref[:, right], lo_ref[:, right]), TN
-        )
-        for j in range(strip.shape[1] // LB):
-            block = strip[:, j * LB : (j + 1) * LB] + mine_ref[at * LB : (at + 1) * LB, :]
-            side, rows = packed_rows(at, chip, half)
+
+    def hand_out(refs):
+        for at in range(mine_ref.shape[0] // LB):
+            side, first = packed_rows(at, chip, half)
             for s in range(2):
-
-                def put(ref, s=s, rows=rows, block=block):
-                    ref[pl.ds(rows[s], piece), :] = block[s * piece : (s + 1) * piece]
-
-                pl.when(core == side)(lambda: put(keep_ref))
-                pl.when(core != side)(lambda: put(send_ref))
-            at += 1
-
-
-def add_children(place, mine, arrived):
+                refs[side][pl.ds(first[s], piece), :] = sum_ref[
+                    at * LB + s * piece : at * LB + (s + 1) * piece, :
+                ]
+
+    pl.when(core == 0)(lambda: hand_out((keep_ref, send_ref)))
+    pl.when(core == 1)(lambda: hand_out((send_ref, keep_ref)))
+
+
+def add_children(parent, mine, arrived):
+    children, rows, width = arrived.shape
     half = jax.ShapeDtypeStruct((mine.shape[0] // 2, LB), F32)
     return pl.pallas_call(
         gram_kernel,
         out_shape=(half, half),
         in_specs=[SMEM, VMEM, VMEM],
         out_specs=(VMEM, VMEM),
-        scratch_shapes=[pltpu.VMEM(arrived.shape, jnp.bfloat16)] * 2,
+        scratch_shapes=[pltpu.VMEM((children * rows, width), jnp.bfloat16)] * 2
+        + [pltpu.VMEM(mine.shape, F32)],
         compiler_params=PARAMS,
         name="add_children",
-    )(place, mine, arrived)
+    )(parent, mine, arrived)
 
 
 def row8(x, i):
@@ -161,15 +216,16 @@
 
 
 def factor_block(slabs):
-    count, panel = len(slabs), 4
+    count, panel, ahead = len(slabs), 4, 2
     sub = lax.broadcasted_iota(jnp.int32, (8, LB), 0)
     lane = lax.broadcasted_iota(jnp.int32, (8, LB), 1)
     inv = [jnp.where(lane == sub + 8 * v, F32(1), F32(0)) for v in range(count)]
     slabs = list(slabs)
     r_out, inv_out = [], []
+    here = [jnp.maximum(lane8(slabs[0], j), F32(-3e38)) for j in range(8)]
     for p in range(0, count, panel):
         end = p + panel
-        here = [jnp.maximum(lane8(slabs[p], 8 * p + j), F32(-3e38)) for j in range(8)]
+        reach = min(end + ahead, count)
         for b in range(p, end):
             a = [[row8(here[j], i) if i <= j else None for j in range(8)] for i in range(8)]
             r = [row8(slabs[b], i) for i in range(8)]
@@ -177,7 +233,7 @@
             rd = [None] * 8
             m = [[None] * 8 for _ in range(8)]
             vectors = [r, y]
-            if b + 1 < end:
+            if b + 1 < reach:
                 c = [lane8(slabs[b + 1], 8 * b + j) for j in range(8)]
                 here = [lane8(slabs[b + 1], 8 * (b + 1) + j) for j in range(8)]
                 vectors.append(c)
@@ -197,7 +253,7 @@
             rs = lax.rsqrt(pivots)
             r_out.append(jnp.where(lane >= sub + 8 * b, rows * rs, F32(0)))
             inv_out.append(invs * rs)
-            if b + 1 == end:
+            if b + 1 == reach:
                 continue
             u = [c[j] * rd[j] for j in range(8)]
             for j in range(8):
@@ -206,7 +262,7 @@
             for j in range(8):
                 for k in range(8):
                     here[j] = here[j] - u[k] * row8(c[k], j)
-            if b + 2 == end:
+            if b + 2 == reach:
                 continue
             z, w = [None] * 8, [None] * 8
             for k in reversed(range(8)):
@@ -215,11 +271,11 @@
                 for i in range(k + 1, 8):
                     z[k] = z[k] - m[k][i] * z[i]
                     w[k] = w[k] - m[k][i] * w[i]
-            for v in range(b + 2, end):
+            for v in range(b + 2, reach):
                 cv = [lane8(slabs[v], 8 * b + j) for j in range(8)]
                 slabs[v] = slabs[v] - total8([cv[j] * z[j] for j in range(8)])
                 inv[v] = inv[v] - total8([cv[j] * w[j] for j in range(8)])
-        if end < count:
+        if reach < count:
             both = jnp.concatenate(
                 [jnp.concatenate(x[p:end], axis=0) for x in (r_out, inv_out)], axis=1
             )
@@ -229,7 +285,7 @@
                 jnp.concatenate([hi, lo, hi], axis=0),
                 TN,
             )
-            for v in range(end, count):
+            for v in range(reach, count):
                 slabs[v] = slabs[v] - taken[8 * v : 8 * v + 8, :LB]
                 inv[v] = inv[v] - taken[8 * v : 8 * v + 8, LB:]
     return r_out, inv_out
@@ -248,13 +304,14 @@
 
 
 def factor_kernel(
-    total_rows, place_ref, mine_ref, other_ref, own_ref, r_ref, q_ref,
+    total_rows, live_ref, mine_ref, other_ref, own_ref, r_ref, q_ref,
     a_ref, inv_ref, strip_ref, q_now_ref,
 ):
     local, width = own_ref.shape
     n = width // LB
     half = mine_ref.shape[0]
-    core, chip = place_ref[2], place_ref[3]
+    place = lax.axis_index("rows")
+    core, chip = place % 2, place // 2
     diag = lax.broadcasted_iota(jnp.int32, (LB, LB), 0) == lax.broadcasted_iota(
         jnp.int32, (LB, LB), 1
     )
@@ -284,9 +341,10 @@
             block = block + shift
         a_ref[i * LB : (i + 1) * LB, j * LB : (j + 1) * LB] = block
     rows = lax.broadcasted_iota(jnp.int32, (local, LB), 0)
+    live = live_here(live_ref, local)
     for j in range(n):
         cols = slice(j * LB, (j + 1) * LB)
-        q_ref[:, cols] = jnp.where(rows < place_ref[0], own_ref[:, cols] * across[j], F32(0))
+        q_ref[:, cols] = jnp.where(rows < live, own_ref[:, cols] * across[j], F32(0))
     strip_ref[...] = jnp.zeros(strip_ref.shape, F32)
     q_now_ref[...] = jnp.zeros(q_now_ref.shape, F32)
 
@@ -327,14 +385,14 @@
 
     for first in (0, n // 2):
         lax.fori_loop(first, first + n // 2, functools.partial(step, first), 0)
-    start = pl.multiple_of(place_ref[1], 8)
+    start = pl.multiple_of(place * r_ref.shape[0], r_ref.shape[0])
     mine = a_ref[pl.ds(start, r_ref.shape[0]), :]
     row = start + lax.broadcasted_iota(jnp.int32, mine.shape, 0)
     column = lax.broadcasted_iota(jnp.int32, mine.shape, 1)
     r_ref[...] = jnp.where(column >= row, mine, F32(0))
 
 
-def factor(place, mine, other, own, out_rows, total_rows):
+def factor(live_rows, mine, other, own, out_rows, total_rows):
     local, width = own.shape
     return pl.pallas_call(
         functools.partial(factor_kernel, total_rows),
@@ -352,12 +410,13 @@
         ],
         compiler_params=PARAMS,
         name="factor",
-    )(place, mine, other, own)
+    )(live_rows, mine, other, own)
 
 
 def to_chip(x, k):
     devices = lax.axis_size("rows")
-    return lax.ppermute(x, "rows", [(i, (i + 2 * k) % devices) for i in range(devices)])
+    pairs = [(i, (i + (2 * k if i % 2 == 0 else -2 * k)) % devices) for i in range(devices)]
+    return lax.ppermute(x, "rows", pairs)
 
 
 def to_core(x):
@@ -392,25 +451,14 @@
 
 
 def body(own_rows, child_tile, col_map, parent, live_rows):
-    group = lax.axis_index("front")
-    place = lax.axis_index("rows")
     own, tile = own_rows[0], child_tile[0]
-    local, width = own.shape
-    tile_rows = tile.shape[0]
-    live = lax.dynamic_index_in_dim(live_rows, group, keepdims=False)
-    my_parent = lax.dynamic_index_in_dim(parent, group, keepdims=False)
-    at = jnp.stack([group, my_parent]).astype(jnp.int32)
     arrived = lax.all_to_all(
-        place_child(at, tile, col_map), "front", split_axis=0, concat_axis=0, tiled=True
+        place_child(parent, tile, col_map), "front", split_axis=0, concat_axis=0, tiled=True
     )
-    where = jnp.stack(
-        [live - place * local, place * tile_rows, place % 2, place // 2]
-    ).astype(jnp.int32)
-    keep, send = add_children(where, own_gram(where, own), arrived.reshape(-1, width))
+    keep, send = add_children(parent, own_gram(live_rows, own), arrived)
     mine, other = sum_over_rows(keep, send)
-    r_rows, panel = factor(
-        where, mine, other, own, tile_rows, local * lax.axis_size("rows")
-    )
+    total_rows = own.shape[0] * lax.axis_size("rows")
+    r_rows, panel = factor(live_rows, mine, other, own, tile.shape[0], total_rows)
     return (r_rows[None], panel[None])
 
 

time: 199 us -> 187 us (0.940)
  starting transfers between devices: 60.5 us -> 43 us
  waiting for transfers between devices: 46.5 us -> 58.9 us
  local copies, waits for them, and re-layouts: 6.52 us -> 2.49 us
  Pallas kernels: 41.3 us -> 37.5 us
  blocking collectives: 40.8 us -> 44 us
    ppermute x6, starting transfers between devices: 34.9 us -> 19.6 us  [to_chip(): return lax.ppermute(x, 'rows', pairs)]
    ppermute x6, waiting for transfers between devices: 21.4 us -> 31.3 us  [to_chip(): return lax.ppermute(x, 'rows', pairs)]
    all_to_all x1, blocking collectives: 21.5 us -> 26 us  [sum_over_rows(): lax.all_to_all(summed, 'rows', split_axis=0, concat_axis=0, axis_index_gr...]
    pallas_call x1, Pallas kernels: 6.69 us -> 3.19 us  [add_children(): pl.pallas_call(gram_kernel, out_shape=(half, half), in_specs=[SMEM, VMEM,...]
    all_to_all x1, waiting for transfers between devices: 20.4 us -> 22.8 us  [body(): lax.all_to_all(place_child(parent, tile, col_map), 'front', split_axis=0,...]
    ppermute x2, starting transfers between devices: 17.9 us -> 15.6 us  [to_core(): lax.ppermute(x, 'rows', [(i, i ^ 1) for i in range(lax.axis_size('rows'))])]
    unnamed x15, local copies, waits for them, and re-layouts: 4.59 us -> 2.47 us
where the time goes in v3:
time: 187 us
  waiting for transfers between devices  58.9 us (31%)
  blocking collectives  44 us (24%)
  starting transfers between devices  43 us (23%)
  Pallas kernels  37.5 us (20%)
  local copies, waits for them, and re-layouts  2.49 us (1%)
    ppermute x6, waiting for transfers between devices, to_chip(): return lax.ppermute(x, 'rows', pairs)  31.3 us
    pallas_call x1, Pallas kernels, factor(): pl.pallas_call(functools.partial(factor_kernel, total_rows), out_shape=(j...  30.4 us
    all_to_all x1, blocking collectives, sum_over_rows(): lax.all_to_all(summed, 'rows', split_axis=0, concat_axis=0, axis_index_gr...  26 us
    all_to_all x1, waiting for transfers between devices, body(): lax.all_to_all(place_child(parent, tile, col_map), 'front', split_axis=0,...  22.8 us
    ppermute x6, starting transfers between devices, to_chip(): return lax.ppermute(x, 'rows', pairs)  19.6 us
    all_gather x1, blocking collectives, sum_over_rows(): lax.all_gather(done, 'rows', axis=0, axis_index_groups=classes, tiled=True)  18 us
    ppermute x2, starting transfers between devices, to_core(): lax.ppermute(x, 'rows', [(i, i ^ 1) for i in range(lax.axis_size('rows'))])  15.6 us
    all_to_all x1, starting transfers between devices, body(): lax.all_to_all(place_child(parent, tile, col_map), 'front', split_axis=0,...  7.79 us
  transfers between devices with their start and end apart: 9, of which 9 were waited for; matrix products, arithmetic and copies ran while one was open for 0% of the time, Pallas kernels for 1%

profile of v3, /device:TPU:1, one launch (start us, length us, event | category | flops | bytes accessed | tf_op | source)
XLA Modules:
  0.0 186.9 jit_solution(4680869159319993693)
XLA Ops:
  0.6 0.0 copy-start.1
  0.6 0.9 copy-done.1
  1.5 0.0 copy-start.2
  1.5 0.8 copy-done.2
  2.4 0.0 copy-start.3
  2.4 0.7 copy-done.3
  3.0 2.0 %place_child.1 = f32[16,32,1024]{2,1,0:T(8,128)} custom-call(s32[16]{0:T(128)S(1)} %copy-done.3, f32[32,1024]{1,0:T(8,128)S(1)} %bitcast.7, s32[16,1024]{1,0:T(8,128)S(1)} %copy-done.2), custom_call_target="tpu_custom_call" | custom-call | tf_op jit(solution)/shard_map/place_child/pallas_call | solution.py:62
  5.0 0.0 copy-start
  5.1 0.0 copy-start.5
  5.1 7.8 %all-to-all-start = ((f32[16,32,1024]{2,1,0:T(8,128)}), f32[16,32,1024]{2,1,0:T(8,128)}, u32[]{:S(2)}, u32[]{:S(2)}) async-start(f32[16,32,1024]{2,1,0:T(8,128)} %place_child.1), calls=%async_computation | async-start | bytes 4194304 | tf_op jit(solution)/shard_map/all_to_all | solution.py:455
  12.9 0.0 copy-done
  12.9 0.0 copy-done.5
  12.9 0.0 copy-start.4
  12.9 1.9 %own_gram.1.mine_ref = f32[4608,128]{1,0:T(8,128)S(1)} custom-call(s32[16]{0:T(128)S(1)} %copy-done.5, f32[256,1024]{1,0:T(8,128)S(1)} %bitcast.5), custom_call_target="tpu_custom_call" | custom-call | tf_op jit(solution)/shard_map/own_gram/pallas_call | solution.py:96
  14.8 22.8 %all-to-all-done.arrived_ref = f32[16,32,1024]{2,1,0:T(8,128)} async-done(((f32[16,32,1024]{2,1,0:T(8,128)}), f32[16,32,1024]{2,1,0:T(8,128)}, u32[]{:S(2)}, u32[]{:S(2)}) %all-to-all-start) | async-done | bytes 2097184 | tf_op jit(solution)/shard_map/all_to_all | solution.py:455
  37.7 0.0 copy-done.4
  37.7 3.2 %add_children.1 = (f32[2304,128]{1,0:T(8,128)S(1)}, f32[2304,128]{1,0:T(8,128)S(1)}) custom-call(s32[16]{0:T(128)S(1)} %copy-done.4, f32[4608,128]{1,0:T(8,128)S(1)} %own_gram.1.mine_ref, f32[16,32,1024]{2,1,0:T(8,128)} %all-to-all-done.arrived_ref), custom_call_target="tpu_custom_call" | custom-call | tf_op jit(solution)/shard_map/add_children/pallas_call | solution.py:192
  40.9 8.3 %collective-permute-start = (f32[2304,128]{1,0:T(8,128)S(1)}, f32[2304,128]{1,0:T(8,128)S(1)}, u32[]{:S(2)}, u32[]{:S(2)}) collective-permute-start(f32[2304,128]{1,0:T(8,128)S(1)} %get-tuple-element.7), channel_id=1, source_target_pairs={{0,1},{1,0},{2,3},{3,2},{4,5},{5,4},{6,7},{7,6},{8,9},{9,8},{10,11... | collective-permute-start | bytes 3538952 | tf_op jit(solution)/shard_map/ppermute | solution.py:423
  49.2 2.5 %collective-permute-done = f32[2304,128]{1,0:T(8,128)S(1)} collective-permute-done((f32[2304,128]{1,0:T(8,128)S(1)}, f32[2304,128]{1,0:T(8,128)S(1)}, u32[]{:S(2)}, u32[]{:S(2)}) %collective-permute-start) | collective-permute-done | bytes 1179680 | tf_op jit(solution)/shard_map/ppermute | solution.py:423
  51.7 5.0 %collective-permute-start.2 = (f32[576,128]{1,0:T(8,128)S(1)}, f32[576,128]{1,0:T(8,128)S(1)}, u32[]{:S(2)}, u32[]{:S(2)}) collective-permute-start(f32[576,128]{1,0:T(8,128)S(1)} %slice_add_fusion.1), channel_id=1, source_target_pairs={{0,30},{1,3},{2,0},{3,5},{4,2},{5,7},{6,4},{7,9},{8,6},{9,11},{10,... | collective-permute-start | bytes 884744 | tf_op jit(solution)/shard_map/ppermute | solution.py:419
  56.7 11.7 %collective-permute-done.2 = f32[576,128]{1,0:T(8,128)S(1)} collective-permute-done((f32[576,128]{1,0:T(8,128)S(1)}, f32[576,128]{1,0:T(8,128)S(1)}, u32[]{:S(2)}, u32[]{:S(2)}) %collective-permute-start.2) | collective-permute-done | bytes 294944 | tf_op jit(solution)/shard_map/ppermute | solution.py:419
  68.4 0.1 slice_add_fusion.2
  68.5 3.7 %collective-permute-start.1 = (f32[576,128]{1,0:T(8,128)S(1)}, f32[576,128]{1,0:T(8,128)S(1)}, u32[]{:S(2)}, u32[]{:S(2)}) collective-permute-start(f32[576,128]{1,0:T(8,128)S(1)} %get-tuple-element.10), channel_id=1, source_target_pairs={{0,2},{1,31},{2,4},{3,1},{4,6},{5,3},{6,8},{7,5},{8,10},{9,7},{10,... | collective-permute-start | bytes 884744 | tf_op jit(solution)/shard_map/ppermute | solution.py:419
  72.1 1.9 %collective-permute-start.3 = (f32[576,128]{1,0:T(8,128)S(1)}, f32[576,128]{1,0:T(8,128)S(1)}, u32[]{:S(2)}, u32[]{:S(2)}) collective-permute-start(f32[576,128]{1,0:T(8,128)S(1)} %get-tuple-element.11), channel_id=1, source_target_pairs={{0,30},{1,3},{2,0},{3,5},{4,2},{5,7},{6,4},{7,9},{8,6},{9,11},{10,... | collective-permute-start | bytes 884744 | tf_op jit(solution)/shard_map/ppermute | solution.py:419
  74.0 2.2 %collective-permute-done.1 = f32[576,128]{1,0:T(8,128)S(1)} collective-permute-done((f32[576,128]{1,0:T(8,128)S(1)}, f32[576,128]{1,0:T(8,128)S(1)}, u32[]{:S(2)}, u32[]{:S(2)}) %collective-permute-start.1) | collective-permute-done | bytes 294944 | tf_op jit(solution)/shard_map/ppermute | solution.py:419
  76.2 5.8 %collective-permute-done.3 = f32[576,128]{1,0:T(8,128)S(1)} collective-permute-done((f32[576,128]{1,0:T(8,128)S(1)}, f32[576,128]{1,0:T(8,128)S(1)}, u32[]{:S(2)}, u32[]{:S(2)}) %collective-permute-start.3) | collective-permute-done | bytes 294944 | tf_op jit(solution)/shard_map/ppermute | solution.py:419
  82.0 0.1 fusion.2
  82.1 26.0 %all_to_all.14 = f32[4,144,128]{2,1,0:T(8,128)S(1)} all-to-all(f32[4,144,128]{2,1,0:T(8,128)S(1)} %bitcast.8), channel_id=1, replica_groups={{0,8,16,24},{2,10,18,26},{4,12,20,28},{6,14,22,30},{1,9,17,25},{3,11,19..., dimensions={0} | all-to-all | bytes 589824 | tf_op jit(solution)/shard_map/all_to_all | solution.py:441
  108.1 18.0 %all_gather.3 = f32[576,128]{1,0:T(8,128)S(1)} all-gather(f32[144,128]{1,0:T(8,128)S(1)} %reduce_sum.9), channel_id=1, replica_groups={{0,8,16,24},{2,10,18,26},{4,12,20,28},{6,14,22,30},{1,9,17,25},{3,11,19..., dimensions={0}, use_global_device_ids=true | all-gather | bytes 368640 | tf_op jit(solution)/shard_map/all_gather | solution.py:445
  126.1 2.5 %collective-permute-start.4 = (f32[576,128]{1,0:T(8,128)S(1)}, f32[576,128]{1,0:T(8,128)S(1)}, u32[]{:S(2)}, u32[]{:S(2)}) collective-permute-start(f32[576,128]{1,0:T(8,128)S(1)} %all_gather.3), channel_id=1, source_target_pairs={{0,30},{1,3},{2,0},{3,5},{4,2},{5,7},{6,4},{7,9},{8,6},{9,11},{10,... | collective-permute-start | bytes 884744 | tf_op jit(solution)/shard_map/ppermute | solution.py:419
  128.7 6.1 %collective-permute-done.4 = f32[576,128]{1,0:T(8,128)S(1)} collective-permute-done((f32[576,128]{1,0:T(8,128)S(1)}, f32[576,128]{1,0:T(8,128)S(1)}, u32[]{:S(2)}, u32[]{:S(2)}) %collective-permute-start.4) | collective-permute-done | bytes 294944 | tf_op jit(solution)/shard_map/ppermute | solution.py:419
  134.8 1.9 %collective-permute-start.5 = (f32[576,128]{1,0:T(8,128)S(1)}, f32[576,128]{1,0:T(8,128)S(1)}, u32[]{:S(2)}, u32[]{:S(2)}) collective-permute-start(f32[576,128]{1,0:T(8,128)S(1)} %collective-permute-done.4), channel_id=1, source_target_pairs={{0,30},{1,3},{2,0},{3,5},{4,2},{5,7},{6,4},{7,9},{8,6},{9,11},{10,... | collective-permute-start | bytes 884744 | tf_op jit(solution)/shard_map/ppermute | solution.py:419
  136.7 4.6 %collective-permute-start.6 = (f32[576,128]{1,0:T(8,128)S(1)}, f32[576,128]{1,0:T(8,128)S(1)}, u32[]{:S(2)}, u32[]{:S(2)}) collective-permute-start(f32[576,128]{1,0:T(8,128)S(1)} %all_gather.3), channel_id=1, source_target_pairs={{0,2},{1,31},{2,4},{3,1},{4,6},{5,3},{6,8},{7,5},{8,10},{9,7},{10,... | collective-permute-start | bytes 884744 | tf_op jit(solution)/shard_map/ppermute | solution.py:419
  141.3 2.1 %collective-permute-done.5 = f32[576,128]{1,0:T(8,128)S(1)} collective-permute-done((f32[576,128]{1,0:T(8,128)S(1)}, f32[576,128]{1,0:T(8,128)S(1)}, u32[]{:S(2)}, u32[]{:S(2)}) %collective-permute-start.5) | collective-permute-done | bytes 294944 | tf_op jit(solution)/shard_map/ppermute | solution.py:419
  143.5 3.4 %collective-permute-done.6 = f32[576,128]{1,0:T(8,128)S(1)} collective-permute-done((f32[576,128]{1,0:T(8,128)S(1)}, f32[576,128]{1,0:T(8,128)S(1)}, u32[]{:S(2)}, u32[]{:S(2)}) %collective-permute-start.6) | collective-permute-done | bytes 294944 | tf_op jit(solution)/shard_map/ppermute | solution.py:419
  146.9 7.3 %collective-permute-start.7 = (f32[2304,128]{1,0:T(8,128)S(1)}, f32[2304,128]{1,0:T(8,128)S(1)}, u32[]{:S(2)}, u32[]{:S(2)}) collective-permute-start(f32[2304,128]{1,0:T(8,128)S(1)} %constant_dynamic-update-slice_fusion.mine_ref), channel_id=1, source_target_pairs={{0,1},{1,0},{2,3},{3,2},{4,5},{5,4},{6,7},{7,6},{8,9},{9,8},{10,11... | collective-permute-start | bytes 3538952 | tf_op jit(solution)/shard_map/ppermute | solution.py:423
  154.2 2.3 %collective-permute-done.7.other_ref = f32[2304,128]{1,0:T(8,128)S(1)} collective-permute-done((f32[2304,128]{1,0:T(8,128)S(1)}, f32[2304,128]{1,0:T(8,128)S(1)}, u32[]{:S(2)}, u32[]{:S(2)}) %collective-permute-start.7) | collective-permute-done | bytes 1179680 | tf_op jit(solution)/shard_map/ppermute | solution.py:423
  156.5 30.4 %factor.1 = (f32[32,1024]{1,0:T(8,128)}, f32[256,1024]{1,0:T(8,128)}) custom-call(s32[16]{0:T(128)S(1)} %copy-done.5, f32[2304,128]{1,0:T(8,128)S(1)} %constant_dynamic-update-slice_fusion.mine_ref, f32[2304,128]{1,0:T(8,128)S(1)} %collective-permute-done.7.other_ref, f32[256,1024]{1,0:T(8,128)S(1)} %bitcast.6), custom_call_target="tpu_custom_call" | custom-call | tf_op jit(solution)/shard_map/factor/pallas_call | solution.py:397
  (6 shorter events, 0.1 us)
Async XLA Ops:
  0.6 0.9 copy-start.1
  1.5 0.8 copy-start.2
  2.4 0.7 copy-start.3
  5.0 7.8 %copy-start = (f32[1,256,1024]{2,1,0:T(8,128)S(1)}, f32[1,256,1024]{2,1,0:T(8,128)}, u32[]{:S(2)}) copy-start(f32[1,256,1024]{2,1,0:T(8,128)} %param.5) | copy-start | bytes 3145732
  5.1 7.8 %copy-start.5 = (s32[16]{0:T(128)S(1)}, s32[16]{0:T(128)}, u32[]{:S(2)}) copy-start(s32[16]{0:T(128)} %live_ref.3) | copy-start | bytes 196
  5.1 32.6 %all-to-all-start = ((f32[16,32,1024]{2,1,0:T(8,128)}), f32[16,32,1024]{2,1,0:T(8,128)}, u32[]{:S(2)}, u32[]{:S(2)}) async-start(f32[16,32,1024]{2,1,0:T(8,128)} %place_child.1), calls=%async_computation | async-start | bytes 4194304 | tf_op jit(solution)/shard_map/all_to_all | solution.py:455
  12.9 24.8 %copy-start.4 = (s32[16]{0:T(128)S(1)}, s32[16]{0:T(128)}, u32[]{:S(2)}) copy-start(s32[16]{0:T(128)} %parent_ref.3) | copy-start | bytes 196
  40.9 10.8 %collective-permute-start = (f32[2304,128]{1,0:T(8,128)S(1)}, f32[2304,128]{1,0:T(8,128)S(1)}, u32[]{:S(2)}, u32[]{:S(2)}) collective-permute-start(f32[2304,128]{1,0:T(8,128)S(1)} %get-tuple-element.7), channel_id=1, source_target_pairs={{0,1},{1,0},{2,3},{3,2},{4,5},{5,4},{6,7},{7,6},{8,9},{9,8},{10,11... | collective-permute-start | bytes 3538952 | tf_op jit(solution)/shard_map/ppermute | solution.py:423
  51.7 16.7 %collective-permute-start.2 = (f32[576,128]{1,0:T(8,128)S(1)}, f32[576,128]{1,0:T(8,128)S(1)}, u32[]{:S(2)}, u32[]{:S(2)}) collective-permute-start(f32[576,128]{1,0:T(8,128)S(1)} %slice_add_fusion.1), channel_id=1, source_target_pairs={{0,30},{1,3},{2,0},{3,5},{4,2},{5,7},{6,4},{7,9},{8,6},{9,11},{10,... | collective-permute-start | bytes 884744 | tf_op jit(solution)/shard_map/ppermute | solution.py:419
  68.5 7.8 %collective-permute-start.1 = (f32[576,128]{1,0:T(8,128)S(1)}, f32[576,128]{1,0:T(8,128)S(1)}, u32[]{:S(2)}, u32[]{:S(2)}) collective-permute-start(f32[576,128]{1,0:T(8,128)S(1)} %get-tuple-element.10), channel_id=1, source_target_pairs={{0,2},{1,31},{2,4},{3,1},{4,6},{5,3},{6,8},{7,5},{8,10},{9,7},{10,... | collective-permute-start | bytes 884744 | tf_op jit(solution)/shard_map/ppermute | solution.py:419
  72.1 9.9 %collective-permute-start.3 = (f32[576,128]{1,0:T(8,128)S(1)}, f32[576,128]{1,0:T(8,128)S(1)}, u32[]{:S(2)}, u32[]{:S(2)}) collective-permute-start(f32[576,128]{1,0:T(8,128)S(1)} %get-tuple-element.11), channel_id=1, source_target_pairs={{0,30},{1,3},{2,0},{3,5},{4,2},{5,7},{6,4},{7,9},{8,6},{9,11},{10,... | collective-permute-start | bytes 884744 | tf_op jit(solution)/shard_map/ppermute | solution.py:419
  126.1 8.7 %collective-permute-start.4 = (f32[576,128]{1,0:T(8,128)S(1)}, f32[576,128]{1,0:T(8,128)S(1)}, u32[]{:S(2)}, u32[]{:S(2)}) collective-permute-start(f32[576,128]{1,0:T(8,128)S(1)} %all_gather.3), channel_id=1, source_target_pairs={{0,30},{1,3},{2,0},{3,5},{4,2},{5,7},{6,4},{7,9},{8,6},{9,11},{10,... | collective-permute-start | bytes 884744 | tf_op jit(solution)/shard_map/ppermute | solution.py:419
  134.8 8.7 %collective-permute-start.5 = (f32[576,128]{1,0:T(8,128)S(1)}, f32[576,128]{1,0:T(8,128)S(1)}, u32[]{:S(2)}, u32[]{:S(2)}) collective-permute-start(f32[576,128]{1,0:T(8,128)S(1)} %collective-permute-done.4), channel_id=1, source_target_pairs={{0,30},{1,3},{2,0},{3,5},{4,2},{5,7},{6,4},{7,9},{8,6},{9,11},{10,... | collective-permute-start | bytes 884744 | tf_op jit(solution)/shard_map/ppermute | solution.py:419
  136.7 10.2 %collective-permute-start.6 = (f32[576,128]{1,0:T(8,128)S(1)}, f32[576,128]{1,0:T(8,128)S(1)}, u32[]{:S(2)}, u32[]{:S(2)}) collective-permute-start(f32[576,128]{1,0:T(8,128)S(1)} %all_gather.3), channel_id=1, source_target_pairs={{0,2},{1,31},{2,4},{3,1},{4,6},{5,3},{6,8},{7,5},{8,10},{9,7},{10,... | collective-permute-start | bytes 884744 | tf_op jit(solution)/shard_map/ppermute | solution.py:419
  146.9 9.5 %collective-permute-start.7 = (f32[2304,128]{1,0:T(8,128)S(1)}, f32[2304,128]{1,0:T(8,128)S(1)}, u32[]{:S(2)}, u32[]{:S(2)}) collective-permute-start(f32[2304,128]{1,0:T(8,128)S(1)} %constant_dynamic-update-slice_fusion.mine_ref), channel_id=1, source_target_pairs={{0,1},{1,0},{2,3},{3,2},{4,5},{5,4},{6,7},{7,6},{8,9},{9,8},{10,11... | collective-permute-start | bytes 3538952 | tf_op jit(solution)/shard_map/ppermute | solution.py:423

commit v4 on v3

--- a/solution.py
+++ b/solution.py
@@ -14,6 +14,7 @@
 NT = ((1,), (1,))
 VMEM = pl.BlockSpec(memory_space=pltpu.VMEM)
 SMEM = pl.BlockSpec(memory_space=pltpu.SMEM)
+ANY = pl.BlockSpec(memory_space=pl.ANY)
 PARAMS = pltpu.CompilerParams(vmem_limit_bytes=32 << 20)
 
 
@@ -36,9 +37,17 @@
     return [(i, j) for i in range(n) for j in range(i, n)]
 
 
-def place_kernel(parent_ref, tile_ref, map_ref, out_ref, moved_ref, sem):
+def place_kernel(parent_ref, tile_hbm, map_hbm, out_ref, tile_ref, map_ref, moved_ref, sems):
     rows, width = tile_ref.shape
     group = lax.axis_index("front")
+    fetches = [
+        pltpu.make_async_copy(tile_hbm, tile_ref, sems.at[0]),
+        pltpu.make_async_copy(map_hbm, map_ref, sems.at[1]),
+    ]
+    for fetch in fetches:
+        fetch.start()
+    for fetch in fetches:
+        fetch.wait()
     tile = tile_ref[...]
     first = tile.astype(jnp.bfloat16)
     rest = tile - first.astype(F32)
@@ -53,7 +62,7 @@
         moved_ref[:, i * LB : (i + 1) * LB] = (
             moved[:rows] + moved[rows : 2 * rows] + moved[2 * rows :]
         )
-    copy = pltpu.make_async_copy(moved_ref, out_ref.at[parent_ref[group]], sem)
+    copy = pltpu.make_async_copy(moved_ref, out_ref.at[parent_ref[group]], sems.at[2])
     copy.start()
     copy.wait()
 
@@ -62,9 +71,14 @@
     return pl.pallas_call(
         place_kernel,
         out_shape=jax.ShapeDtypeStruct((col_map.shape[0],) + tile.shape, F32),
-        in_specs=[SMEM, VMEM, VMEM],
-        out_specs=pl.BlockSpec(memory_space=pl.ANY),
-        scratch_shapes=[pltpu.VMEM(tile.shape, F32), pltpu.SemaphoreType.DMA(())],
+        in_specs=[SMEM, ANY, ANY],
+        out_specs=ANY,
+        scratch_shapes=[
+            pltpu.VMEM(tile.shape, F32),
+            pltpu.VMEM(col_map.shape, jnp.int32),
+            pltpu.VMEM(tile.shape, F32),
+            pltpu.SemaphoreType.DMA((3,)),
+        ],
         compiler_params=PARAMS,
         name="place_child",
     )(parent, tile, col_map)
@@ -219,7 +233,6 @@
     count, panel, ahead = len(slabs), 4, 2
     sub = lax.broadcasted_iota(jnp.int32, (8, LB), 0)
     lane = lax.broadcasted_iota(jnp.int32, (8, LB), 1)
-    inv = [jnp.where(lane == sub + 8 * v, F32(1), F32(0)) for v in range(count)]
     slabs = list(slabs)
     r_out, inv_out = [], []
     here = [jnp.maximum(lane8(slabs[0], j), F32(-3e38)) for j in range(8)]
@@ -228,11 +241,12 @@
         reach = min(end + ahead, count)
         for b in range(p, end):
             a = [[row8(here[j], i) if i <= j else None for j in range(8)] for i in range(8)]
-            r = [row8(slabs[b], i) for i in range(8)]
-            y = [row8(inv[b], i) for i in range(8)]
+            row = sub + 8 * b
+            joined = slabs[b] + jnp.where(lane == row, F32(1), F32(0))
+            r = [row8(joined, i) for i in range(8)]
             rd = [None] * 8
             m = [[None] * 8 for _ in range(8)]
-            vectors = [r, y]
+            vectors = [r]
             if b + 1 < reach:
                 c = [lane8(slabs[b + 1], 8 * b + j) for j in range(8)]
                 here = [lane8(slabs[b + 1], 8 * (b + 1) + j) for j in range(8)]
@@ -245,49 +259,43 @@
                         a[j][i] = a[j][i] - m[k][j] * a[k][i]
                     for vector in vectors:
                         vector[j] = vector[j] - m[k][j] * vector[k]
-            pivots, rows, invs = a[0][0], r[0], y[0]
+            pivots, rows = a[0][0], r[0]
             for k in range(1, 8):
                 pivots = jnp.where(sub == k, a[k][k], pivots)
                 rows = jnp.where(sub == k, r[k], rows)
-                invs = jnp.where(sub == k, y[k], invs)
             rs = lax.rsqrt(pivots)
-            r_out.append(jnp.where(lane >= sub + 8 * b, rows * rs, F32(0)))
-            inv_out.append(invs * rs)
+            rows = rows * rs
+            r_out.append(
+                jnp.where(lane > row, rows, jnp.where(lane == row, pivots * rs, F32(0)))
+            )
+            inv_out.append(jnp.where(lane < row, rows, jnp.where(lane == row, rs, F32(0))))
             if b + 1 == reach:
                 continue
             u = [c[j] * rd[j] for j in range(8)]
             for j in range(8):
                 slabs[b + 1] = slabs[b + 1] - u[j] * r[j]
-                inv[b + 1] = inv[b + 1] - u[j] * y[j]
             for j in range(8):
                 for k in range(8):
                     here[j] = here[j] - u[k] * row8(c[k], j)
             if b + 2 == reach:
                 continue
-            z, w = [None] * 8, [None] * 8
+            z = [None] * 8
             for k in reversed(range(8)):
                 z[k] = r[k] * rd[k]
-                w[k] = y[k] * rd[k]
                 for i in range(k + 1, 8):
                     z[k] = z[k] - m[k][i] * z[i]
-                    w[k] = w[k] - m[k][i] * w[i]
             for v in range(b + 2, reach):
                 cv = [lane8(slabs[v], 8 * b + j) for j in range(8)]
                 slabs[v] = slabs[v] - total8([cv[j] * z[j] for j in range(8)])
-                inv[v] = inv[v] - total8([cv[j] * w[j] for j in range(8)])
         if reach < count:
-            both = jnp.concatenate(
-                [jnp.concatenate(x[p:end], axis=0) for x in (r_out, inv_out)], axis=1
-            )
-            hi, lo = split(both)
+            both = [jnp.where(lane >= 8 * end, r_out[v], inv_out[v]) for v in range(p, end)]
+            hi, lo = split(jnp.concatenate(both, axis=0))
             taken = dot(
-                jnp.concatenate([hi[:, :LB], hi[:, :LB], lo[:, :LB]], axis=0),
-                jnp.concatenate([hi, lo, hi], axis=0),
-                TN,
-            )
+                jnp.concatenate([hi, hi, lo], axis=0), jnp.concatenate([hi, lo, hi], axis=0), TN
+            )
+            dead = (lane >= 8 * p) & (lane < 8 * end)
             for v in range(reach, count):
-                slabs[v] = slabs[v] - taken[8 * v : 8 * v + 8, :LB]
-                inv[v] = inv[v] - taken[8 * v : 8 * v + 8, LB:]
+                slabs[v] = jnp.where(dead, F32(0), slabs[v]) - taken[8 * v : 8 * v + 8, :]
     return r_out, inv_out
 
 
@@ -334,24 +342,29 @@
             lax.rsqrt(jnp.sum(only, axis=0, keepdims=True) / total_rows + F32(1e-6))
         )
         down.append(lax.rsqrt(jnp.sum(only, axis=1, keepdims=True) / total_rows + F32(1e-6)))
-    shift = jnp.where(diag, F32(0.25 * total_rows), F32(0))
-    for at, (i, j) in enumerate(blocks):
+    root = 2.0 ** ((total_rows.bit_length() - 1) // 2)
+    down = [x * F32(1 / root**2) for x in down]
+    shift = jnp.where(diag, F32(0.25 * total_rows / root**2), F32(0))
+
+    def scaled(at):
+        i, j = blocks[at]
         block = fetch(at) * down[i] * across[j]
-        if i == j:
-            block = block + shift
-        a_ref[i * LB : (i + 1) * LB, j * LB : (j + 1) * LB] = block
-    rows = lax.broadcasted_iota(jnp.int32, (local, LB), 0)
-    live = live_here(live_ref, local)
-    for j in range(n):
-        cols = slice(j * LB, (j + 1) * LB)
-        q_ref[:, cols] = jnp.where(rows < live, own_ref[:, cols] * across[j], F32(0))
-    strip_ref[...] = jnp.zeros(strip_ref.shape, F32)
-    q_now_ref[...] = jnp.zeros(q_now_ref.shape, F32)
-
-    def step(first, k, carry):
-        o = pl.multiple_of(k * LB, LB)
+        return block + shift if i == j else block
+
+    def unpack():
+        for at, (i, j) in enumerate(blocks):
+            if at > 0:
+                a_ref[i * LB : (i + 1) * LB, j * LB : (j + 1) * LB] = scaled(at)
+        rows = lax.broadcasted_iota(jnp.int32, (local, LB), 0)
+        live = live_here(live_ref, local)
+        for j in range(n):
+            cols = slice(j * LB, (j + 1) * LB)
+            q_ref[:, cols] = jnp.where(
+                rows < live, own_ref[:, cols] * (across[j] * F32(1 / root)), F32(0)
+            )
+
+    def take_strip(first):
         left = first * LB
-        slabs = [a_ref[pl.ds(o + 8 * v, 8), pl.ds(o, LB)] for v in range(LB // 8)]
         old = split(strip_ref[...])
         old_tall, old_wide = tall(old, 0), wide(old, 0)
         for i in range(first, n):
@@ -362,6 +375,18 @@
         q_ref[:, left:] = q_ref[:, left:] - dot(
             tall(split(q_now_ref[...]), 1), old_wide[:, left:], NN
         )
+
+    def step(first, k, carry):
+        o = pl.multiple_of(k * LB, LB)
+        if first is None:
+            left = 0
+            block = scaled(0)
+            slabs = [block[8 * v : 8 * v + 8, :] for v in range(LB // 8)]
+            unpack()
+        else:
+            left = first * LB
+            slabs = [a_ref[pl.ds(o + 8 * v, 8), pl.ds(o, LB)] for v in range(LB // 8)]
+            take_strip(first)
         r_rows, inv_rows = factor_block(slabs)
         for v in range(LB // 8):
             inv_ref[8 * v : 8 * v + 8, :] = inv_rows[v]
@@ -383,13 +408,14 @@
         q_ref[:, pl.ds(o, LB)] = q_now
         return carry
 
-    for first in (0, n // 2):
-        lax.fori_loop(first, first + n // 2, functools.partial(step, first), 0)
+    step(None, jnp.int32(0), 0)
+    lax.fori_loop(1, n // 2, functools.partial(step, 0), 0)
+    lax.fori_loop(n // 2, n, functools.partial(step, n // 2), 0)
     start = pl.multiple_of(place * r_ref.shape[0], r_ref.shape[0])
     mine = a_ref[pl.ds(start, r_ref.shape[0]), :]
     row = start + lax.broadcasted_iota(jnp.int32, mine.shape, 0)
     column = lax.broadcasted_iota(jnp.int32, mine.shape, 1)
-    r_ref[...] = jnp.where(column >= row, mine, F32(0))
+    r_ref[...] = jnp.where(column >= row, mine * F32(root), F32(0))
 
 
 def factor(live_rows, mine, other, own, out_rows, total_rows):
@@ -434,10 +460,8 @@
         keep[k * quarter : (k + 1) * quarter] + got[k * quarter : (k + 1) * quarter]
         for k in range(4)
     ]
-    passing = to_chip(part[2], -1)
-    before = to_chip(part[1], 1)
-    after = to_chip(passing + part[3], -1)
-    summed = part[0] + before + after
+    far = to_chip(part[2], -2)
+    summed = part[0] + to_chip(part[1], 1) + to_chip(part[3], -1) + far
     pieces = lax.all_to_all(
         summed, "rows", split_axis=0, concat_axis=0, axis_index_groups=classes, tiled=True
     )

time: 187 us -> 186 us (level)
  starting transfers between devices: 43 us -> 55.6 us
  waiting for transfers between devices: 58.9 us -> 46.7 us
    ppermute x6, waiting for transfers between devices: 31.3 us -> 19.2 us  [to_chip(): return lax.ppermute(x, 'rows', pairs)]
    ppermute x6, starting transfers between devices: 19.6 us -> 27.2 us  [to_chip(): return lax.ppermute(x, 'rows', pairs)]
    ppermute x2, starting transfers between devices: 15.6 us -> 20.7 us  [to_core(): lax.ppermute(x, 'rows', [(i, i ^ 1) for i in range(lax.axis_size('rows'))])]
  transfers between devices with their start and end apart: 9 -> 9, of which waited for: 9 -> 8; matrix products, arithmetic and copies ran while one was open for 0% -> 0% of each run, Pallas kernels for 1% -> 1%
where the time goes in v4:
time: 186 us; the launch traced here: 185 us
  starting transfers between devices  55.6 us (30%)
  waiting for transfers between devices  46.7 us (25%)
  blocking collectives  43.1 us (23%)
  Pallas kernels  36.4 us (20%)
  local copies, waits for them, and re-layouts  2.49 us (1%)
    pallas_call x1, Pallas kernels, factor(): pl.pallas_call(functools.partial(factor_kernel, total_rows), out_shape=(j...  29 us
    ppermute x6, starting transfers between devices, to_chip(): return lax.ppermute(x, 'rows', pairs)  27.2 us
    all_to_all x1, blocking collectives, sum_over_rows(): lax.all_to_all(summed, 'rows', split_axis=0, concat_axis=0, axis_index_gr...  25.6 us
    all_to_all x1, waiting for transfers between devices, body(): lax.all_to_all(place_child(parent, tile, col_map), 'front', split_axis=0,...  22.9 us
    ppermute x2, starting transfers between devices, to_core(): lax.ppermute(x, 'rows', [(i, i ^ 1) for i in range(lax.axis_size('rows'))])  20.7 us
    ppermute x6, waiting for transfers between devices, to_chip(): return lax.ppermute(x, 'rows', pairs)  19.2 us
    all_gather x1, blocking collectives, sum_over_rows(): lax.all_gather(done, 'rows', axis=0, axis_index_groups=classes, tiled=True)  17.5 us
    all_to_all x1, starting transfers between devices, body(): lax.all_to_all(place_child(parent, tile, col_map), 'front', split_axis=0,...  7.76 us
  transfers between devices with their start and end apart: 9, of which 8 were waited for; matrix products, arithmetic and copies ran while one was open for 0% of the time, Pallas kernels for 1%

profile of v4, /device:TPU:1, one launch (start us, length us, event | category | flops | bytes accessed | tf_op | source)
XLA Modules:
  0.0 185.4 jit_solution(15502995894971366261)
XLA Ops:
  0.6 0.0 copy-start.1
  0.6 0.9 copy-done.1
  1.5 0.0 copy-start.2
  1.5 0.8 copy-done.2
  2.4 0.0 copy-start.3
  2.4 0.7 copy-done.3
  3.0 2.3 %place_child.1 = f32[16,32,1024]{2,1,0:T(8,128)} custom-call(s32[16]{0:T(128)S(1)} %copy-done.3, f32[32,1024]{1,0:T(8,128)S(1)} %bitcast.7, s32[16,1024]{1,0:T(8,128)S(1)} %copy-done.2), custom_call_target="tpu_custom_call" | custom-call | tf_op jit(solution)/shard_map/place_child/pallas_call | solution.py:71
  5.3 0.0 copy-start
  5.3 0.0 copy-start.5
  5.4 7.8 %all-to-all-start = ((f32[16,32,1024]{2,1,0:T(8,128)}), f32[16,32,1024]{2,1,0:T(8,128)}, u32[]{:S(2)}, u32[]{:S(2)}) async-start(f32[16,32,1024]{2,1,0:T(8,128)} %place_child.1), calls=%async_computation | async-start | bytes 4194304 | tf_op jit(solution)/shard_map/all_to_all | solution.py:479
  13.1 0.0 copy-done
  13.1 0.0 copy-done.5
  13.2 0.0 copy-start.4
  13.2 1.9 %own_gram.1.mine_ref = f32[4608,128]{1,0:T(8,128)S(1)} custom-call(s32[16]{0:T(128)S(1)} %copy-done.5, f32[256,1024]{1,0:T(8,128)S(1)} %bitcast.5), custom_call_target="tpu_custom_call" | custom-call | tf_op jit(solution)/shard_map/own_gram/pallas_call | solution.py:110
  15.1 22.9 %all-to-all-done.arrived_ref = f32[16,32,1024]{2,1,0:T(8,128)} async-done(((f32[16,32,1024]{2,1,0:T(8,128)}), f32[16,32,1024]{2,1,0:T(8,128)}, u32[]{:S(2)}, u32[]{:S(2)}) %all-to-all-start) | async-done | bytes 2097184 | tf_op jit(solution)/shard_map/all_to_all | solution.py:479
  37.9 0.0 copy-done.4
  37.9 3.2 %add_children.1 = (f32[2304,128]{1,0:T(8,128)S(1)}, f32[2304,128]{1,0:T(8,128)S(1)}) custom-call(s32[16]{0:T(128)S(1)} %copy-done.4, f32[4608,128]{1,0:T(8,128)S(1)} %own_gram.1.mine_ref, f32[16,32,1024]{2,1,0:T(8,128)} %all-to-all-done.arrived_ref), custom_call_target="tpu_custom_call" | custom-call | tf_op jit(solution)/shard_map/add_children/pallas_call | solution.py:206
  41.1 8.4 %collective-permute-start = (f32[2304,128]{1,0:T(8,128)S(1)}, f32[2304,128]{1,0:T(8,128)S(1)}, u32[]{:S(2)}, u32[]{:S(2)}) collective-permute-start(f32[2304,128]{1,0:T(8,128)S(1)} %get-tuple-element.7), channel_id=1, source_target_pairs={{0,1},{1,0},{2,3},{3,2},{4,5},{5,4},{6,7},{7,6},{8,9},{9,8},{10,11... | collective-permute-start | bytes 3538952 | tf_op jit(solution)/shard_map/ppermute | solution.py:449
  49.5 2.5 %collective-permute-done = f32[2304,128]{1,0:T(8,128)S(1)} collective-permute-done((f32[2304,128]{1,0:T(8,128)S(1)}, f32[2304,128]{1,0:T(8,128)S(1)}, u32[]{:S(2)}, u32[]{:S(2)}) %collective-permute-start) | collective-permute-done | bytes 1179680 | tf_op jit(solution)/shard_map/ppermute | solution.py:449
  52.0 0.1 slice_add_fusion.2
  52.1 12.5 %collective-permute-start.1 = (f32[576,128]{1,0:T(8,128)S(1)}, f32[576,128]{1,0:T(8,128)S(1)}, u32[]{:S(2)}, u32[]{:S(2)}) collective-permute-start(f32[576,128]{1,0:T(8,128)S(1)} %get-tuple-element.10), channel_id=1, source_target_pairs={{0,2},{1,31},{2,4},{3,1},{4,6},{5,3},{6,8},{7,5},{8,10},{9,7},{10,... | collective-permute-start | bytes 884744 | tf_op jit(solution)/shard_map/ppermute | solution.py:445
  64.6 1.9 %collective-permute-start.3 = (f32[576,128]{1,0:T(8,128)S(1)}, f32[576,128]{1,0:T(8,128)S(1)}, u32[]{:S(2)}, u32[]{:S(2)}) collective-permute-start(f32[576,128]{1,0:T(8,128)S(1)} %get-tuple-element.11), channel_id=1, source_target_pairs={{0,28},{1,5},{2,30},{3,7},{4,0},{5,9},{6,2},{7,11},{8,4},{9,13},{1... | collective-permute-start | bytes 884744 | tf_op jit(solution)/shard_map/ppermute | solution.py:445
  66.5 1.9 %collective-permute-start.2 = (f32[576,128]{1,0:T(8,128)S(1)}, f32[576,128]{1,0:T(8,128)S(1)}, u32[]{:S(2)}, u32[]{:S(2)}) collective-permute-start(f32[576,128]{1,0:T(8,128)S(1)} %get-tuple-element.12), channel_id=1, source_target_pairs={{0,30},{1,3},{2,0},{3,5},{4,2},{5,7},{6,4},{7,9},{8,6},{9,11},{10,... | collective-permute-start | bytes 884744 | tf_op jit(solution)/shard_map/ppermute | solution.py:445
  68.5 0.0 collective-permute-done.1
  68.5 7.0 %collective-permute-done.3 = f32[576,128]{1,0:T(8,128)S(1)} collective-permute-done((f32[576,128]{1,0:T(8,128)S(1)}, f32[576,128]{1,0:T(8,128)S(1)}, u32[]{:S(2)}, u32[]{:S(2)}) %collective-permute-start.3) | collective-permute-done | bytes 294944 | tf_op jit(solution)/shard_map/ppermute | solution.py:445
  75.4 3.3 %collective-permute-done.2 = f32[576,128]{1,0:T(8,128)S(1)} collective-permute-done((f32[576,128]{1,0:T(8,128)S(1)}, f32[576,128]{1,0:T(8,128)S(1)}, u32[]{:S(2)}, u32[]{:S(2)}) %collective-permute-start.2) | collective-permute-done | bytes 294944 | tf_op jit(solution)/shard_map/ppermute | solution.py:445
  78.7 0.1 fusion.2
  78.8 25.6 %all_to_all.14 = f32[4,144,128]{2,1,0:T(8,128)S(1)} all-to-all(f32[4,144,128]{2,1,0:T(8,128)S(1)} %bitcast.8), channel_id=1, replica_groups={{0,8,16,24},{2,10,18,26},{4,12,20,28},{6,14,22,30},{1,9,17,25},{3,11,19..., dimensions={0} | all-to-all | bytes 589824 | tf_op jit(solution)/shard_map/all_to_all | solution.py:465
  104.4 17.5 %all_gather.3 = f32[576,128]{1,0:T(8,128)S(1)} all-gather(f32[144,128]{1,0:T(8,128)S(1)} %reduce_sum.9), channel_id=1, replica_groups={{0,8,16,24},{2,10,18,26},{4,12,20,28},{6,14,22,30},{1,9,17,25},{3,11,19..., dimensions={0}, use_global_device_ids=true | all-gather | bytes 368640 | tf_op jit(solution)/shard_map/all_gather | solution.py:469
  121.9 4.3 %collective-permute-start.4 = (f32[576,128]{1,0:T(8,128)S(1)}, f32[576,128]{1,0:T(8,128)S(1)}, u32[]{:S(2)}, u32[]{:S(2)}) collective-permute-start(f32[576,128]{1,0:T(8,128)S(1)} %all_gather.3), channel_id=1, source_target_pairs={{0,30},{1,3},{2,0},{3,5},{4,2},{5,7},{6,4},{7,9},{8,6},{9,11},{10,... | collective-permute-start | bytes 884744 | tf_op jit(solution)/shard_map/ppermute | solution.py:445
  126.2 5.0 %collective-permute-done.4 = f32[576,128]{1,0:T(8,128)S(1)} collective-permute-done((f32[576,128]{1,0:T(8,128)S(1)}, f32[576,128]{1,0:T(8,128)S(1)}, u32[]{:S(2)}, u32[]{:S(2)}) %collective-permute-start.4) | collective-permute-done | bytes 294944 | tf_op jit(solution)/shard_map/ppermute | solution.py:445
  131.2 3.1 %collective-permute-start.5 = (f32[576,128]{1,0:T(8,128)S(1)}, f32[576,128]{1,0:T(8,128)S(1)}, u32[]{:S(2)}, u32[]{:S(2)}) collective-permute-start(f32[576,128]{1,0:T(8,128)S(1)} %collective-permute-done.4), channel_id=1, source_target_pairs={{0,30},{1,3},{2,0},{3,5},{4,2},{5,7},{6,4},{7,9},{8,6},{9,11},{10,... | collective-permute-start | bytes 884744 | tf_op jit(solution)/shard_map/ppermute | solution.py:445
  134.3 3.4 %collective-permute-start.6 = (f32[576,128]{1,0:T(8,128)S(1)}, f32[576,128]{1,0:T(8,128)S(1)}, u32[]{:S(2)}, u32[]{:S(2)}) collective-permute-start(f32[576,128]{1,0:T(8,128)S(1)} %all_gather.3), channel_id=1, source_target_pairs={{0,2},{1,31},{2,4},{3,1},{4,6},{5,3},{6,8},{7,5},{8,10},{9,7},{10,... | collective-permute-start | bytes 884744 | tf_op jit(solution)/shard_map/ppermute | solution.py:445
  137.8 2.1 %collective-permute-done.5 = f32[576,128]{1,0:T(8,128)S(1)} collective-permute-done((f32[576,128]{1,0:T(8,128)S(1)}, f32[576,128]{1,0:T(8,128)S(1)}, u32[]{:S(2)}, u32[]{:S(2)}) %collective-permute-start.5) | collective-permute-done | bytes 294944 | tf_op jit(solution)/shard_map/ppermute | solution.py:445
  139.9 1.8 collective-permute-done.6
  141.8 12.3 %collective-permute-start.7 = (f32[2304,128]{1,0:T(8,128)S(1)}, f32[2304,128]{1,0:T(8,128)S(1)}, u32[]{:S(2)}, u32[]{:S(2)}) collective-permute-start(f32[2304,128]{1,0:T(8,128)S(1)} %constant_dynamic-update-slice_fusion.mine_ref), channel_id=1, source_target_pairs={{0,1},{1,0},{2,3},{3,2},{4,5},{5,4},{6,7},{7,6},{8,9},{9,8},{10,11... | collective-permute-start | bytes 3538952 | tf_op jit(solution)/shard_map/ppermute | solution.py:449
  154.1 2.3 %collective-permute-done.7.other_ref = f32[2304,128]{1,0:T(8,128)S(1)} collective-permute-done((f32[2304,128]{1,0:T(8,128)S(1)}, f32[2304,128]{1,0:T(8,128)S(1)}, u32[]{:S(2)}, u32[]{:S(2)}) %collective-permute-start.7) | collective-permute-done | bytes 1179680 | tf_op jit(solution)/shard_map/ppermute | solution.py:449
  156.3 29.0 %factor.1 = (f32[32,1024]{1,0:T(8,128)}, f32[256,1024]{1,0:T(8,128)}) custom-call(s32[16]{0:T(128)S(1)} %copy-done.5, f32[2304,128]{1,0:T(8,128)S(1)} %constant_dynamic-update-slice_fusion.mine_ref, f32[2304,128]{1,0:T(8,128)S(1)} %collective-permute-done.7.other_ref, f32[256,1024]{1,0:T(8,128)S(1)} %bitcast.6), custom_call_target="tpu_custom_call" | custom-call | tf_op jit(solution)/shard_map/factor/pallas_call | solution.py:423
  (5 shorter events, 0.1 us)
Async XLA Ops:
  0.6 0.9 copy-start.1
  1.5 0.8 copy-start.2
  2.4 0.7 copy-start.3
  5.3 7.8 %copy-start = (f32[1,256,1024]{2,1,0:T(8,128)S(1)}, f32[1,256,1024]{2,1,0:T(8,128)}, u32[]{:S(2)}) copy-start(f32[1,256,1024]{2,1,0:T(8,128)} %param.5) | copy-start | bytes 3145732
  5.3 7.8 %copy-start.5 = (s32[16]{0:T(128)S(1)}, s32[16]{0:T(128)}, u32[]{:S(2)}) copy-start(s32[16]{0:T(128)} %live_ref.3) | copy-start | bytes 196
  5.4 32.6 %all-to-all-start = ((f32[16,32,1024]{2,1,0:T(8,128)}), f32[16,32,1024]{2,1,0:T(8,128)}, u32[]{:S(2)}, u32[]{:S(2)}) async-start(f32[16,32,1024]{2,1,0:T(8,128)} %place_child.1), calls=%async_computation | async-start | bytes 4194304 | tf_op jit(solution)/shard_map/all_to_all | solution.py:479
  13.2 24.8 %copy-start.4 = (s32[16]{0:T(128)S(1)}, s32[16]{0:T(128)}, u32[]{:S(2)}) copy-start(s32[16]{0:T(128)} %parent_ref.3) | copy-start | bytes 196
  41.1 10.8 %collective-permute-start = (f32[2304,128]{1,0:T(8,128)S(1)}, f32[2304,128]{1,0:T(8,128)S(1)}, u32[]{:S(2)}, u32[]{:S(2)}) collective-permute-start(f32[2304,128]{1,0:T(8,128)S(1)} %get-tuple-element.7), channel_id=1, source_target_pairs={{0,1},{1,0},{2,3},{3,2},{4,5},{5,4},{6,7},{7,6},{8,9},{9,8},{10,11... | collective-permute-start | bytes 3538952 | tf_op jit(solution)/shard_map/ppermute | solution.py:449
  52.1 16.4 %collective-permute-start.1 = (f32[576,128]{1,0:T(8,128)S(1)}, f32[576,128]{1,0:T(8,128)S(1)}, u32[]{:S(2)}, u32[]{:S(2)}) collective-permute-start(f32[576,128]{1,0:T(8,128)S(1)} %get-tuple-element.10), channel_id=1, source_target_pairs={{0,2},{1,31},{2,4},{3,1},{4,6},{5,3},{6,8},{7,5},{8,10},{9,7},{10,... | collective-permute-start | bytes 884744 | tf_op jit(solution)/shard_map/ppermute | solution.py:445
  64.6 10.8 %collective-permute-start.3 = (f32[576,128]{1,0:T(8,128)S(1)}, f32[576,128]{1,0:T(8,128)S(1)}, u32[]{:S(2)}, u32[]{:S(2)}) collective-permute-start(f32[576,128]{1,0:T(8,128)S(1)} %get-tuple-element.11), channel_id=1, source_target_pairs={{0,28},{1,5},{2,30},{3,7},{4,0},{5,9},{6,2},{7,11},{8,4},{9,13},{1... | collective-permute-start | bytes 884744 | tf_op jit(solution)/shard_map/ppermute | solution.py:445
  66.5 12.2 %collective-permute-start.2 = (f32[576,128]{1,0:T(8,128)S(1)}, f32[576,128]{1,0:T(8,128)S(1)}, u32[]{:S(2)}, u32[]{:S(2)}) collective-permute-start(f32[576,128]{1,0:T(8,128)S(1)} %get-tuple-element.12), channel_id=1, source_target_pairs={{0,30},{1,3},{2,0},{3,5},{4,2},{5,7},{6,4},{7,9},{8,6},{9,11},{10,... | collective-permute-start | bytes 884744 | tf_op jit(solution)/shard_map/ppermute | solution.py:445
  121.9 9.3 %collective-permute-start.4 = (f32[576,128]{1,0:T(8,128)S(1)}, f32[576,128]{1,0:T(8,128)S(1)}, u32[]{:S(2)}, u32[]{:S(2)}) collective-permute-start(f32[576,128]{1,0:T(8,128)S(1)} %all_gather.3), channel_id=1, source_target_pairs={{0,30},{1,3},{2,0},{3,5},{4,2},{5,7},{6,4},{7,9},{8,6},{9,11},{10,... | collective-permute-start | bytes 884744 | tf_op jit(solution)/shard_map/ppermute | solution.py:445
  131.2 8.7 %collective-permute-start.5 = (f32[576,128]{1,0:T(8,128)S(1)}, f32[576,128]{1,0:T(8,128)S(1)}, u32[]{:S(2)}, u32[]{:S(2)}) collective-permute-start(f32[576,128]{1,0:T(8,128)S(1)} %collective-permute-done.4), channel_id=1, source_target_pairs={{0,30},{1,3},{2,0},{3,5},{4,2},{5,7},{6,4},{7,9},{8,6},{9,11},{10,... | collective-permute-start | bytes 884744 | tf_op jit(solution)/shard_map/ppermute | solution.py:445
  134.3 7.5 %collective-permute-start.6 = (f32[576,128]{1,0:T(8,128)S(1)}, f32[576,128]{1,0:T(8,128)S(1)}, u32[]{:S(2)}, u32[]{:S(2)}) collective-permute-start(f32[576,128]{1,0:T(8,128)S(1)} %all_gather.3), channel_id=1, source_target_pairs={{0,2},{1,31},{2,4},{3,1},{4,6},{5,3},{6,8},{7,5},{8,10},{9,7},{10,... | collective-permute-start | bytes 884744 | tf_op jit(solution)/shard_map/ppermute | solution.py:445
  141.8 14.6 %collective-permute-start.7 = (f32[2304,128]{1,0:T(8,128)S(1)}, f32[2304,128]{1,0:T(8,128)S(1)}, u32[]{:S(2)}, u32[]{:S(2)}) collective-permute-start(f32[2304,128]{1,0:T(8,128)S(1)} %constant_dynamic-update-slice_fusion.mine_ref), channel_id=1, source_target_pairs={{0,1},{1,0},{2,3},{3,2},{4,5},{5,4},{6,7},{7,6},{8,9},{9,8},{10,11... | collective-permute-start | bytes 3538952 | tf_op jit(solution)/shard_map/ppermute | solution.py:449

commit v5 on v4

--- a/solution.py
+++ b/solution.py
@@ -14,7 +14,7 @@
 NT = ((1,), (1,))
 VMEM = pl.BlockSpec(memory_space=pltpu.VMEM)
 SMEM = pl.BlockSpec(memory_space=pltpu.SMEM)
-ANY = pl.BlockSpec(memory_space=pl.ANY)
+HBM = pl.BlockSpec(memory_space=pltpu.HBM)
 PARAMS = pltpu.CompilerParams(vmem_limit_bytes=32 << 20)
 
 
@@ -37,12 +37,15 @@
     return [(i, j) for i in range(n) for j in range(i, n)]
 
 
-def place_kernel(parent_ref, tile_hbm, map_hbm, out_ref, tile_ref, map_ref, moved_ref, sems):
+def place_kernel(
+    parent_hbm, tile_hbm, map_hbm, out_ref, parent_ref, tile_ref, map_ref, moved_ref, sems
+):
     rows, width = tile_ref.shape
     group = lax.axis_index("front")
     fetches = [
         pltpu.make_async_copy(tile_hbm, tile_ref, sems.at[0]),
         pltpu.make_async_copy(map_hbm, map_ref, sems.at[1]),
+        pltpu.make_async_copy(parent_hbm, parent_ref, sems.at[3]),
     ]
     for fetch in fetches:
         fetch.start()
@@ -71,13 +74,14 @@
     return pl.pallas_call(
         place_kernel,
         out_shape=jax.ShapeDtypeStruct((col_map.shape[0],) + tile.shape, F32),
-        in_specs=[SMEM, ANY, ANY],
-        out_specs=ANY,
+        in_specs=[HBM, HBM, HBM],
+        out_specs=HBM,
         scratch_shapes=[
+            pltpu.SMEM(parent.shape, jnp.int32),
             pltpu.VMEM(tile.shape, F32),
             pltpu.VMEM(col_map.shape, jnp.int32),
             pltpu.VMEM(tile.shape, F32),
-            pltpu.SemaphoreType.DMA((3,)),
+            pltpu.SemaphoreType.DMA((4,)),
         ],
         compiler_params=PARAMS,
         name="place_child",
@@ -469,7 +473,7 @@
     whole = lax.all_gather(done, "rows", axis=0, axis_index_groups=classes, tiled=True)
     right = to_chip(whole, -1)
     left = to_chip(whole, 1)
-    far = to_chip(right, -1)
+    far = to_chip(whole, -2)
     mine = jnp.concatenate([whole, right, far, left])
     return mine, to_core(mine)
 

time: 186 us -> 182 us (0.978)
  starting transfers between devices: 55.6 us -> 52.9 us
    ppermute x2, starting transfers between devices: 20.7 us -> 16.4 us  [to_core(): lax.ppermute(x, 'rows', [(i, i ^ 1) for i in range(lax.axis_size('rows'))])]
  transfers between devices with their start and end apart: 9 -> 9, of which waited for: 8 -> 7; matrix products, arithmetic and copies ran while one was open for 0% -> 0% of each run, Pallas kernels for 1% -> 1%
where the time goes in v5:
time: 182 us
  starting transfers between devices  52.9 us (29%)
  waiting for transfers between devices  46.4 us (25%)
  blocking collectives  42.6 us (23%)
  Pallas kernels  36.4 us (20%)
  local copies, waits for them, and re-layouts  2.49 us (1%)
    pallas_call x1, Pallas kernels, factor(): pl.pallas_call(functools.partial(factor_kernel, total_rows), out_shape=(j...  29 us
    ppermute x6, starting transfers between devices, to_chip(): return lax.ppermute(x, 'rows', pairs)  28.7 us
    all_to_all x1, blocking collectives, sum_over_rows(): lax.all_to_all(summed, 'rows', split_axis=0, concat_axis=0, axis_index_gr...  25.6 us
    all_to_all x1, waiting for transfers between devices, body(): lax.all_to_all(place_child(parent, tile, col_map), 'front', split_axis=0,...  22.9 us
    ppermute x6, waiting for transfers between devices, to_chip(): return lax.ppermute(x, 'rows', pairs)  18.8 us
    all_gather x1, blocking collectives, sum_over_rows(): lax.all_gather(done, 'rows', axis=0, axis_index_groups=classes, tiled=True)  17 us
    ppermute x2, starting transfers between devices, to_core(): lax.ppermute(x, 'rows', [(i, i ^ 1) for i in range(lax.axis_size('rows'))])  16.4 us
    all_to_all x1, starting transfers between devices, body(): lax.all_to_all(place_child(parent, tile, col_map), 'front', split_axis=0,...  7.78 us
  transfers between devices with their start and end apart: 9, of which 7 were waited for; matrix products, arithmetic and copies ran while one was open for 0% of the time, Pallas kernels for 1%

profile of v5, /device:TPU:1, one launch (start us, length us, event | category | flops | bytes accessed | tf_op | source)
XLA Modules:
  0.0 181.8 jit_solution(14933409344436709562)
XLA Ops:
  0.6 0.0 copy-start.1
  0.6 0.9 copy-done.1
  1.5 0.0 copy-start.2
  1.5 0.8 copy-done.2
  2.4 0.0 copy-start.3
  2.4 0.7 copy-done.3
  3.0 2.2 %place_child.1 = f32[16,32,1024]{2,1,0:T(8,128)} custom-call(s32[16]{0:T(128)S(1)} %copy-done.3, f32[32,1024]{1,0:T(8,128)S(1)} %bitcast.7, s32[16,1024]{1,0:T(8,128)S(1)} %copy-done.2), custom_call_target="tpu_custom_call" | custom-call | tf_op jit(solution)/shard_map/place_child/pallas_call | solution.py:74
  5.3 0.0 copy-start
  5.3 0.0 copy-start.5
  5.3 7.8 %all-to-all-start = ((f32[16,32,1024]{2,1,0:T(8,128)}), f32[16,32,1024]{2,1,0:T(8,128)}, u32[]{:S(2)}, u32[]{:S(2)}) async-start(f32[16,32,1024]{2,1,0:T(8,128)} %place_child.1), calls=%async_computation | async-start | bytes 4194304 | tf_op jit(solution)/shard_map/all_to_all | solution.py:483
  13.1 0.0 copy-done
  13.1 0.0 copy-done.5
  13.1 0.0 copy-start.4
  13.1 1.9 %own_gram.1.mine_ref = f32[4608,128]{1,0:T(8,128)S(1)} custom-call(s32[16]{0:T(128)S(1)} %copy-done.5, f32[256,1024]{1,0:T(8,128)S(1)} %bitcast.5), custom_call_target="tpu_custom_call" | custom-call | tf_op jit(solution)/shard_map/own_gram/pallas_call | solution.py:114
  15.0 22.9 %all-to-all-done.arrived_ref = f32[16,32,1024]{2,1,0:T(8,128)} async-done(((f32[16,32,1024]{2,1,0:T(8,128)}), f32[16,32,1024]{2,1,0:T(8,128)}, u32[]{:S(2)}, u32[]{:S(2)}) %all-to-all-start) | async-done | bytes 2097184 | tf_op jit(solution)/shard_map/all_to_all | solution.py:483
  37.9 0.0 copy-done.4
  37.9 3.2 %add_children.1 = (f32[2304,128]{1,0:T(8,128)S(1)}, f32[2304,128]{1,0:T(8,128)S(1)}) custom-call(s32[16]{0:T(128)S(1)} %copy-done.4, f32[4608,128]{1,0:T(8,128)S(1)} %own_gram.1.mine_ref, f32[16,32,1024]{2,1,0:T(8,128)} %all-to-all-done.arrived_ref), custom_call_target="tpu_custom_call" | custom-call | tf_op jit(solution)/shard_map/add_children/pallas_call | solution.py:210
  41.1 8.3 %collective-permute-start = (f32[2304,128]{1,0:T(8,128)S(1)}, f32[2304,128]{1,0:T(8,128)S(1)}, u32[]{:S(2)}, u32[]{:S(2)}) collective-permute-start(f32[2304,128]{1,0:T(8,128)S(1)} %get-tuple-element.7), channel_id=1, source_target_pairs={{0,1},{1,0},{2,3},{3,2},{4,5},{5,4},{6,7},{7,6},{8,9},{9,8},{10,11... | collective-permute-start | bytes 3538952 | tf_op jit(solution)/shard_map/ppermute | solution.py:453
  49.4 2.5 %collective-permute-done = f32[2304,128]{1,0:T(8,128)S(1)} collective-permute-done((f32[2304,128]{1,0:T(8,128)S(1)}, f32[2304,128]{1,0:T(8,128)S(1)}, u32[]{:S(2)}, u32[]{:S(2)}) %collective-permute-start) | collective-permute-done | bytes 1179680 | tf_op jit(solution)/shard_map/ppermute | solution.py:453
  51.9 0.1 slice_add_fusion.2
  52.0 12.6 %collective-permute-start.1 = (f32[576,128]{1,0:T(8,128)S(1)}, f32[576,128]{1,0:T(8,128)S(1)}, u32[]{:S(2)}, u32[]{:S(2)}) collective-permute-start(f32[576,128]{1,0:T(8,128)S(1)} %get-tuple-element.10), channel_id=1, source_target_pairs={{0,2},{1,31},{2,4},{3,1},{4,6},{5,3},{6,8},{7,5},{8,10},{9,7},{10,... | collective-permute-start | bytes 884744 | tf_op jit(solution)/shard_map/ppermute | solution.py:449
  64.6 1.9 %collective-permute-start.3 = (f32[576,128]{1,0:T(8,128)S(1)}, f32[576,128]{1,0:T(8,128)S(1)}, u32[]{:S(2)}, u32[]{:S(2)}) collective-permute-start(f32[576,128]{1,0:T(8,128)S(1)} %get-tuple-element.11), channel_id=1, source_target_pairs={{0,28},{1,5},{2,30},{3,7},{4,0},{5,9},{6,2},{7,11},{8,4},{9,13},{1... | collective-permute-start | bytes 884744 | tf_op jit(solution)/shard_map/ppermute | solution.py:449
  66.5 1.9 %collective-permute-start.2 = (f32[576,128]{1,0:T(8,128)S(1)}, f32[576,128]{1,0:T(8,128)S(1)}, u32[]{:S(2)}, u32[]{:S(2)}) collective-permute-start(f32[576,128]{1,0:T(8,128)S(1)} %get-tuple-element.12), channel_id=1, source_target_pairs={{0,30},{1,3},{2,0},{3,5},{4,2},{5,7},{6,4},{7,9},{8,6},{9,11},{10,... | collective-permute-start | bytes 884744 | tf_op jit(solution)/shard_map/ppermute | solution.py:449
  68.4 0.0 collective-permute-done.1
  68.4 7.0 %collective-permute-done.3 = f32[576,128]{1,0:T(8,128)S(1)} collective-permute-done((f32[576,128]{1,0:T(8,128)S(1)}, f32[576,128]{1,0:T(8,128)S(1)}, u32[]{:S(2)}, u32[]{:S(2)}) %collective-permute-start.3) | collective-permute-done | bytes 294944 | tf_op jit(solution)/shard_map/ppermute | solution.py:449
  75.5 3.2 %collective-permute-done.2 = f32[576,128]{1,0:T(8,128)S(1)} collective-permute-done((f32[576,128]{1,0:T(8,128)S(1)}, f32[576,128]{1,0:T(8,128)S(1)}, u32[]{:S(2)}, u32[]{:S(2)}) %collective-permute-start.2) | collective-permute-done | bytes 294944 | tf_op jit(solution)/shard_map/ppermute | solution.py:449
  78.7 0.1 fusion.2
  78.8 25.6 %all_to_all.14 = f32[4,144,128]{2,1,0:T(8,128)S(1)} all-to-all(f32[4,144,128]{2,1,0:T(8,128)S(1)} %bitcast.8), channel_id=1, replica_groups={{0,8,16,24},{2,10,18,26},{4,12,20,28},{6,14,22,30},{1,9,17,25},{3,11,19..., dimensions={0} | all-to-all | bytes 589824 | tf_op jit(solution)/shard_map/all_to_all | solution.py:469
  104.4 17.0 %all_gather.3 = f32[576,128]{1,0:T(8,128)S(1)} all-gather(f32[144,128]{1,0:T(8,128)S(1)} %reduce_sum.9), channel_id=1, replica_groups={{0,8,16,24},{2,10,18,26},{4,12,20,28},{6,14,22,30},{1,9,17,25},{3,11,19..., dimensions={0}, use_global_device_ids=true | all-gather | bytes 368640 | tf_op jit(solution)/shard_map/all_gather | solution.py:473
  121.4 4.5 %collective-permute-start.4 = (f32[576,128]{1,0:T(8,128)S(1)}, f32[576,128]{1,0:T(8,128)S(1)}, u32[]{:S(2)}, u32[]{:S(2)}) collective-permute-start(f32[576,128]{1,0:T(8,128)S(1)} %all_gather.3), channel_id=1, source_target_pairs={{0,30},{1,3},{2,0},{3,5},{4,2},{5,7},{6,4},{7,9},{8,6},{9,11},{10,... | collective-permute-start | bytes 884744 | tf_op jit(solution)/shard_map/ppermute | solution.py:449
  125.9 3.2 %collective-permute-start.5 = (f32[576,128]{1,0:T(8,128)S(1)}, f32[576,128]{1,0:T(8,128)S(1)}, u32[]{:S(2)}, u32[]{:S(2)}) collective-permute-start(f32[576,128]{1,0:T(8,128)S(1)} %all_gather.3), channel_id=1, source_target_pairs={{0,28},{1,5},{2,30},{3,7},{4,0},{5,9},{6,2},{7,11},{8,4},{9,13},{1... | collective-permute-start | bytes 884744 | tf_op jit(solution)/shard_map/ppermute | solution.py:449
  129.1 4.6 %collective-permute-start.6 = (f32[576,128]{1,0:T(8,128)S(1)}, f32[576,128]{1,0:T(8,128)S(1)}, u32[]{:S(2)}, u32[]{:S(2)}) collective-permute-start(f32[576,128]{1,0:T(8,128)S(1)} %all_gather.3), channel_id=1, source_target_pairs={{0,2},{1,31},{2,4},{3,1},{4,6},{5,3},{6,8},{7,5},{8,10},{9,7},{10,... | collective-permute-start | bytes 884744 | tf_op jit(solution)/shard_map/ppermute | solution.py:449
  133.7 0.0 collective-permute-done.4
  133.8 2.9 %collective-permute-done.5 = f32[576,128]{1,0:T(8,128)S(1)} collective-permute-done((f32[576,128]{1,0:T(8,128)S(1)}, f32[576,128]{1,0:T(8,128)S(1)}, u32[]{:S(2)}, u32[]{:S(2)}) %collective-permute-start.5) | collective-permute-done | bytes 294944 | tf_op jit(solution)/shard_map/ppermute | solution.py:449
  136.6 5.7 %collective-permute-done.6 = f32[576,128]{1,0:T(8,128)S(1)} collective-permute-done((f32[576,128]{1,0:T(8,128)S(1)}, f32[576,128]{1,0:T(8,128)S(1)}, u32[]{:S(2)}, u32[]{:S(2)}) %collective-permute-start.6) | collective-permute-done | bytes 294944 | tf_op jit(solution)/shard_map/ppermute | solution.py:449
  142.4 8.1 %collective-permute-start.7 = (f32[2304,128]{1,0:T(8,128)S(1)}, f32[2304,128]{1,0:T(8,128)S(1)}, u32[]{:S(2)}, u32[]{:S(2)}) collective-permute-start(f32[2304,128]{1,0:T(8,128)S(1)} %constant_dynamic-update-slice_fusion.mine_ref), channel_id=1, source_target_pairs={{0,1},{1,0},{2,3},{3,2},{4,5},{5,4},{6,7},{7,6},{8,9},{9,8},{10,11... | collective-permute-start | bytes 3538952 | tf_op jit(solution)/shard_map/ppermute | solution.py:453
  150.5 2.3 %collective-permute-done.7.other_ref = f32[2304,128]{1,0:T(8,128)S(1)} collective-permute-done((f32[2304,128]{1,0:T(8,128)S(1)}, f32[2304,128]{1,0:T(8,128)S(1)}, u32[]{:S(2)}, u32[]{:S(2)}) %collective-permute-start.7) | collective-permute-done | bytes 1179680 | tf_op jit(solution)/shard_map/ppermute | solution.py:453
  152.7 29.0 %factor.1 = (f32[32,1024]{1,0:T(8,128)}, f32[256,1024]{1,0:T(8,128)}) custom-call(s32[16]{0:T(128)S(1)} %copy-done.5, f32[2304,128]{1,0:T(8,128)S(1)} %constant_dynamic-update-slice_fusion.mine_ref, f32[2304,128]{1,0:T(8,128)S(1)} %collective-permute-done.7.other_ref, f32[256,1024]{1,0:T(8,128)S(1)} %bitcast.6), custom_call_target="tpu_custom_call" | custom-call | tf_op jit(solution)/shard_map/factor/pallas_call | solution.py:427
  (5 shorter events, 0.1 us)
Async XLA Ops:
  0.6 0.9 copy-start.1
  1.5 0.8 copy-start.2
  2.4 0.7 copy-start.3
  5.3 7.8 %copy-start = (f32[1,256,1024]{2,1,0:T(8,128)S(1)}, f32[1,256,1024]{2,1,0:T(8,128)}, u32[]{:S(2)}) copy-start(f32[1,256,1024]{2,1,0:T(8,128)} %param.5) | copy-start | bytes 3145732
  5.3 7.8 %copy-start.5 = (s32[16]{0:T(128)S(1)}, s32[16]{0:T(128)}, u32[]{:S(2)}) copy-start(s32[16]{0:T(128)} %live_ref.3) | copy-start | bytes 196
  5.3 32.6 %all-to-all-start = ((f32[16,32,1024]{2,1,0:T(8,128)}), f32[16,32,1024]{2,1,0:T(8,128)}, u32[]{:S(2)}, u32[]{:S(2)}) async-start(f32[16,32,1024]{2,1,0:T(8,128)} %place_child.1), calls=%async_computation | async-start | bytes 4194304 | tf_op jit(solution)/shard_map/all_to_all | solution.py:483
  13.1 24.8 %copy-start.4 = (s32[16]{0:T(128)S(1)}, s32[16]{0:T(128)}, u32[]{:S(2)}) copy-start(s32[16]{0:T(128)} %parent_ref.1) | copy-start | bytes 196
  41.1 10.8 %collective-permute-start = (f32[2304,128]{1,0:T(8,128)S(1)}, f32[2304,128]{1,0:T(8,128)S(1)}, u32[]{:S(2)}, u32[]{:S(2)}) collective-permute-start(f32[2304,128]{1,0:T(8,128)S(1)} %get-tuple-element.7), channel_id=1, source_target_pairs={{0,1},{1,0},{2,3},{3,2},{4,5},{5,4},{6,7},{7,6},{8,9},{9,8},{10,11... | collective-permute-start | bytes 3538952 | tf_op jit(solution)/shard_map/ppermute | solution.py:453
  52.0 16.4 %collective-permute-start.1 = (f32[576,128]{1,0:T(8,128)S(1)}, f32[576,128]{1,0:T(8,128)S(1)}, u32[]{:S(2)}, u32[]{:S(2)}) collective-permute-start(f32[576,128]{1,0:T(8,128)S(1)} %get-tuple-element.10), channel_id=1, source_target_pairs={{0,2},{1,31},{2,4},{3,1},{4,6},{5,3},{6,8},{7,5},{8,10},{9,7},{10,... | collective-permute-start | bytes 884744 | tf_op jit(solution)/shard_map/ppermute | solution.py:449
  64.6 10.9 %collective-permute-start.3 = (f32[576,128]{1,0:T(8,128)S(1)}, f32[576,128]{1,0:T(8,128)S(1)}, u32[]{:S(2)}, u32[]{:S(2)}) collective-permute-start(f32[576,128]{1,0:T(8,128)S(1)} %get-tuple-element.11), channel_id=1, source_target_pairs={{0,28},{1,5},{2,30},{3,7},{4,0},{5,9},{6,2},{7,11},{8,4},{9,13},{1... | collective-permute-start | bytes 884744 | tf_op jit(solution)/shard_map/ppermute | solution.py:449
  66.5 12.2 %collective-permute-start.2 = (f32[576,128]{1,0:T(8,128)S(1)}, f32[576,128]{1,0:T(8,128)S(1)}, u32[]{:S(2)}, u32[]{:S(2)}) collective-permute-start(f32[576,128]{1,0:T(8,128)S(1)} %get-tuple-element.12), channel_id=1, source_target_pairs={{0,30},{1,3},{2,0},{3,5},{4,2},{5,7},{6,4},{7,9},{8,6},{9,11},{10,... | collective-permute-start | bytes 884744 | tf_op jit(solution)/shard_map/ppermute | solution.py:449
  121.4 12.3 %collective-permute-start.4 = (f32[576,128]{1,0:T(8,128)S(1)}, f32[576,128]{1,0:T(8,128)S(1)}, u32[]{:S(2)}, u32[]{:S(2)}) collective-permute-start(f32[576,128]{1,0:T(8,128)S(1)} %all_gather.3), channel_id=1, source_target_pairs={{0,30},{1,3},{2,0},{3,5},{4,2},{5,7},{6,4},{7,9},{8,6},{9,11},{10,... | collective-permute-start | bytes 884744 | tf_op jit(solution)/shard_map/ppermute | solution.py:449
  125.9 10.7 %collective-permute-start.5 = (f32[576,128]{1,0:T(8,128)S(1)}, f32[576,128]{1,0:T(8,128)S(1)}, u32[]{:S(2)}, u32[]{:S(2)}) collective-permute-start(f32[576,128]{1,0:T(8,128)S(1)} %all_gather.3), channel_id=1, source_target_pairs={{0,28},{1,5},{2,30},{3,7},{4,0},{5,9},{6,2},{7,11},{8,4},{9,13},{1... | collective-permute-start | bytes 884744 | tf_op jit(solution)/shard_map/ppermute | solution.py:449
  129.1 13.2 %collective-permute-start.6 = (f32[576,128]{1,0:T(8,128)S(1)}, f32[576,128]{1,0:T(8,128)S(1)}, u32[]{:S(2)}, u32[]{:S(2)}) collective-permute-start(f32[576,128]{1,0:T(8,128)S(1)} %all_gather.3), channel_id=1, source_target_pairs={{0,2},{1,31},{2,4},{3,1},{4,6},{5,3},{6,8},{7,5},{8,10},{9,7},{10,... | collective-permute-start | bytes 884744 | tf_op jit(solution)/shard_map/ppermute | solution.py:449
  142.4 10.4 %collective-permute-start.7 = (f32[2304,128]{1,0:T(8,128)S(1)}, f32[2304,128]{1,0:T(8,128)S(1)}, u32[]{:S(2)}, u32[]{:S(2)}) collective-permute-start(f32[2304,128]{1,0:T(8,128)S(1)} %constant_dynamic-update-slice_fusion.mine_ref), channel_id=1, source_target_pairs={{0,1},{1,0},{2,3},{3,2},{4,5},{5,4},{6,7},{7,6},{8,9},{9,8},{10,11... | collective-permute-start | bytes 3538952 | tf_op jit(solution)/shard_map/ppermute | solution.py:453

commit v6 on v5

--- a/solution.py
+++ b/solution.py
@@ -83,7 +83,7 @@
             pltpu.VMEM(tile.shape, F32),
             pltpu.SemaphoreType.DMA((4,)),
         ],
-        compiler_params=PARAMS,
+        compiler_params=pltpu.CompilerParams(vmem_limit_bytes=63 << 20),
         name="place_child",
     )(parent, tile, col_map)
 
@@ -413,7 +413,7 @@
         return carry
 
     step(None, jnp.int32(0), 0)
-    lax.fori_loop(1, n // 2, functools.partial(step, 0), 0)
+    lax.fori_loop(1, n // 2, functools.partial(step, 1), 0)
     lax.fori_loop(n // 2, n, functools.partial(step, n // 2), 0)
     start = pl.multiple_of(place * r_ref.shape[0], r_ref.shape[0])
     mine = a_ref[pl.ds(start, r_ref.shape[0]), :]

time: 182 us -> 180 us (0.989)
  local copies, waits for them, and re-layouts: 2.49 us -> 0.1 us
    unnamed x15 -> x9, local copies, waits for them, and re-layouts: 2.47 us -> 0.08 us
where the time goes in v6:
time: 180 us; the launch traced here: 179 us
  starting transfers between devices  51.8 us (29%)
  waiting for transfers between devices  46.9 us (26%)
  blocking collectives  43.4 us (24%)
  Pallas kernels  36.2 us (20%)
    pallas_call x1, Pallas kernels, factor(): pl.pallas_call(functools.partial(factor_kernel, total_rows), out_shape=(j...  28.7 us
    ppermute x6, starting transfers between devices, to_chip(): return lax.ppermute(x, 'rows', pairs)  27.2 us
    all_to_all x1, blocking collectives, sum_over_rows(): lax.all_to_all(summed, 'rows', split_axis=0, concat_axis=0, axis_index_gr...  25.5 us
    all_to_all x1, waiting for transfers between devices, body(): lax.all_to_all(place_child(parent, tile, col_map), 'front', split_axis=0,...  22.8 us
    ppermute x6, waiting for transfers between devices, to_chip(): return lax.ppermute(x, 'rows', pairs)  19.3 us
    all_gather x1, blocking collectives, sum_over_rows(): lax.all_gather(done, 'rows', axis=0, axis_index_groups=classes, tiled=True)  17.8 us
    ppermute x2, starting transfers between devices, to_core(): lax.ppermute(x, 'rows', [(i, i ^ 1) for i in range(lax.axis_size('rows'))])  16.8 us
    all_to_all x1, starting transfers between devices, body(): lax.all_to_all(place_child(parent, tile, col_map), 'front', split_axis=0,...  7.78 us
  transfers between devices with their start and end apart: 9, of which 7 were waited for; matrix products, arithmetic and copies ran while one was open for 0% of the time, Pallas kernels for 1%

profile of v6, /device:TPU:1, one launch (start us, length us, event | category | flops | bytes accessed | tf_op | source)
XLA Modules:
  0.0 179.4 jit_solution(14153891265056738)
XLA Ops:
  0.6 2.4 %place_child.1 = f32[16,32,1024]{2,1,0:T(8,128)} custom-call(s32[16]{0:T(128)} %parent_ref.1, f32[32,1024]{1,0:T(8,128)} %bitcast.8, s32[16,1024]{1,0:T(8,128)} %map_hbm.1), custom_call_target="tpu_custom_call" | custom-call | tf_op jit(solution)/shard_map/place_child/pallas_call | solution.py:74
  3.0 0.0 copy-start
  3.0 0.0 copy-start.2
  3.1 7.8 %all-to-all-start = ((f32[16,32,1024]{2,1,0:T(8,128)}), f32[16,32,1024]{2,1,0:T(8,128)}, u32[]{:S(2)}, u32[]{:S(2)}) async-start(f32[16,32,1024]{2,1,0:T(8,128)} %place_child.1), calls=%async_computation | async-start | bytes 4194304 | tf_op jit(solution)/shard_map/all_to_all | solution.py:483
  10.8 0.0 copy-done
  10.9 0.0 copy-done.2
  10.9 0.0 copy-start.1
  10.9 1.9 %own_gram.1.mine_ref = f32[4608,128]{1,0:T(8,128)S(1)} custom-call(s32[16]{0:T(128)S(1)} %copy-done.2, f32[256,1024]{1,0:T(8,128)S(1)} %bitcast.5), custom_call_target="tpu_custom_call" | custom-call | tf_op jit(solution)/shard_map/own_gram/pallas_call | solution.py:114
  12.8 22.8 %all-to-all-done.arrived_ref = f32[16,32,1024]{2,1,0:T(8,128)} async-done(((f32[16,32,1024]{2,1,0:T(8,128)}), f32[16,32,1024]{2,1,0:T(8,128)}, u32[]{:S(2)}, u32[]{:S(2)}) %all-to-all-start) | async-done | bytes 2097184 | tf_op jit(solution)/shard_map/all_to_all | solution.py:483
  35.6 0.0 copy-done.1
  35.6 3.2 %add_children.1 = (f32[2304,128]{1,0:T(8,128)S(1)}, f32[2304,128]{1,0:T(8,128)S(1)}) custom-call(s32[16]{0:T(128)S(1)} %copy-done.1, f32[4608,128]{1,0:T(8,128)S(1)} %own_gram.1.mine_ref, f32[16,32,1024]{2,1,0:T(8,128)} %all-to-all-done.arrived_ref), custom_call_target="tpu_custom_call" | custom-call | tf_op jit(solution)/shard_map/add_children/pallas_call | solution.py:210
  38.9 8.3 %collective-permute-start = (f32[2304,128]{1,0:T(8,128)S(1)}, f32[2304,128]{1,0:T(8,128)S(1)}, u32[]{:S(2)}, u32[]{:S(2)}) collective-permute-start(f32[2304,128]{1,0:T(8,128)S(1)} %get-tuple-element.7), channel_id=1, source_target_pairs={{0,1},{1,0},{2,3},{3,2},{4,5},{5,4},{6,7},{7,6},{8,9},{9,8},{10,11... | collective-permute-start | bytes 3538952 | tf_op jit(solution)/shard_map/ppermute | solution.py:453
  47.2 2.5 %collective-permute-done = f32[2304,128]{1,0:T(8,128)S(1)} collective-permute-done((f32[2304,128]{1,0:T(8,128)S(1)}, f32[2304,128]{1,0:T(8,128)S(1)}, u32[]{:S(2)}, u32[]{:S(2)}) %collective-permute-start) | collective-permute-done | bytes 1179680 | tf_op jit(solution)/shard_map/ppermute | solution.py:453
  49.6 0.1 slice_add_fusion.2
  49.7 12.6 %collective-permute-start.1 = (f32[576,128]{1,0:T(8,128)S(1)}, f32[576,128]{1,0:T(8,128)S(1)}, u32[]{:S(2)}, u32[]{:S(2)}) collective-permute-start(f32[576,128]{1,0:T(8,128)S(1)} %get-tuple-element.10), channel_id=1, source_target_pairs={{0,2},{1,31},{2,4},{3,1},{4,6},{5,3},{6,8},{7,5},{8,10},{9,7},{10,... | collective-permute-start | bytes 884744 | tf_op jit(solution)/shard_map/ppermute | solution.py:449
  62.4 1.9 %collective-permute-start.3 = (f32[576,128]{1,0:T(8,128)S(1)}, f32[576,128]{1,0:T(8,128)S(1)}, u32[]{:S(2)}, u32[]{:S(2)}) collective-permute-start(f32[576,128]{1,0:T(8,128)S(1)} %get-tuple-element.11), channel_id=1, source_target_pairs={{0,28},{1,5},{2,30},{3,7},{4,0},{5,9},{6,2},{7,11},{8,4},{9,13},{1... | collective-permute-start | bytes 884744 | tf_op jit(solution)/shard_map/ppermute | solution.py:449
  64.3 1.9 %collective-permute-start.2 = (f32[576,128]{1,0:T(8,128)S(1)}, f32[576,128]{1,0:T(8,128)S(1)}, u32[]{:S(2)}, u32[]{:S(2)}) collective-permute-start(f32[576,128]{1,0:T(8,128)S(1)} %get-tuple-element.12), channel_id=1, source_target_pairs={{0,30},{1,3},{2,0},{3,5},{4,2},{5,7},{6,4},{7,9},{8,6},{9,11},{10,... | collective-permute-start | bytes 884744 | tf_op jit(solution)/shard_map/ppermute | solution.py:449
  66.2 0.0 collective-permute-done.1
  66.2 7.0 %collective-permute-done.3 = f32[576,128]{1,0:T(8,128)S(1)} collective-permute-done((f32[576,128]{1,0:T(8,128)S(1)}, f32[576,128]{1,0:T(8,128)S(1)}, u32[]{:S(2)}, u32[]{:S(2)}) %collective-permute-start.3) | collective-permute-done | bytes 294944 | tf_op jit(solution)/shard_map/ppermute | solution.py:449
  73.2 3.2 %collective-permute-done.2 = f32[576,128]{1,0:T(8,128)S(1)} collective-permute-done((f32[576,128]{1,0:T(8,128)S(1)}, f32[576,128]{1,0:T(8,128)S(1)}, u32[]{:S(2)}, u32[]{:S(2)}) %collective-permute-start.2) | collective-permute-done | bytes 294944 | tf_op jit(solution)/shard_map/ppermute | solution.py:449
  76.5 0.1 fusion.2
  76.6 25.5 %all_to_all.14 = f32[4,144,128]{2,1,0:T(8,128)S(1)} all-to-all(f32[4,144,128]{2,1,0:T(8,128)S(1)} %bitcast.7), channel_id=1, replica_groups={{0,8,16,24},{2,10,18,26},{4,12,20,28},{6,14,22,30},{1,9,17,25},{3,11,19..., dimensions={0} | all-to-all | bytes 589824 | tf_op jit(solution)/shard_map/all_to_all | solution.py:469
  102.1 17.8 %all_gather.3 = f32[576,128]{1,0:T(8,128)S(1)} all-gather(f32[144,128]{1,0:T(8,128)S(1)} %reduce_sum.9), channel_id=1, replica_groups={{0,8,16,24},{2,10,18,26},{4,12,20,28},{6,14,22,30},{1,9,17,25},{3,11,19..., dimensions={0}, use_global_device_ids=true | all-gather | bytes 368640 | tf_op jit(solution)/shard_map/all_gather | solution.py:473
  120.0 3.3 %collective-permute-start.4 = (f32[576,128]{1,0:T(8,128)S(1)}, f32[576,128]{1,0:T(8,128)S(1)}, u32[]{:S(2)}, u32[]{:S(2)}) collective-permute-start(f32[576,128]{1,0:T(8,128)S(1)} %all_gather.3), channel_id=1, source_target_pairs={{0,30},{1,3},{2,0},{3,5},{4,2},{5,7},{6,4},{7,9},{8,6},{9,11},{10,... | collective-permute-start | bytes 884744 | tf_op jit(solution)/shard_map/ppermute | solution.py:449
  123.3 2.9 %collective-permute-start.5 = (f32[576,128]{1,0:T(8,128)S(1)}, f32[576,128]{1,0:T(8,128)S(1)}, u32[]{:S(2)}, u32[]{:S(2)}) collective-permute-start(f32[576,128]{1,0:T(8,128)S(1)} %all_gather.3), channel_id=1, source_target_pairs={{0,28},{1,5},{2,30},{3,7},{4,0},{5,9},{6,2},{7,11},{8,4},{9,13},{1... | collective-permute-start | bytes 884744 | tf_op jit(solution)/shard_map/ppermute | solution.py:449
  126.2 4.6 %collective-permute-start.6 = (f32[576,128]{1,0:T(8,128)S(1)}, f32[576,128]{1,0:T(8,128)S(1)}, u32[]{:S(2)}, u32[]{:S(2)}) collective-permute-start(f32[576,128]{1,0:T(8,128)S(1)} %all_gather.3), channel_id=1, source_target_pairs={{0,2},{1,31},{2,4},{3,1},{4,6},{5,3},{6,8},{7,5},{8,10},{9,7},{10,... | collective-permute-start | bytes 884744 | tf_op jit(solution)/shard_map/ppermute | solution.py:449
  130.8 0.0 collective-permute-done.4
  130.9 3.7 %collective-permute-done.5 = f32[576,128]{1,0:T(8,128)S(1)} collective-permute-done((f32[576,128]{1,0:T(8,128)S(1)}, f32[576,128]{1,0:T(8,128)S(1)}, u32[]{:S(2)}, u32[]{:S(2)}) %collective-permute-start.5) | collective-permute-done | bytes 294944 | tf_op jit(solution)/shard_map/ppermute | solution.py:449
  134.5 5.4 %collective-permute-done.6 = f32[576,128]{1,0:T(8,128)S(1)} collective-permute-done((f32[576,128]{1,0:T(8,128)S(1)}, f32[576,128]{1,0:T(8,128)S(1)}, u32[]{:S(2)}, u32[]{:S(2)}) %collective-permute-start.6) | collective-permute-done | bytes 294944 | tf_op jit(solution)/shard_map/ppermute | solution.py:449
  140.0 8.5 %collective-permute-start.7 = (f32[2304,128]{1,0:T(8,128)S(1)}, f32[2304,128]{1,0:T(8,128)S(1)}, u32[]{:S(2)}, u32[]{:S(2)}) collective-permute-start(f32[2304,128]{1,0:T(8,128)S(1)} %constant_dynamic-update-slice_fusion.mine_ref), channel_id=1, source_target_pairs={{0,1},{1,0},{2,3},{3,2},{4,5},{5,4},{6,7},{7,6},{8,9},{9,8},{10,11... | collective-permute-start | bytes 3538952 | tf_op jit(solution)/shard_map/ppermute | solution.py:453
  148.4 2.3 %collective-permute-done.7.other_ref = f32[2304,128]{1,0:T(8,128)S(1)} collective-permute-done((f32[2304,128]{1,0:T(8,128)S(1)}, f32[2304,128]{1,0:T(8,128)S(1)}, u32[]{:S(2)}, u32[]{:S(2)}) %collective-permute-start.7) | collective-permute-done | bytes 1179680 | tf_op jit(solution)/shard_map/ppermute | solution.py:453
  150.7 28.7 %factor.1 = (f32[32,1024]{1,0:T(8,128)}, f32[256,1024]{1,0:T(8,128)}) custom-call(s32[16]{0:T(128)S(1)} %copy-done.2, f32[2304,128]{1,0:T(8,128)S(1)} %constant_dynamic-update-slice_fusion.mine_ref, f32[2304,128]{1,0:T(8,128)S(1)} %collective-permute-done.7.other_ref, f32[256,1024]{1,0:T(8,128)S(1)} %bitcast.6), custom_call_target="tpu_custom_call" | custom-call | tf_op jit(solution)/shard_map/factor/pallas_call | solution.py:427
  (5 shorter events, 0.1 us)
Async XLA Ops:
  3.0 7.8 %copy-start = (f32[1,256,1024]{2,1,0:T(8,128)S(1)}, f32[1,256,1024]{2,1,0:T(8,128)}, u32[]{:S(2)}) copy-start(f32[1,256,1024]{2,1,0:T(8,128)} %param.5) | copy-start | bytes 3145732
  3.0 7.8 %copy-start.2 = (s32[16]{0:T(128)S(1)}, s32[16]{0:T(128)}, u32[]{:S(2)}) copy-start(s32[16]{0:T(128)} %live_ref.3) | copy-start | bytes 196
  3.1 32.6 %all-to-all-start = ((f32[16,32,1024]{2,1,0:T(8,128)}), f32[16,32,1024]{2,1,0:T(8,128)}, u32[]{:S(2)}, u32[]{:S(2)}) async-start(f32[16,32,1024]{2,1,0:T(8,128)} %place_child.1), calls=%async_computation | async-start | bytes 4194304 | tf_op jit(solution)/shard_map/all_to_all | solution.py:483
  10.9 24.8 %copy-start.1 = (s32[16]{0:T(128)S(1)}, s32[16]{0:T(128)}, u32[]{:S(2)}) copy-start(s32[16]{0:T(128)} %parent_ref.1) | copy-start | bytes 196
  38.9 10.8 %collective-permute-start = (f32[2304,128]{1,0:T(8,128)S(1)}, f32[2304,128]{1,0:T(8,128)S(1)}, u32[]{:S(2)}, u32[]{:S(2)}) collective-permute-start(f32[2304,128]{1,0:T(8,128)S(1)} %get-tuple-element.7), channel_id=1, source_target_pairs={{0,1},{1,0},{2,3},{3,2},{4,5},{5,4},{6,7},{7,6},{8,9},{9,8},{10,11... | collective-permute-start | bytes 3538952 | tf_op jit(solution)/shard_map/ppermute | solution.py:453
  49.7 16.5 %collective-permute-start.1 = (f32[576,128]{1,0:T(8,128)S(1)}, f32[576,128]{1,0:T(8,128)S(1)}, u32[]{:S(2)}, u32[]{:S(2)}) collective-permute-start(f32[576,128]{1,0:T(8,128)S(1)} %get-tuple-element.10), channel_id=1, source_target_pairs={{0,2},{1,31},{2,4},{3,1},{4,6},{5,3},{6,8},{7,5},{8,10},{9,7},{10,... | collective-permute-start | bytes 884744 | tf_op jit(solution)/shard_map/ppermute | solution.py:449
  62.4 10.9 %collective-permute-start.3 = (f32[576,128]{1,0:T(8,128)S(1)}, f32[576,128]{1,0:T(8,128)S(1)}, u32[]{:S(2)}, u32[]{:S(2)}) collective-permute-start(f32[576,128]{1,0:T(8,128)S(1)} %get-tuple-element.11), channel_id=1, source_target_pairs={{0,28},{1,5},{2,30},{3,7},{4,0},{5,9},{6,2},{7,11},{8,4},{9,13},{1... | collective-permute-start | bytes 884744 | tf_op jit(solution)/shard_map/ppermute | solution.py:449
  64.3 12.2 %collective-permute-start.2 = (f32[576,128]{1,0:T(8,128)S(1)}, f32[576,128]{1,0:T(8,128)S(1)}, u32[]{:S(2)}, u32[]{:S(2)}) collective-permute-start(f32[576,128]{1,0:T(8,128)S(1)} %get-tuple-element.12), channel_id=1, source_target_pairs={{0,30},{1,3},{2,0},{3,5},{4,2},{5,7},{6,4},{7,9},{8,6},{9,11},{10,... | collective-permute-start | bytes 884744 | tf_op jit(solution)/shard_map/ppermute | solution.py:449
  120.0 10.8 %collective-permute-start.4 = (f32[576,128]{1,0:T(8,128)S(1)}, f32[576,128]{1,0:T(8,128)S(1)}, u32[]{:S(2)}, u32[]{:S(2)}) collective-permute-start(f32[576,128]{1,0:T(8,128)S(1)} %all_gather.3), channel_id=1, source_target_pairs={{0,30},{1,3},{2,0},{3,5},{4,2},{5,7},{6,4},{7,9},{8,6},{9,11},{10,... | collective-permute-start | bytes 884744 | tf_op jit(solution)/shard_map/ppermute | solution.py:449
  123.3 11.2 %collective-permute-start.5 = (f32[576,128]{1,0:T(8,128)S(1)}, f32[576,128]{1,0:T(8,128)S(1)}, u32[]{:S(2)}, u32[]{:S(2)}) collective-permute-start(f32[576,128]{1,0:T(8,128)S(1)} %all_gather.3), channel_id=1, source_target_pairs={{0,28},{1,5},{2,30},{3,7},{4,0},{5,9},{6,2},{7,11},{8,4},{9,13},{1... | collective-permute-start | bytes 884744 | tf_op jit(solution)/shard_map/ppermute | solution.py:449
  126.2 13.8 %collective-permute-start.6 = (f32[576,128]{1,0:T(8,128)S(1)}, f32[576,128]{1,0:T(8,128)S(1)}, u32[]{:S(2)}, u32[]{:S(2)}) collective-permute-start(f32[576,128]{1,0:T(8,128)S(1)} %all_gather.3), channel_id=1, source_target_pairs={{0,2},{1,31},{2,4},{3,1},{4,6},{5,3},{6,8},{7,5},{8,10},{9,7},{10,... | collective-permute-start | bytes 884744 | tf_op jit(solution)/shard_map/ppermute | solution.py:449
  140.0 10.7 %collective-permute-start.7 = (f32[2304,128]{1,0:T(8,128)S(1)}, f32[2304,128]{1,0:T(8,128)S(1)}, u32[]{:S(2)}, u32[]{:S(2)}) collective-permute-start(f32[2304,128]{1,0:T(8,128)S(1)} %constant_dynamic-update-slice_fusion.mine_ref), channel_id=1, source_target_pairs={{0,1},{1,0},{2,3},{3,2},{4,5},{5,4},{6,7},{7,6},{8,9},{9,8},{10,11... | collective-permute-start | bytes 3538952 | tf_op jit(solution)/shard_map/ppermute | solution.py:453

commit v7 on v6

--- a/solution.py
+++ b/solution.py
@@ -413,8 +413,8 @@
         return carry
 
     step(None, jnp.int32(0), 0)
-    lax.fori_loop(1, n // 2, functools.partial(step, 1), 0)
-    lax.fori_loop(n // 2, n, functools.partial(step, n // 2), 0)
+    for first, last in ((1, 3), (3, 5), (5, n)):
+        lax.fori_loop(first, last, functools.partial(step, first), 0)
     start = pl.multiple_of(place * r_ref.shape[0], r_ref.shape[0])
     mine = a_ref[pl.ds(start, r_ref.shape[0]), :]
     row = start + lax.broadcasted_iota(jnp.int32, mine.shape, 0)

time: 180 us -> 180 us (level)
  no operation moved by 1% of the time
where the time goes in v7:
time: 180 us; the launch traced here: 179 us
  starting transfers between devices  52.2 us (29%)
  waiting for transfers between devices  46.9 us (26%)
  blocking collectives  43 us (24%)
  Pallas kernels  35.8 us (20%)
    pallas_call x1, Pallas kernels, factor(): pl.pallas_call(functools.partial(factor_kernel, total_rows), out_shape=(j...  28.3 us
    ppermute x6, starting transfers between devices, to_chip(): return lax.ppermute(x, 'rows', pairs)  27.6 us
    all_to_all x1, blocking collectives, sum_over_rows(): lax.all_to_all(summed, 'rows', split_axis=0, concat_axis=0, axis_index_gr...  25.5 us
    all_to_all x1, waiting for transfers between devices, body(): lax.all_to_all(place_child(parent, tile, col_map), 'front', split_axis=0,...  22.8 us
    ppermute x6, waiting for transfers between devices, to_chip(): return lax.ppermute(x, 'rows', pairs)  19.3 us
    all_gather x1, blocking collectives, sum_over_rows(): lax.all_gather(done, 'rows', axis=0, axis_index_groups=classes, tiled=True)  17.4 us
    ppermute x2, starting transfers between devices, to_core(): lax.ppermute(x, 'rows', [(i, i ^ 1) for i in range(lax.axis_size('rows'))])  16.8 us
    all_to_all x1, starting transfers between devices, body(): lax.all_to_all(place_child(parent, tile, col_map), 'front', split_axis=0,...  7.78 us
  transfers between devices with their start and end apart: 9, of which 7 were waited for; matrix products, arithmetic and copies ran while one was open for 0% of the time, Pallas kernels for 1%

profile of v7, /device:TPU:1, one launch (start us, length us, event | category | flops | bytes accessed | tf_op | source)
XLA Modules:
  0.0 179.0 jit_solution(2550479800043276833)
XLA Ops:
  0.6 2.4 %place_child.1 = f32[16,32,1024]{2,1,0:T(8,128)} custom-call(s32[16]{0:T(128)} %parent_ref.1, f32[32,1024]{1,0:T(8,128)} %bitcast.8, s32[16,1024]{1,0:T(8,128)} %map_hbm.1), custom_call_target="tpu_custom_call" | custom-call | tf_op jit(solution)/shard_map/place_child/pallas_call | solution.py:74
  3.0 0.0 copy-start
  3.0 0.0 copy-start.2
  3.1 7.8 %all-to-all-start = ((f32[16,32,1024]{2,1,0:T(8,128)}), f32[16,32,1024]{2,1,0:T(8,128)}, u32[]{:S(2)}, u32[]{:S(2)}) async-start(f32[16,32,1024]{2,1,0:T(8,128)} %place_child.1), calls=%async_computation | async-start | bytes 4194304 | tf_op jit(solution)/shard_map/all_to_all | solution.py:483
  10.8 0.0 copy-done
  10.9 0.0 copy-done.2
  10.9 0.0 copy-start.1
  10.9 1.9 %own_gram.1.mine_ref = f32[4608,128]{1,0:T(8,128)S(1)} custom-call(s32[16]{0:T(128)S(1)} %copy-done.2, f32[256,1024]{1,0:T(8,128)S(1)} %bitcast.5), custom_call_target="tpu_custom_call" | custom-call | tf_op jit(solution)/shard_map/own_gram/pallas_call | solution.py:114
  12.8 22.8 %all-to-all-done.arrived_ref = f32[16,32,1024]{2,1,0:T(8,128)} async-done(((f32[16,32,1024]{2,1,0:T(8,128)}), f32[16,32,1024]{2,1,0:T(8,128)}, u32[]{:S(2)}, u32[]{:S(2)}) %all-to-all-start) | async-done | bytes 2097184 | tf_op jit(solution)/shard_map/all_to_all | solution.py:483
  35.6 0.0 copy-done.1
  35.6 3.2 %add_children.1 = (f32[2304,128]{1,0:T(8,128)S(1)}, f32[2304,128]{1,0:T(8,128)S(1)}) custom-call(s32[16]{0:T(128)S(1)} %copy-done.1, f32[4608,128]{1,0:T(8,128)S(1)} %own_gram.1.mine_ref, f32[16,32,1024]{2,1,0:T(8,128)} %all-to-all-done.arrived_ref), custom_call_target="tpu_custom_call" | custom-call | tf_op jit(solution)/shard_map/add_children/pallas_call | solution.py:210
  38.9 8.3 %collective-permute-start = (f32[2304,128]{1,0:T(8,128)S(1)}, f32[2304,128]{1,0:T(8,128)S(1)}, u32[]{:S(2)}, u32[]{:S(2)}) collective-permute-start(f32[2304,128]{1,0:T(8,128)S(1)} %get-tuple-element.7), channel_id=1, source_target_pairs={{0,1},{1,0},{2,3},{3,2},{4,5},{5,4},{6,7},{7,6},{8,9},{9,8},{10,11... | collective-permute-start | bytes 3538952 | tf_op jit(solution)/shard_map/ppermute | solution.py:453
  47.2 2.5 %collective-permute-done = f32[2304,128]{1,0:T(8,128)S(1)} collective-permute-done((f32[2304,128]{1,0:T(8,128)S(1)}, f32[2304,128]{1,0:T(8,128)S(1)}, u32[]{:S(2)}, u32[]{:S(2)}) %collective-permute-start) | collective-permute-done | bytes 1179680 | tf_op jit(solution)/shard_map/ppermute | solution.py:453
  49.6 0.1 slice_add_fusion.2
  49.7 12.6 %collective-permute-start.1 = (f32[576,128]{1,0:T(8,128)S(1)}, f32[576,128]{1,0:T(8,128)S(1)}, u32[]{:S(2)}, u32[]{:S(2)}) collective-permute-start(f32[576,128]{1,0:T(8,128)S(1)} %get-tuple-element.10), channel_id=1, source_target_pairs={{0,2},{1,31},{2,4},{3,1},{4,6},{5,3},{6,8},{7,5},{8,10},{9,7},{10,... | collective-permute-start | bytes 884744 | tf_op jit(solution)/shard_map/ppermute | solution.py:449
  62.3 1.9 %collective-permute-start.3 = (f32[576,128]{1,0:T(8,128)S(1)}, f32[576,128]{1,0:T(8,128)S(1)}, u32[]{:S(2)}, u32[]{:S(2)}) collective-permute-start(f32[576,128]{1,0:T(8,128)S(1)} %get-tuple-element.11), channel_id=1, source_target_pairs={{0,28},{1,5},{2,30},{3,7},{4,0},{5,9},{6,2},{7,11},{8,4},{9,13},{1... | collective-permute-start | bytes 884744 | tf_op jit(solution)/shard_map/ppermute | solution.py:449
  64.3 1.9 %collective-permute-start.2 = (f32[576,128]{1,0:T(8,128)S(1)}, f32[576,128]{1,0:T(8,128)S(1)}, u32[]{:S(2)}, u32[]{:S(2)}) collective-permute-start(f32[576,128]{1,0:T(8,128)S(1)} %get-tuple-element.12), channel_id=1, source_target_pairs={{0,30},{1,3},{2,0},{3,5},{4,2},{5,7},{6,4},{7,9},{8,6},{9,11},{10,... | collective-permute-start | bytes 884744 | tf_op jit(solution)/shard_map/ppermute | solution.py:449
  66.2 0.0 collective-permute-done.1
  66.2 7.0 %collective-permute-done.3 = f32[576,128]{1,0:T(8,128)S(1)} collective-permute-done((f32[576,128]{1,0:T(8,128)S(1)}, f32[576,128]{1,0:T(8,128)S(1)}, u32[]{:S(2)}, u32[]{:S(2)}) %collective-permute-start.3) | collective-permute-done | bytes 294944 | tf_op jit(solution)/shard_map/ppermute | solution.py:449
  73.2 3.2 %collective-permute-done.2 = f32[576,128]{1,0:T(8,128)S(1)} collective-permute-done((f32[576,128]{1,0:T(8,128)S(1)}, f32[576,128]{1,0:T(8,128)S(1)}, u32[]{:S(2)}, u32[]{:S(2)}) %collective-permute-start.2) | collective-permute-done | bytes 294944 | tf_op jit(solution)/shard_map/ppermute | solution.py:449
  76.5 0.1 fusion.2
  76.5 25.5 %all_to_all.14 = f32[4,144,128]{2,1,0:T(8,128)S(1)} all-to-all(f32[4,144,128]{2,1,0:T(8,128)S(1)} %bitcast.7), channel_id=1, replica_groups={{0,8,16,24},{2,10,18,26},{4,12,20,28},{6,14,22,30},{1,9,17,25},{3,11,19..., dimensions={0} | all-to-all | bytes 589824 | tf_op jit(solution)/shard_map/all_to_all | solution.py:469
  102.1 17.4 %all_gather.3 = f32[576,128]{1,0:T(8,128)S(1)} all-gather(f32[144,128]{1,0:T(8,128)S(1)} %reduce_sum.9), channel_id=1, replica_groups={{0,8,16,24},{2,10,18,26},{4,12,20,28},{6,14,22,30},{1,9,17,25},{3,11,19..., dimensions={0}, use_global_device_ids=true | all-gather | bytes 368640 | tf_op jit(solution)/shard_map/all_gather | solution.py:473
  119.6 3.7 %collective-permute-start.4 = (f32[576,128]{1,0:T(8,128)S(1)}, f32[576,128]{1,0:T(8,128)S(1)}, u32[]{:S(2)}, u32[]{:S(2)}) collective-permute-start(f32[576,128]{1,0:T(8,128)S(1)} %all_gather.3), channel_id=1, source_target_pairs={{0,30},{1,3},{2,0},{3,5},{4,2},{5,7},{6,4},{7,9},{8,6},{9,11},{10,... | collective-permute-start | bytes 884744 | tf_op jit(solution)/shard_map/ppermute | solution.py:449
  123.3 2.9 %collective-permute-start.5 = (f32[576,128]{1,0:T(8,128)S(1)}, f32[576,128]{1,0:T(8,128)S(1)}, u32[]{:S(2)}, u32[]{:S(2)}) collective-permute-start(f32[576,128]{1,0:T(8,128)S(1)} %all_gather.3), channel_id=1, source_target_pairs={{0,28},{1,5},{2,30},{3,7},{4,0},{5,9},{6,2},{7,11},{8,4},{9,13},{1... | collective-permute-start | bytes 884744 | tf_op jit(solution)/shard_map/ppermute | solution.py:449
  126.2 4.6 %collective-permute-start.6 = (f32[576,128]{1,0:T(8,128)S(1)}, f32[576,128]{1,0:T(8,128)S(1)}, u32[]{:S(2)}, u32[]{:S(2)}) collective-permute-start(f32[576,128]{1,0:T(8,128)S(1)} %all_gather.3), channel_id=1, source_target_pairs={{0,2},{1,31},{2,4},{3,1},{4,6},{5,3},{6,8},{7,5},{8,10},{9,7},{10,... | collective-permute-start | bytes 884744 | tf_op jit(solution)/shard_map/ppermute | solution.py:449
  130.8 0.0 collective-permute-done.4
  130.8 3.6 %collective-permute-done.5 = f32[576,128]{1,0:T(8,128)S(1)} collective-permute-done((f32[576,128]{1,0:T(8,128)S(1)}, f32[576,128]{1,0:T(8,128)S(1)}, u32[]{:S(2)}, u32[]{:S(2)}) %collective-permute-start.5) | collective-permute-done | bytes 294944 | tf_op jit(solution)/shard_map/ppermute | solution.py:449
  134.5 5.4 %collective-permute-done.6 = f32[576,128]{1,0:T(8,128)S(1)} collective-permute-done((f32[576,128]{1,0:T(8,128)S(1)}, f32[576,128]{1,0:T(8,128)S(1)}, u32[]{:S(2)}, u32[]{:S(2)}) %collective-permute-start.6) | collective-permute-done | bytes 294944 | tf_op jit(solution)/shard_map/ppermute | solution.py:449
  139.9 8.5 %collective-permute-start.7 = (f32[2304,128]{1,0:T(8,128)S(1)}, f32[2304,128]{1,0:T(8,128)S(1)}, u32[]{:S(2)}, u32[]{:S(2)}) collective-permute-start(f32[2304,128]{1,0:T(8,128)S(1)} %constant_dynamic-update-slice_fusion.mine_ref), channel_id=1, source_target_pairs={{0,1},{1,0},{2,3},{3,2},{4,5},{5,4},{6,7},{7,6},{8,9},{9,8},{10,11... | collective-permute-start | bytes 3538952 | tf_op jit(solution)/shard_map/ppermute | solution.py:453
  148.5 2.3 %collective-permute-done.7.other_ref = f32[2304,128]{1,0:T(8,128)S(1)} collective-permute-done((f32[2304,128]{1,0:T(8,128)S(1)}, f32[2304,128]{1,0:T(8,128)S(1)}, u32[]{:S(2)}, u32[]{:S(2)}) %collective-permute-start.7) | collective-permute-done | bytes 1179680 | tf_op jit(solution)/shard_map/ppermute | solution.py:453
  150.7 28.3 %factor.1 = (f32[32,1024]{1,0:T(8,128)}, f32[256,1024]{1,0:T(8,128)}) custom-call(s32[16]{0:T(128)S(1)} %copy-done.2, f32[2304,128]{1,0:T(8,128)S(1)} %constant_dynamic-update-slice_fusion.mine_ref, f32[2304,128]{1,0:T(8,128)S(1)} %collective-permute-done.7.other_ref, f32[256,1024]{1,0:T(8,128)S(1)} %bitcast.6), custom_call_target="tpu_custom_call" | custom-call | tf_op jit(solution)/shard_map/factor/pallas_call | solution.py:427
  (5 shorter events, 0.1 us)
Async XLA Ops:
  3.0 7.8 %copy-start = (f32[1,256,1024]{2,1,0:T(8,128)S(1)}, f32[1,256,1024]{2,1,0:T(8,128)}, u32[]{:S(2)}) copy-start(f32[1,256,1024]{2,1,0:T(8,128)} %param.5) | copy-start | bytes 3145732
  3.0 7.8 %copy-start.2 = (s32[16]{0:T(128)S(1)}, s32[16]{0:T(128)}, u32[]{:S(2)}) copy-start(s32[16]{0:T(128)} %live_ref.3) | copy-start | bytes 196
  3.1 32.6 %all-to-all-start = ((f32[16,32,1024]{2,1,0:T(8,128)}), f32[16,32,1024]{2,1,0:T(8,128)}, u32[]{:S(2)}, u32[]{:S(2)}) async-start(f32[16,32,1024]{2,1,0:T(8,128)} %place_child.1), calls=%async_computation | async-start | bytes 4194304 | tf_op jit(solution)/shard_map/all_to_all | solution.py:483
  10.9 24.8 %copy-start.1 = (s32[16]{0:T(128)S(1)}, s32[16]{0:T(128)}, u32[]{:S(2)}) copy-start(s32[16]{0:T(128)} %parent_ref.1) | copy-start | bytes 196
  38.9 10.8 %collective-permute-start = (f32[2304,128]{1,0:T(8,128)S(1)}, f32[2304,128]{1,0:T(8,128)S(1)}, u32[]{:S(2)}, u32[]{:S(2)}) collective-permute-start(f32[2304,128]{1,0:T(8,128)S(1)} %get-tuple-element.7), channel_id=1, source_target_pairs={{0,1},{1,0},{2,3},{3,2},{4,5},{5,4},{6,7},{7,6},{8,9},{9,8},{10,11... | collective-permute-start | bytes 3538952 | tf_op jit(solution)/shard_map/ppermute | solution.py:453
  49.7 16.5 %collective-permute-start.1 = (f32[576,128]{1,0:T(8,128)S(1)}, f32[576,128]{1,0:T(8,128)S(1)}, u32[]{:S(2)}, u32[]{:S(2)}) collective-permute-start(f32[576,128]{1,0:T(8,128)S(1)} %get-tuple-element.10), channel_id=1, source_target_pairs={{0,2},{1,31},{2,4},{3,1},{4,6},{5,3},{6,8},{7,5},{8,10},{9,7},{10,... | collective-permute-start | bytes 884744 | tf_op jit(solution)/shard_map/ppermute | solution.py:449
  62.3 10.9 %collective-permute-start.3 = (f32[576,128]{1,0:T(8,128)S(1)}, f32[576,128]{1,0:T(8,128)S(1)}, u32[]{:S(2)}, u32[]{:S(2)}) collective-permute-start(f32[576,128]{1,0:T(8,128)S(1)} %get-tuple-element.11), channel_id=1, source_target_pairs={{0,28},{1,5},{2,30},{3,7},{4,0},{5,9},{6,2},{7,11},{8,4},{9,13},{1... | collective-permute-start | bytes 884744 | tf_op jit(solution)/shard_map/ppermute | solution.py:449
  64.3 12.2 %collective-permute-start.2 = (f32[576,128]{1,0:T(8,128)S(1)}, f32[576,128]{1,0:T(8,128)S(1)}, u32[]{:S(2)}, u32[]{:S(2)}) collective-permute-start(f32[576,128]{1,0:T(8,128)S(1)} %get-tuple-element.12), channel_id=1, source_target_pairs={{0,30},{1,3},{2,0},{3,5},{4,2},{5,7},{6,4},{7,9},{8,6},{9,11},{10,... | collective-permute-start | bytes 884744 | tf_op jit(solution)/shard_map/ppermute | solution.py:449
  119.6 11.2 %collective-permute-start.4 = (f32[576,128]{1,0:T(8,128)S(1)}, f32[576,128]{1,0:T(8,128)S(1)}, u32[]{:S(2)}, u32[]{:S(2)}) collective-permute-start(f32[576,128]{1,0:T(8,128)S(1)} %all_gather.3), channel_id=1, source_target_pairs={{0,30},{1,3},{2,0},{3,5},{4,2},{5,7},{6,4},{7,9},{8,6},{9,11},{10,... | collective-permute-start | bytes 884744 | tf_op jit(solution)/shard_map/ppermute | solution.py:449
  123.3 11.2 %collective-permute-start.5 = (f32[576,128]{1,0:T(8,128)S(1)}, f32[576,128]{1,0:T(8,128)S(1)}, u32[]{:S(2)}, u32[]{:S(2)}) collective-permute-start(f32[576,128]{1,0:T(8,128)S(1)} %all_gather.3), channel_id=1, source_target_pairs={{0,28},{1,5},{2,30},{3,7},{4,0},{5,9},{6,2},{7,11},{8,4},{9,13},{1... | collective-permute-start | bytes 884744 | tf_op jit(solution)/shard_map/ppermute | solution.py:449
  126.2 13.7 %collective-permute-start.6 = (f32[576,128]{1,0:T(8,128)S(1)}, f32[576,128]{1,0:T(8,128)S(1)}, u32[]{:S(2)}, u32[]{:S(2)}) collective-permute-start(f32[576,128]{1,0:T(8,128)S(1)} %all_gather.3), channel_id=1, source_target_pairs={{0,2},{1,31},{2,4},{3,1},{4,6},{5,3},{6,8},{7,5},{8,10},{9,7},{10,... | collective-permute-start | bytes 884744 | tf_op jit(solution)/shard_map/ppermute | solution.py:449
  139.9 10.8 %collective-permute-start.7 = (f32[2304,128]{1,0:T(8,128)S(1)}, f32[2304,128]{1,0:T(8,128)S(1)}, u32[]{:S(2)}, u32[]{:S(2)}) collective-permute-start(f32[2304,128]{1,0:T(8,128)S(1)} %constant_dynamic-update-slice_fusion.mine_ref), channel_id=1, source_target_pairs={{0,1},{1,0},{2,3},{3,2},{4,5},{5,4},{6,7},{7,6},{8,9},{9,8},{10,11... | collective-permute-start | bytes 3538952 | tf_op jit(solution)/shard_map/ppermute | solution.py:453
